TPU v7x, 32 devices: a whole 2x2x4 slice. The times are simulated.
32 devices in a mesh: groups: 2 (over x), wide: 16 (over z, y, core).
Axes of the slice: x: 2, y: 2, z: 4, core: 2. Of those that a mesh axis runs over, the one named last changes fastest.
Arguments:
- tokens: bfloat16 [64, 384, 768], P(('groups', 'wide')), parts along dimension 0, may hold values from -6 to 6
- item_lengths: int32 [64, 64], P(('groups', 'wide')), parts along dimension 0, may hold values from 1 to 16, 384 in all within a row
- w_query: bfloat16 [768, 768], replicated
- w_key: bfloat16 [768, 768], replicated, may hold values from -0.21875 to 0.21875
- w_value: bfloat16 [768, 768], replicated, may hold values from -0.21875 to 0.21875
- w_output: bfloat16 [768, 768], replicated, may hold values from -0.21875 to 0.21875
- w_input: bfloat16 [3072, 768], P('wide'), may hold values from -0.21875 to 0.21875
- w_down: bfloat16 [3072, 768], P('wide'), may hold values from -0.109375 to 0.109375
- norm_attn: float32 [768], replicated, may hold values from 0.1 to 1.9
- norm_ffn: float32 [768], replicated, may hold values from 0.1 to 1.9
- norm_final: float32 [768], replicated, may hold values from 0.1 to 1.9
- owner: int32 [4096, 1], P(('groups', 'wide')), parts along dimension 0, may hold values from 0 to 15; in each aligned block of 128 rows (0 to 127, 128 to 255, ...) at most 16 rows name the same one
- cluster_slot: int32 [4096], P(('groups', 'wide')), parts along dimension 0, may hold values from 0 to 7
- coarse: bfloat16 [128, 768], P('wide'), may hold values from -4 to 4
- centroids: bfloat16 [128, 256, 768], P('wide'), may hold values from -0.21875 to 0.21875
Outputs:
- item_embed: bfloat16 [4096, 768], P(('groups', 'wide')), parts along dimension 0
- item_codes: float32 [4096, 256], P(('groups', 'wide')), parts along dimension 0
There are 2 independent parts, one for each index of `groups`. A program takes and returns all parts, laid end to end along the dimension named above; an argument that names none is the same for every part. Nothing has to cross between parts.
Inputs may be any that keep to these rules, and one draw needn't show every extreme that they name: In each device's 128 rows no owner is named more than 16 times, a bound that some block reaches. `item_lengths`: each pack's lengths sum to 384; some item has exactly 16 tokens.
All inputs are finite; a program needn't handle non-finite values.
Results may differ from a plain program's by a relative error of at most 0.012.
The roundings to bfloat16 on the way count: a program that leaves them out, or rounds other values in their place, can miss the bound.
Values may be sent and summed in bfloat16 or wider, within the bound.
No kernel may reach another device: no remote copies, remote signals or barrier semaphores. Data moves between devices by JAX's collectives and lax.ppermute only.
A program may use at most 128 MiB of HBM per device.

v0:
```python
import jax
import jax.numpy as jnp
from jax import lax
from jax.sharding import PartitionSpec as P

HEADS = 12


def rms(values, gain):
    mean_sq = jnp.mean(values * values, axis=-1, keepdims=True)
    return values * lax.rsqrt(mean_sq + 1e-06) * gain


def local(
    tokens,
    item_lengths,
    w_query,
    w_key,
    w_value,
    w_output,
    w_input,
    w_down,
    norm_attn,
    norm_ffn,
    norm_final,
    owner,
    cluster_slot,
    coarse,
    centroids,
):
    packs, seq, width = tokens.shape
    per_pack = item_lengths.shape[1]
    heads = HEADS
    head_size = width // heads
    wide_count = lax.axis_size("wide")
    items_dev = packs * per_pack
    capacity = max(2, 2 * items_dev // wide_count)
    slots = wide_count * capacity
    local_clusters = centroids.shape[0]
    codes_count = centroids.shape[1]
    ends = jnp.cumsum(item_lengths, axis=1)
    places = jnp.arange(seq, dtype=jnp.int32)
    item = jnp.sum((ends[:, None, :] <= places[None, :, None]).astype(jnp.int32), axis=2)
    same = item[:, :, None] == item[:, None, :]
    stream0 = tokens.reshape(packs * seq, width).astype(jnp.float32)
    normed = rms(stream0, norm_attn).astype(jnp.bfloat16)
    query = (
        jnp.dot(normed, w_query, preferred_element_type=jnp.float32)
        .astype(jnp.bfloat16)
        .reshape(packs, seq, heads, head_size)
    )
    keys = (
        jnp.dot(normed, w_key, preferred_element_type=jnp.float32)
        .astype(jnp.bfloat16)
        .reshape(packs, seq, heads, head_size)
    )
    values = (
        jnp.dot(normed, w_value, preferred_element_type=jnp.float32)
        .astype(jnp.bfloat16)
        .reshape(packs, seq, heads, head_size)
    )
    scores = jnp.einsum("pqhe,pkhe->phqk", query, keys, preferred_element_type=jnp.float32)
    scores = jnp.where(same[:, None], scores, -1e30)
    top = jnp.max(scores, axis=-1, keepdims=True)
    expo = jnp.exp(scores - top)
    probs = (expo / jnp.sum(expo, axis=-1, keepdims=True)).astype(jnp.bfloat16)
    context = (
        jnp.einsum("phqk,pkhe->pqhe", probs, values, preferred_element_type=jnp.float32)
        .astype(jnp.bfloat16)
        .reshape(packs * seq, width)
    )
    stream = (stream0 + jnp.dot(context, w_output, preferred_element_type=jnp.float32)).astype(
        jnp.bfloat16
    )
    normed2 = rms(stream.astype(jnp.float32), norm_ffn).astype(jnp.bfloat16)
    hidden = jax.nn.relu(
        jnp.einsum(
            "td,fd->tf",
            normed2,
            lax.all_gather(w_input, "wide", axis=0, tiled=True),
            preferred_element_type=jnp.float32,
        )
    ).astype(jnp.bfloat16)
    ffn_out = jnp.dot(
        hidden,
        lax.all_gather(w_down, "wide", axis=0, tiled=True),
        preferred_element_type=jnp.float32,
    )
    final = (stream.astype(jnp.float32) + ffn_out).reshape(packs, seq, width)
    select = (item[:, None, :] == jnp.arange(per_pack, dtype=jnp.int32)[None, :, None]).astype(
        jnp.float32
    )
    pooled = jnp.einsum("pis,psd->pid", select, final, precision=lax.Precision.HIGHEST)
    item_embed = rms(pooled, norm_final).astype(jnp.bfloat16).reshape(items_dev, width)
    target = owner[:, 0]
    target_onehot = (target[:, None] == jnp.arange(wide_count, dtype=jnp.int32)[None, :]).astype(
        jnp.int32
    )
    earlier = jnp.cumsum(target_onehot, axis=0) - target_onehot
    rank_in = jnp.sum(earlier * target_onehot, axis=1)
    slot_of = target * capacity + rank_in
    placing = (slot_of[None, :] == jnp.arange(slots, dtype=jnp.int32)[:, None]).astype(jnp.bfloat16)
    cluster_onehot = (
        cluster_slot[:, None] == jnp.arange(local_clusters, dtype=jnp.int32)[None, :]
    ).astype(jnp.bfloat16)
    send_rows = (
        jnp.dot(placing, item_embed, preferred_element_type=jnp.float32)
        .astype(jnp.bfloat16)
        .reshape(wide_count, capacity, width)
    )
    send_cluster = (
        jnp.dot(placing, cluster_onehot, preferred_element_type=jnp.float32)
        .astype(jnp.bfloat16)
        .reshape(wide_count, capacity, local_clusters)
    )
    book_flat = centroids.reshape(local_clusters * codes_count, width)
    center_proj = jnp.einsum("ld,ljd->lj", coarse, centroids, preferred_element_type=jnp.float32)
    rows = lax.all_to_all(send_rows, "wide", split_axis=0, concat_axis=0, tiled=True)
    chosen = lax.all_to_all(send_cluster, "wide", split_axis=0, concat_axis=0, tiled=True)
    count = rows.shape[1]
    flat_rows = rows.reshape(wide_count * count, width)
    flat_chosen = chosen.reshape(wide_count * count, local_clusters).astype(jnp.float32)
    direct = jnp.einsum("nd,cd->nc", flat_rows, book_flat, preferred_element_type=jnp.float32)
    direct = direct.reshape(wide_count * count, local_clusters, codes_count)
    picked = jnp.sum(direct * flat_chosen[:, :, None], axis=1)
    offset = jnp.dot(flat_chosen, center_proj, precision=lax.Precision.HIGHEST)
    codes = (picked - offset).reshape(wide_count, count, codes_count)
    returned = lax.all_to_all(codes, "wide", split_axis=0, concat_axis=0, tiled=True)
    returned = returned.reshape(slots, codes_count)
    item_codes = jnp.dot(placing.astype(jnp.float32).T, returned, precision=lax.Precision.HIGHEST)
    return (item_embed, item_codes)


def solution(mesh):
    return jax.shard_map(
        local,
        mesh=mesh,
        in_specs=(
            P(("groups", "wide"), None, None),
            P(("groups", "wide"), None),
            P(),
            P(),
            P(),
            P(),
            P("wide", None),
            P("wide", None),
            P(),
            P(),
            P(),
            P(("groups", "wide"), None),
            P(("groups", "wide")),
            P("wide", None),
            P("wide", None, None),
        ),
        out_specs=(P(("groups", "wide"), None), P(("groups", "wide"), None)),
        check_vma=False,
    )
```

profile of v0, /device:TPU:0, one launch (start us, length us, event | category | flops | bytes accessed | tf_op | source)
XLA Modules:
  0.0 178.0 jit_solution(4979652820406230361)
XLA Ops:
  12.7 7.4 %all-to-all-start.1 = ((bf16[16,16,8]{1,2,0:T(8,128)(2,1)}), bf16[16,16,8]{1,2,0:T(8,128)(2,1)S(1)}, u32[]{:S(2)}, u32[]{:S(2)}) async-start(bf16[16,16,8]{1,2,0:T(8,128)(2,1)} %copy.56), calls=%async_computation.1 | async-start | bytes 65536 | tf_op jit(solution)/shard_map/all_to_all | solution.py:119
  20.1 1.6 fusion.10
  21.8 1.7 fusion.12
  24.5 2.1 %convolution_convert_fusion.1 = bf16[768,768]{1,0:T(8,128)(2,1)} fusion(bf16[768,768]{1,0:T(8,128)(2,1)S(1)} %fusion.12, bf16[768,768]{1,0:T(8,128)(2,1)S(1)} %copy-done.8), kind=kOutput, calls=%fused_computation.25 | convolution fusion | flops 906559488 | bytes 3538944 | tf_op jit(solution)/shard_map/dot_general | solution.py:48
  26.6 2.4 %copy.49 = bf16[768,768]{0,1:T(8,128)(2,1)} copy(bf16[768,768]{1,0:T(8,128)(2,1)} %convolution_convert_fusion.1) | data formatting | bytes 2359296 | tf_op jit(solution)/shard_map/convert_element_type | solution.py:49
  29.0 3.6 %reshape.106 = bf16[2,384,12,64]{1,0,3,2:T(2,128)(2,1)} reshape(bf16[768,768]{0,1:T(8,128)(2,1)} %copy.49) | data formatting | bytes 2359296 | tf_op jit(solution)/shard_map/reshape | solution.py:50
  32.6 3.7 %convolution_convert_fusion = bf16[768,768]{1,0:T(8,128)(2,1)} fusion(bf16[768,768]{1,0:T(8,128)(2,1)} %copy-done.2, bf16[768,768]{1,0:T(8,128)(2,1)} %param.18), kind=kOutput, calls=%fused_computation.24 | convolution fusion | flops 906559488 | bytes 3538944 | tf_op jit(solution)/shard_map/dot_general | solution.py:53
  36.3 2.4 %copy.50 = bf16[768,768]{0,1:T(8,128)(2,1)} copy(bf16[768,768]{1,0:T(8,128)(2,1)} %convolution_convert_fusion) | data formatting | bytes 2359296 | tf_op jit(solution)/shard_map/convert_element_type | solution.py:54
  38.7 3.6 %reshape.107 = bf16[2,384,12,64]{1,0,3,2:T(2,128)(2,1)} reshape(bf16[768,768]{0,1:T(8,128)(2,1)} %copy.50) | data formatting | bytes 2359296 | tf_op jit(solution)/shard_map/reshape | solution.py:55
  42.5 3.8 %convolution_convert_fusion.2 = bf16[768,768]{1,0:T(8,128)(2,1)} fusion(bf16[768,768]{1,0:T(8,128)(2,1)} %copy-done.2, bf16[768,768]{1,0:T(8,128)(2,1)} %param.19), kind=kOutput, calls=%fused_computation.26 | convolution fusion | flops 906559488 | bytes 3538944 | tf_op jit(solution)/shard_map/dot_general | solution.py:58
  46.3 2.4 %copy.48 = bf16[768,768]{0,1:T(8,128)(2,1)} copy(bf16[768,768]{1,0:T(8,128)(2,1)} %convolution_convert_fusion.2) | data formatting | bytes 2359296 | tf_op jit(solution)/shard_map/convert_element_type | solution.py:59
  48.7 3.6 %reshape.105 = bf16[2,384,12,64]{1,0,3,2:T(2,128)(2,1)} reshape(bf16[768,768]{0,1:T(8,128)(2,1)} %copy.48) | data formatting | bytes 2359296 | tf_op jit(solution)/shard_map/reshape | solution.py:60
  52.5 9.0 %fusion.51 = (f32[2,12,384]{2,1,0:T(8,128)S(1)}, f32[2,12,384,384]{2,3,1,0:T(8,128)}) fusion(pred[2,384,384]{1,2,0:T(8,128)(4,1)S(1)} %broadcast_compare_fusion, bf16[2,384,12,64]{1,0,3,2:T(2,128)(2,1)} %reshape.107, bf16[2,384,12,64]{1,0,3,2:T(2,128)(2,1)} %reshape.106), kind=kOutput, calls=%fused_computation.68 | convolution fusion | flops 463602048 | bytes 16846848 | tf_op jit(solution)/shard_map/sub | solution.py:65
  61.6 6.9 %fusion.17 = bf16[2,384,12,64]{1,3,2,0:T(8,128)(2,1)S(1)} fusion(f32[2,12,384,384]{2,3,1,0:T(8,128)} %get-tuple-element.3, f32[2,12,384]{2,1,0:T(8,128)S(1)} %get-tuple-element.2, bf16[2,384,12,64]{1,0,3,2:T(2,128)(2,1)} %reshape.105), kind=kOutput, calls=%fused_computation.28 | convolution fusion | flops 460652544 | bytes 16551936 | tf_op jit(solution)/shard_map/phqk,pkhe->pqhe/dot_general | solution.py:68
  68.5 1.2 copy.55
  70.0 1.0 copy-done.1
  71.4 2.3 %fusion.7 = (f32[768]{0:T(1024)S(1)}, bf16[768,768]{1,0:T(8,128)(2,1)}) fusion(bf16[768,768]{0,1:T(8,128)(2,1)S(1)} %bitcast.59, bf16[768,768]{1,0:T(8,128)(2,1)S(1)} %copy-done.9, bf16[2,384,768]{2,1,0:T(8,128)(2,1)S(1)} %copy-done.1), kind=kOutput, calls=%fused_computation.12 | convolution fusion | flops 909507840 | bytes 4721664 | tf_op jit(solution)/shard_map/dot_general | solution.py:72
  73.6 47.1 %all-gather.5.cloned.1.call-done = bf16[3072,768]{1,0:T(8,128)(2,1)} async-done(((bf16[192,768]{1,0:T(8,128)(2,1)}), bf16[3072,768]{1,0:T(8,128)(2,1)}) %all-gather.5.cloned.1.call-update) | async-done | bytes 4718608 | tf_op jit(solution)/shard_map/all_gather | solution.py:86
  120.7 13.5 %convert_add_fusion = f32[768,768]{1,0:T(8,128)} fusion(bf16[768,768]{1,0:T(8,128)(2,1)} %get-tuple-element.5, bf16[3072,768]{1,0:T(8,128)(2,1)} %all-gather.5.cloned.1.call-done, bf16[3072,768]{1,0:T(8,128)(2,1)} %all-gather.3.cloned.1.call-done, f32[768]{0:T(1024)S(1)} %copy-done.10, f32[768]{0:T(1024)S(1)} %add_rsqrt_fusion), kind=kOutput, calls=%fused_computation.9 | convolution fusion | flops 7256014848 | bytes 12982272 | tf_op jit(solution)/shard_map/dot_general | solution.py:84
  134.2 2.8 %multiply_reduce_fusion.1 = (f32[2,64]{1,0:T(2,128)S(1)}, f32[2,64,768]{2,1,0:T(8,128)S(1)}) fusion(f32[2,384,768]{2,1,0:T(8,128)} %bitcast.58, s32[2,384]{1,0:T(2,128)S(1)} %convert_reduce_fusion), kind=kOutput, calls=%fused_computation.42 | convolution fusion | flops 453230464 | bytes 2756096 | tf_op jit(solution)/shard_map/pis,psd->pid/dot_general | solution.py:93
  138.2 4.2 %all-to-all-start = ((bf16[16,16,768]{2,1,0:T(8,128)(2,1)}), bf16[16,16,768]{2,1,0:T(8,128)(2,1)}, u32[]{:S(2)}, u32[]{:S(2)}) async-start(bf16[16,16,768]{2,1,0:T(8,128)(2,1)} %bitcast.5), calls=%async_computation | async-start | bytes 786432 | tf_op jit(solution)/shard_map/all_to_all | solution.py:118
  143.4 11.1 %all-to-all-done = bf16[16,16,768]{2,1,0:T(8,128)(2,1)} async-done(((bf16[16,16,768]{2,1,0:T(8,128)(2,1)}), bf16[16,16,768]{2,1,0:T(8,128)(2,1)}, u32[]{:S(2)}, u32[]{:S(2)}) %all-to-all-start) | async-done | bytes 393248 | tf_op jit(solution)/shard_map/all_to_all | solution.py:118
  154.6 2.0 %multiply_reduce_fusion = f32[256,256]{1,0:T(8,128)S(1)} fusion(bf16[256,768,1]{1,0,2:T(8,128)(2,1)} %bitcast.7, bf16[8,256,768]{2,1,0:T(8,128)(2,1)S(1)} %copy-done, f32[256,8]{0,1:T(8,128)S(1)} %convert_element_type.88), kind=kOutput, calls=%fused_computation.22 | convolution fusion | flops 806289408 | bytes 3809280 | tf_op jit(solution)/shard_map/nd,cd->nc/dot_general | solution.py:123
  156.9 13.3 %all_to_all.15 = f32[16,16,256]{2,1,0:T(8,128)S(1)} all-to-all(f32[16,16,256]{2,1,0:T(8,128)S(1)} %bitcast.60), channel_id=1, replica_groups=mesh['groups'=2,'wide'=16] {'wide'}, dimensions={0} | all-to-all | bytes 524288 | tf_op jit(solution)/shard_map/all_to_all | solution.py:128
  (50 shorter events, 11.1 us)
Async XLA Ops:
  7.2 135.2 %copy-start = (bf16[8,256,768]{2,1,0:T(8,128)(2,1)S(1)}, bf16[8,256,768]{2,1,0:T(8,128)(2,1)}, u32[]{:S(2)}) copy-start(bf16[8,256,768]{2,1,0:T(8,128)(2,1)} %param.29) | copy-start | bytes 9437188
  7.2 14.6 %copy-start.5 = (f32[768]{0:T(1024)S(1)}, f32[768]{0:T(1024)}, u32[]{:S(2)}) copy-start(f32[768]{0:T(1024)} %param.23) | copy-start | bytes 9220
  7.2 66.4 %all-gather.3.cloned.1.call-start = ((), (), s32[]{:S(2)}) async-start(), calls=%async_computation.3 | async-start | bytes 5013504 | tf_op jit(solution)/shard_map/all_gather | solution.py:80
  7.9 112.8 %all-gather.5.cloned.1.call-start = ((), (), s32[]{:S(2)}) async-start(), calls=%async_computation.4 | async-start | bytes 5013504 | tf_op jit(solution)/shard_map/all_gather | solution.py:86
  12.7 125.4 %all-to-all-start.1 = ((bf16[16,16,8]{1,2,0:T(8,128)(2,1)}), bf16[16,16,8]{1,2,0:T(8,128)(2,1)S(1)}, u32[]{:S(2)}, u32[]{:S(2)}) async-start(bf16[16,16,8]{1,2,0:T(8,128)(2,1)} %copy.56), calls=%async_computation.1 | async-start | bytes 65536 | tf_op jit(solution)/shard_map/all_to_all | solution.py:119
  21.8 2.7 %copy-start.8 = (bf16[768,768]{1,0:T(8,128)(2,1)S(1)}, bf16[768,768]{1,0:T(8,128)(2,1)}, u32[]{:S(2)}) copy-start(bf16[768,768]{1,0:T(8,128)(2,1)} %param.17) | copy-start | bytes 3538948
  23.5 1.0 copy-start.2
  38.7 3.6 %copy-start.7 = (s32[2,64]{1,0:T(2,128)S(1)}, s32[2,64]{1,0:T(2,128)}, u32[]{:S(2)}) copy-start(s32[2,64]{1,0:T(2,128)} %param.16) | copy-start | bytes 1540
  69.7 1.3 copy-start.1
  69.7 1.6 copy-start.9
  71.4 49.4 %copy-start.10 = (f32[768]{0:T(1024)S(1)}, f32[768]{0:T(1024)}, u32[]{:S(2)}) copy-start(f32[768]{0:T(1024)} %param.24) | copy-start | bytes 9220
  134.2 2.8 %copy-start.6 = (f32[768]{0:T(1024)S(1)}, f32[768]{0:T(1024)}, u32[]{:S(2)}) copy-start(f32[768]{0:T(1024)} %param.25) | copy-start | bytes 9220
  137.0 5.4 %copy-start.4 = (bf16[8,768]{1,0:T(8,128)(2,1)S(1)}, bf16[8,768]{1,0:T(8,128)(2,1)}, u32[]{:S(2)}) copy-start(bf16[8,768]{1,0:T(8,128)(2,1)} %param.28) | copy-start | bytes 36868
  137.1 6.2 %copy-start.3 = (bf16[2,64,768]{2,1,0:T(8,128)(2,1)}, bf16[2,64,768]{2,1,0:T(8,128)(2,1)S(1)}, u32[]{:S(2)}) copy-start(bf16[2,64,768]{2,1,0:T(8,128)(2,1)S(1)} %multiply_convert_fusion) | copy-start | bytes 589828
  138.2 16.4 %all-to-all-start = ((bf16[16,16,768]{2,1,0:T(8,128)(2,1)}), bf16[16,16,768]{2,1,0:T(8,128)(2,1)}, u32[]{:S(2)}, u32[]{:S(2)}) async-start(bf16[16,16,768]{2,1,0:T(8,128)(2,1)} %bitcast.5), calls=%async_computation | async-start | bytes 786432 | tf_op jit(solution)/shard_map/all_to_all | solution.py:118
Sparse Core Ops, SparseCore 0:
  10.3 56.1 all-gather.2
  68.8 51.9 all-gather.4
where the time goes:
time: 179 us; the launch traced here: 178 us
  waiting for transfers between devices  59.6 us (33%)
  matrix products  50.2 us (28%)
  local copies, waits for them, and re-layouts  22.6 us (13%)
  between operations  14.3 us (8%)
  blocking collectives  13.3 us (7%)
  starting transfers between devices  11.7 us (7%)
  other arithmetic  6.42 us (4%)
    all_gather x1, waiting for transfers between devices, local(): lax.all_gather(w_down, 'wide', axis=0, tiled=True)  47.1 us
    dot_general x1, matrix products, local(): jnp.dot(hidden, lax.all_gather(w_down, 'wide', axis=0, tiled=True), prefe...  13.5 us
    all_to_all x1, blocking collectives, local(): lax.all_to_all(codes, 'wide', split_axis=0, concat_axis=0, tiled=True)  13.3 us
    all_to_all x1, waiting for transfers between devices, local(): lax.all_to_all(send_rows, 'wide', split_axis=0, concat_axis=0, tiled=True)  11.1 us
    sub x1, matrix products, local(): expo = jnp.exp(scores - top)  9.04 us
    all_to_all x1, starting transfers between devices, local(): lax.all_to_all(send_cluster, 'wide', split_axis=0, concat_axis=0, tiled=T...  7.39 us
    dot_general x1, matrix products, local(): jnp.einsum('phqk,pkhe->pqhe', probs, values, preferred_element_type=jnp.f...  6.9 us
    all_to_all x1, starting transfers between devices, local(): lax.all_to_all(send_rows, 'wide', split_axis=0, concat_axis=0, tiled=True)  4.2 us
  transfers between devices with their start and end apart: 4, of which 2 were waited for; matrix products, arithmetic and copies ran while one was open for 41% of the time, Pallas kernels for 0%

commit v1 on v0

v1 whole, which is shorter than its diff:
```python
import functools

import jax
import jax.numpy as jnp
from jax import lax
from jax.experimental import pallas as pl
from jax.experimental.pallas import tpu as pltpu
from jax.sharding import PartitionSpec as P

HEADS = 12
EPS = 1e-06
VMEM_BYTES = 56 * 1024 * 1024
F32 = jnp.float32
BF16 = jnp.bfloat16


def params():
    return pltpu.CompilerParams(vmem_limit_bytes=VMEM_BYTES)


def cost(flops, nbytes):
    return pl.CostEstimate(flops=int(flops), bytes_accessed=int(nbytes), transcendentals=0)


def dot(a, b):
    return jnp.dot(a, b, preferred_element_type=F32)


def dot_nt(a, b):
    return lax.dot_general(a, b, (((1,), (1,)), ((), ())), preferred_element_type=F32)


def rms(values, gain):
    mean_sq = jnp.mean(values * values, axis=-1, keepdims=True)
    return values * lax.rsqrt(mean_sq + EPS) * gain


def item_rows(lengths, seq):
    items = lengths.shape[1]
    tri = (
        lax.broadcasted_iota(jnp.int32, (items, items), 0)
        <= lax.broadcasted_iota(jnp.int32, (items, items), 1)
    ).astype(F32)
    rows = jnp.broadcast_to(lengths.astype(F32), (8, items))
    ends = dot(rows.astype(BF16), tri.astype(BF16))[:1]
    starts = ends - rows[:1]
    place = lax.broadcasted_iota(jnp.int32, (seq, items), 0).astype(F32)
    return jnp.where((place < ends) & (place >= starts), 1.0, 0.0).astype(BF16)


def item_columns(lengths, seq):
    items = lengths.shape[1]
    row = lax.broadcasted_iota(jnp.int32, (items, items), 0)
    column = lax.broadcasted_iota(jnp.int32, (items, items), 1)
    rows = jnp.broadcast_to(lengths.astype(F32), (8, items)).astype(BF16)
    ends = dot_nt((column <= row).astype(F32).astype(BF16), rows)[:, :1]
    starts = dot_nt((column < row).astype(F32).astype(BF16), rows)[:, :1]
    place = lax.broadcasted_iota(jnp.int32, (items, seq), 1).astype(F32)
    return jnp.where((place < ends) & (place >= starts), 1.0, 0.0).astype(BF16)


def encoder_kernel(
    lengths_ref, x_ref, wq_ref, wk_ref, wv_ref, wo_ref, gain_ref, gain2_ref,
    normed2_ref, pooled_ref, q_ref, k_ref, v_ref, ctx_ref,
):
    seq, width = x_ref.shape
    lengths = lengths_ref[...]
    head = width // HEADS
    x = x_ref[...].astype(F32)
    normed = rms(x, gain_ref[...]).astype(BF16)
    q_ref[...] = dot(normed, wq_ref[...]).astype(BF16)
    k_ref[...] = dot(normed, wk_ref[...]).astype(BF16)
    v_ref[...] = dot(normed, wv_ref[...]).astype(BF16)
    onehot = item_rows(lengths, seq)
    block, window, lanes = 64, 128, 256
    heads = lanes // head
    lane_head = lax.broadcasted_iota(jnp.int32, (block, lanes), 1) // head
    for start in range(0, seq, block):
        first = min(max(start - (window - block) // 2, 0), seq - window)
        same = dot_nt(onehot[start : start + block], onehot[first : first + window])
        same = jnp.concatenate([same] * heads, axis=0) > 0.5
        for column in range(0, width, lanes):
            query = q_ref[start : start + block, column : column + lanes]
            stacked = jnp.concatenate(
                [jnp.where(lane_head == h, query, jnp.zeros_like(query)) for h in range(heads)], axis=0
            )
            scores = dot_nt(stacked, k_ref[first : first + window, column : column + lanes])
            scores = jnp.where(same, scores, -1e30)
            expo = jnp.exp(scores - jnp.max(scores, axis=-1, keepdims=True))
            probs = (expo / jnp.sum(expo, axis=-1, keepdims=True)).astype(BF16)
            mixed = dot(probs, v_ref[first : first + window, column : column + lanes])
            context = jnp.zeros((block, lanes), F32)
            for h in range(heads):
                context = jnp.where(lane_head == h, mixed[h * block : (h + 1) * block], context)
            ctx_ref[start : start + block, column : column + lanes] = context.astype(BF16)
    stream = (x + dot(ctx_ref[...], wo_ref[...])).astype(BF16)
    normed2_ref[...] = rms(stream.astype(F32), gain2_ref[...]).astype(BF16)
    pooled_ref[...] = dot(item_columns(lengths, seq), stream)


def encode_pack(lengths, x, wq, wk, wv, wo, gain, gain2):
    seq, width = x.shape
    items = lengths.shape[1]
    return pl.pallas_call(
        encoder_kernel,
        out_shape=(
            jax.ShapeDtypeStruct((seq, width), BF16),
            jax.ShapeDtypeStruct((items, width), F32),
        ),
        scratch_shapes=[pltpu.VMEM((seq, width), BF16)] * 4,
        compiler_params=params(),
        cost_estimate=cost(16 * seq * width * width, 8 * width * width + 8 * seq * width),
        name="encode_pack",
    )(lengths, x, wq, wk, wv, wo, gain, gain2)


def feed_kernel(n_in, n_down, has_acc, *refs):
    lengths_refs, normed_refs = refs[0:2], refs[2:4]
    ins, downs = refs[4 : 4 + n_in], refs[4 + n_in : 4 + n_in + n_down]
    rest = refs[4 + n_in + n_down :]
    w_in = jnp.concatenate([r[...] for r in ins], axis=0) if n_in > 1 else ins[0][...]
    w_down = jnp.concatenate([r[...] for r in downs], axis=0) if n_down > 1 else downs[0][...]
    for side in range(2):
        out_ref = rest[-2 + side]
        lengths = lengths_refs[side][...]
        packs, items = lengths.shape
        seq = normed_refs[side].shape[0] // packs
        for pack in range(packs):
            tokens = normed_refs[side][pack * seq : (pack + 1) * seq]
            hidden = jnp.maximum(dot_nt(tokens, w_in), 0.0).astype(BF16)
            pooled = dot(item_columns(lengths[pack : pack + 1], seq), hidden)
            part = dot(pooled.astype(BF16), w_down)
            rows = slice(pack * items, (pack + 1) * items)
            out_ref[rows] = part + rest[side][rows] if has_acc else part


def feed(lengths, normed, w_in, w_down, acc):
    items = lengths[0].shape[0] * lengths[0].shape[1]
    width = normed[0].shape[1]
    units = sum(w.shape[0] for w in w_in)
    tokens = 2 * normed[0].shape[0]
    acc = list(acc) if acc else []
    return pl.pallas_call(
        functools.partial(feed_kernel, len(w_in), len(w_down), bool(acc)),
        out_shape=(jax.ShapeDtypeStruct((items, width), F32),) * 2,
        compiler_params=params(),
        cost_estimate=cost(2 * tokens * width * units * 1.5, 2 * tokens * width + 4 * units * width),
        name="feed",
    )(*lengths, *normed, *w_in, *w_down, *acc)


def place_kernel(acc_ref, other_ref, pooled_ref, gain_ref, slot_ref, cluster_ref, embed_ref, send_ref):
    width = embed_ref.shape[1]
    embed = rms(acc_ref[...] + other_ref[...] + pooled_ref[...], gain_ref[...]).astype(BF16)
    embed_ref[...] = embed
    slots, items = send_ref.shape[0], embed.shape[0]
    placing = jnp.where(
        lax.broadcasted_iota(jnp.int32, (slots, items), 0) == slot_ref[...], 1.0, 0.0
    ).astype(BF16)
    send_ref[:, :width] = dot(placing, embed).astype(BF16)
    clusters = send_ref.shape[1] - width
    chosen = jnp.where(
        lax.broadcasted_iota(jnp.int32, (clusters, items), 0) == cluster_ref[...], 1.0, 0.0
    ).astype(BF16)
    send_ref[:, width:] = dot_nt(placing, chosen).astype(BF16)


def code_kernel(rows_ref, coarse_ref, books_ref, out_ref):
    clusters, codes, width = books_ref.shape
    slots = rows_ref.shape[0]
    rows = rows_ref[:, :width]
    coarse = coarse_ref[...]
    total = jnp.zeros((slots, codes), F32)
    for cluster in range(clusters):
        book = books_ref[cluster]
        offset = dot_nt(coarse, book)[cluster : cluster + 1]
        chosen = rows_ref[:, width + cluster : width + cluster + 1].astype(F32)
        total = total + (dot_nt(rows, book) - offset) * chosen
    out_ref[...] = total.astype(BF16)


def flip(axis_name, count, bits):
    pairs = [(i, i ^ bits) for i in range(count)]
    return lambda value: lax.ppermute(value, axis_name, pairs)


def gather_sixteen(w_input, w_down):
    rows = w_input.shape[0]
    common = rows // 3 // 16 * 16
    half = (rows - common) // 2
    start = common + lax.axis_index("groups") * half

    def mine(weights):
        return lax.dynamic_slice_in_dim(weights, start, half, 0)

    near, far, side = flip("wide", 16, 4), flip("wide", 16, 12), flip("wide", 16, 2)
    twin = flip("groups", 2, 1)
    held = jnp.concatenate([w_input[:common], w_down[:common], mine(w_input), mine(w_down)], axis=0)
    split = 2 * common

    def blocks(main, others):
        w_in = [main[:common], main[split : split + half], others[:half]]
        down = [main[common:split], main[split + half :], others[half:]]
        return w_in, down

    def join(first, second):
        return [a + b for a, b in zip(first, second)]

    side0 = side(held)
    near1 = near(held)
    far2 = far(held)
    x0 = twin(jnp.concatenate([side0[split:], near1[split:]], axis=0))
    side1 = side(near1)
    far3 = near(far2)
    side2 = side(far2)
    x1 = twin(jnp.concatenate([side1[split:], far2[split:]], axis=0))
    side3 = side(far3)
    x2 = twin(jnp.concatenate([side2[split:], far3[split:]], axis=0))
    x3 = twin(side3[split:])
    n = 2 * half
    chunks = [
        join(([w_input], [w_down]), blocks(side0, x0[:n])),
        join(blocks(near1, x0[n:]), blocks(side1, x1[:n])),
        join(blocks(far2, x1[n:]), blocks(side2, x2[:n])),
        join(blocks(far3, x2[n:]), blocks(side3, x3)),
    ]
    return chunks


def gather_any(w_input, w_down, count):
    groups = [list(range(core, count, 2)) for core in range(2)]
    w_in = lax.all_gather(w_input, "wide", axis=0, tiled=True, axis_index_groups=groups)
    down = lax.all_gather(w_down, "wide", axis=0, tiled=True, axis_index_groups=groups)
    return [([w_in], [down])]


def local(
    tokens, item_lengths, w_query, w_key, w_value, w_output, w_input, w_down,
    norm_attn, norm_ffn, norm_final, owner, cluster_slot, coarse, centroids,
):
    packs, seq, width = tokens.shape
    per_pack = item_lengths.shape[1]
    wide_count = lax.axis_size("wide")
    items_dev = packs * per_pack
    capacity = max(2, 2 * items_dev // wide_count)
    slots = wide_count * capacity
    local_clusters, codes_count, _ = centroids.shape
    sibling = flip("wide", wide_count, 1)

    if wide_count == 16:
        chunks = gather_sixteen(w_input, w_down)
    else:
        chunks = gather_any(w_input, w_down, wide_count)

    gain = norm_attn[None]
    gain2 = norm_ffn[None]
    normed, pooled = [], []
    for pack in range(packs):
        a, b = encode_pack(
            item_lengths[pack : pack + 1], tokens[pack], w_query, w_key, w_value, w_output, gain, gain2
        )
        normed.append(a)
        pooled.append(b)
    normed = jnp.concatenate(normed, axis=0)
    pooled = jnp.concatenate(pooled, axis=0)
    both_lengths = (item_lengths, sibling(item_lengths))
    both_normed = (normed, sibling(normed))

    acc = None
    for w_in, down in chunks:
        acc = feed(both_lengths, both_normed, w_in, down, acc)
    other = sibling(acc[1])

    target = owner[:, 0]
    onehot = (target[:, None] == jnp.arange(wide_count, dtype=jnp.int32)[None, :]).astype(jnp.int32)
    earlier = jnp.cumsum(onehot, axis=0) - onehot
    slot_of = target * capacity + jnp.sum(earlier * onehot, axis=1)

    item_embed, send = pl.pallas_call(
        place_kernel,
        out_shape=(
            jax.ShapeDtypeStruct((items_dev, width), BF16),
            jax.ShapeDtypeStruct((slots, width + 128), BF16),
        ),
        compiler_params=params(),
        name="place",
    )(acc[0], other, pooled, norm_final[None], slot_of[None], cluster_slot[None])
    send = send.reshape(wide_count, capacity, width + 128)
    rows = lax.all_to_all(send, "wide", split_axis=0, concat_axis=0, tiled=True)
    codes = pl.pallas_call(
        code_kernel,
        out_shape=jax.ShapeDtypeStruct((slots, codes_count), BF16),
        compiler_params=params(),
        name="codes",
    )(rows.reshape(slots, width + 128), coarse, centroids)
    codes = codes.reshape(wide_count, capacity, codes_count)
    returned = lax.all_to_all(codes, "wide", split_axis=0, concat_axis=0, tiled=True)
    taking = (slot_of[:, None] == jnp.arange(slots, dtype=jnp.int32)[None, :]).astype(BF16)
    item_codes = jnp.dot(taking, returned.reshape(slots, codes_count), preferred_element_type=F32)
    return (item_embed, item_codes)


def solution(mesh):
    return jax.shard_map(
        local,
        mesh=mesh,
        in_specs=(
            P(("groups", "wide"), None, None),
            P(("groups", "wide"), None),
            P(),
            P(),
            P(),
            P(),
            P("wide", None),
            P("wide", None),
            P(),
            P(),
            P(),
            P(("groups", "wide"), None),
            P(("groups", "wide")),
            P("wide", None),
            P("wide", None, None),
        ),
        out_specs=(P(("groups", "wide"), None), P(("groups", "wide"), None)),
        check_vma=False,
    )
```

time: 179 us -> 136 us (0.76)
  Pallas kernels: 0 us -> 51 us
  matrix products: 50.2 us -> 0.86 us
  waiting for transfers between devices: 59.6 us -> 29.7 us
  between operations: 14.3 us -> 0.83 us
  local copies, waits for them, and re-layouts: 22.6 us -> 16.5 us
  starting transfers between devices: 11.7 us -> 17 us
  other arithmetic: 6.42 us -> 1.88 us
  blocking collectives: 13.3 us -> 17.8 us
    pallas_call x0 -> x8, Pallas kernels: none -> 51 us  [the longest x4 24.5 us: feed(): pl.pallas_call(functools.partial(feed_kernel, len(w_in), len(w_down), boo...]
    all_gather x2 -> x0, waiting for transfers between devices: 47.1 us -> none  [the longest x1 47.1 us: local(): lax.all_gather(w_down, 'wide', axis=0, tiled=True)]
    dot_general x13 -> x1, matrix products: 41.1 us -> 0.86 us  [local(): jnp.dot(taking, returned.reshape(slots, codes_count), preferred_element_t...]
    ppermute x0 -> x14, waiting for transfers between devices: none -> 21.8 us  [flip(): return lambda value: lax.ppermute(value, axis_name, pairs)]
    ppermute x0 -> x14, starting transfers between devices: none -> 13.1 us  [flip(): return lambda value: lax.ppermute(value, axis_name, pairs)]
    reshape x6 -> x0, local copies, waits for them, and re-layouts: 11.5 us -> none  [the longest x1 3.58 us: local(): keys = jnp.dot(normed, w_key, preferred_element_type=jnp.float32).astype(...]
    slice x0 -> x20, local copies, waits for them, and re-layouts: none -> 10.2 us  [the longest x11 8.35 us: blocks(): down = [main[common:split], main[split + half:], others[half:]]]
    sub x1 -> x0, matrix products: 9.04 us -> none  [local(): expo = jnp.exp(scores - top)]
  transfers between devices with their start and end apart: 4 -> 15, of which waited for: 2 -> 5; matrix products, arithmetic and copies ran while one was open for 41% -> 11% of each run, Pallas kernels for 0% -> 28%
where the time goes in v1:
time: 136 us
  Pallas kernels  51 us (38%)
  waiting for transfers between devices  29.7 us (22%)
  blocking collectives  17.8 us (13%)
  starting transfers between devices  17 us (12%)
  local copies, waits for them, and re-layouts  16.5 us (12%)
  other arithmetic  1.88 us (1%)
    pallas_call x4, Pallas kernels, feed(): pl.pallas_call(functools.partial(feed_kernel, len(w_in), len(w_down), boo...  24.5 us
    ppermute x14, waiting for transfers between devices, flip(): return lambda value: lax.ppermute(value, axis_name, pairs)  21.8 us
    pallas_call x2, Pallas kernels, encode_pack(): pl.pallas_call(encoder_kernel, out_shape=(jax.ShapeDtypeStruct((seq, widt...  19.5 us
    all_to_all x1, blocking collectives, local(): rows = lax.all_to_all(send, 'wide', split_axis=0, concat_axis=0, tiled=True)  17.8 us
    ppermute x14, starting transfers between devices, flip(): return lambda value: lax.ppermute(value, axis_name, pairs)  13.1 us
    slice x11, local copies, waits for them, and re-layouts, blocks(): down = [main[common:split], main[split + half:], others[half:]]  8.35 us
    all_to_all x1, waiting for transfers between devices, local(): lax.all_to_all(codes, 'wide', split_axis=0, concat_axis=0, tiled=True)  7.92 us
    pallas_call x1, Pallas kernels, local(): pl.pallas_call(code_kernel, out_shape=jax.ShapeDtypeStruct((slots, codes_...  4.53 us
  transfers between devices with their start and end apart: 15, of which 5 were waited for; matrix products, arithmetic and copies ran while one was open for 11% of the time, Pallas kernels for 28%

profile of v1, /device:TPU:0, one launch (start us, length us, event | category | flops | bytes accessed | tf_op | source)
XLA Modules:
  0.0 135.7 jit_solution(518179932909082306)
XLA Ops:
  0.7 1.2 fusion.14
  1.9 3.1 %collective-permute-start.8 = (bf16[256,768]{1,0:T(8,128)(2,1)S(1)}, bf16[256,768]{1,0:T(8,128)(2,1)S(1)}, u32[]{:S(2)}, u32[]{:S(2)}) collective-permute-start(bf16[256,768]{1,0:T(8,128)(2,1)S(1)} %pad_maximum_fusion), channel_id=1, source_target_pairs={{0,4},{1,5},{2,6},{3,7},{4,0},{5,1},{6,2},{7,3},{8,12},{9,13},{10,... | collective-permute-start | bytes 1179656 | tf_op jit(solution)/shard_map/ppermute | solution.py:184
  4.9 1.5 %collective-permute-start.11 = (bf16[256,768]{1,0:T(8,128)(2,1)S(1)}, bf16[256,768]{1,0:T(8,128)(2,1)S(1)}, u32[]{:S(2)}, u32[]{:S(2)}) collective-permute-start(bf16[256,768]{1,0:T(8,128)(2,1)S(1)} %pad_maximum_fusion), channel_id=1, source_target_pairs={{0,2},{1,3},{2,0},{3,1},{4,6},{5,7},{6,4},{7,5},{8,10},{9,11},{10,... | collective-permute-start | bytes 1179656 | tf_op jit(solution)/shard_map/ppermute | solution.py:184
  6.5 2.5 %collective-permute-start.2 = (bf16[256,768]{1,0:T(8,128)(2,1)S(1)}, bf16[256,768]{1,0:T(8,128)(2,1)S(1)}, u32[]{:S(2)}, u32[]{:S(2)}) collective-permute-start(bf16[256,768]{1,0:T(8,128)(2,1)S(1)} %pad_maximum_fusion), channel_id=1, source_target_pairs={{0,12},{1,13},{2,14},{3,15},{4,8},{5,9},{6,10},{7,11},{8,4},{9,5},... | collective-permute-start | bytes 1179656 | tf_op jit(solution)/shard_map/ppermute | solution.py:184
  9.6 1.1 slice_bitcast_fusion
  11.8 9.7 %encode_pack.2 = (bf16[384,768]{1,0:T(8,128)(2,1)}, f32[64,768]{1,0:T(8,128)}) custom-call(s32[1,64]{1,0:T(1,128)} %get-tuple-element.79.lengths_ref, bf16[384,768]{1,0:T(8,128)(2,1)} %get-tuple-element.31.x_ref, bf16[768,768]{1,0:T(8,128)(2,1)} %wq_ref.3, bf16[768,768]{1,0:T(8,128)(2,1)} %wk_ref.3, bf16[768,768]{1,0:T(8,128)(2,1)} %wv_ref.3, ...), custom_call_target="tpu_custom_call" | custom-call | flops 3623878656 | bytes 7077888 | tf_op jit(solution)/shard_map/encode_pack/pallas_call | solution.py:104
  21.5 9.8 %encode_pack.3 = (bf16[384,768]{1,0:T(8,128)(2,1)}, f32[64,768]{1,0:T(8,128)}) custom-call(s32[1,64]{1,0:T(1,128)} %get-tuple-element.78.lengths_ref, bf16[384,768]{1,0:T(8,128)(2,1)} %get-tuple-element.30.x_ref, bf16[768,768]{1,0:T(8,128)(2,1)} %wq_ref.3, bf16[768,768]{1,0:T(8,128)(2,1)} %wk_ref.3, bf16[768,768]{1,0:T(8,128)(2,1)} %wv_ref.3, ...), custom_call_target="tpu_custom_call" | custom-call | flops 3623878656 | bytes 7077888 | tf_op jit(solution)/shard_map/encode_pack/pallas_call | solution.py:104
  31.4 0.9 constant_dynamic-update-slice_fusion.1
  32.6 0.9 constant_dynamic-update-slice_fusion.refs_2_
  34.3 1.6 %collective-permute-start.12 = (bf16[256,768]{1,0:T(8,128)(2,1)S(1)}, bf16[256,768]{1,0:T(8,128)(2,1)S(1)}, u32[]{:S(2)}, u32[]{:S(2)}) collective-permute-start(bf16[256,768]{1,0:T(8,128)(2,1)S(1)} %pad_maximum_fusion.3), channel_id=1, source_target_pairs={{0,16},{16,0},{1,17},{17,1},{2,18},{18,2},{3,19},{19,3},{4,20},{20... | collective-permute-start | bytes 1179656 | tf_op jit(solution)/shard_map/ppermute | solution.py:184
  39.4 7.2 %collective-permute-done.9 = bf16[256,768]{1,0:T(8,128)(2,1)S(1)} collective-permute-done((bf16[256,768]{1,0:T(8,128)(2,1)S(1)}, bf16[256,768]{1,0:T(8,128)(2,1)S(1)}, u32[]{:S(2)}, u32[]{:S(2)}) %collective-permute-start.9) | collective-permute-done | bytes 393248 | tf_op jit(solution)/shard_map/ppermute | solution.py:184
  49.3 7.2 %collective-permute-done.4 = bf16[256,768]{1,0:T(8,128)(2,1)S(1)} collective-permute-done((bf16[256,768]{1,0:T(8,128)(2,1)S(1)}, bf16[256,768]{1,0:T(8,128)(2,1)S(1)}, u32[]{:S(2)}, u32[]{:S(2)}) %collective-permute-start.4) | collective-permute-done | bytes 393248 | tf_op jit(solution)/shard_map/ppermute | solution.py:184
  59.2 6.2 %collective-permute-done.6 = bf16[256,768]{1,0:T(8,128)(2,1)S(1)} collective-permute-done((bf16[256,768]{1,0:T(8,128)(2,1)S(1)}, bf16[256,768]{1,0:T(8,128)(2,1)S(1)}, u32[]{:S(2)}, u32[]{:S(2)}) %collective-permute-start.6) | collective-permute-done | bytes 393248 | tf_op jit(solution)/shard_map/ppermute | solution.py:184
  66.8 1.2 collective-permute-done.5
  69.3 5.9 %feed.4 = (f32[128,768]{1,0:T(8,128)}, f32[128,768]{1,0:T(8,128)}) custom-call(s32[2,64]{1,0:T(2,128)} %refs_0_.7, s32[2,64]{1,0:T(2,128)} %copy-done.11, bf16[768,768]{1,0:T(8,128)(2,1)} %constant_dynamic-update-slice_fusion.refs_2_, bf16[768,768]{1,0:T(8,128)(2,1)} %collective-permute-done.1.refs_3_, bf16[192,768]{1,0:T(8,128)(2,1)} %refs_4_.1, ...), custom_call_target="tpu_custom_call" | custom-call | flops 1358954496 | bytes 3538944 | tf_op jit(solution)/shard_map/feed/pallas_call | solution.py:143
  75.3 6.2 %feed.5 = (f32[128,768]{1,0:T(8,128)}, f32[128,768]{1,0:T(8,128)}) custom-call(s32[2,64]{1,0:T(2,128)} %refs_0_.7, s32[2,64]{1,0:T(2,128)} %copy-done.11, bf16[768,768]{1,0:T(8,128)(2,1)} %constant_dynamic-update-slice_fusion.refs_2_, bf16[768,768]{1,0:T(8,128)(2,1)} %collective-permute-done.1.refs_3_, bf16[64,768]{1,0:T(8,128)(2,1)} %get-tuple-element.51.refs_4_, ...), custom_call_target="tpu_custom_call" | custom-call | flops 1358954496 | bytes 3538944 | tf_op jit(solution)/shard_map/feed/pallas_call | solution.py:143
  81.4 6.2 %feed.6 = (f32[128,768]{1,0:T(8,128)}, f32[128,768]{1,0:T(8,128)}) custom-call(s32[2,64]{1,0:T(2,128)} %refs_0_.7, s32[2,64]{1,0:T(2,128)} %copy-done.11, bf16[768,768]{1,0:T(8,128)(2,1)} %constant_dynamic-update-slice_fusion.refs_2_, bf16[768,768]{1,0:T(8,128)(2,1)} %collective-permute-done.1.refs_3_, bf16[64,768]{1,0:T(8,128)(2,1)} %get-tuple-element.63.refs_4_, ...), custom_call_target="tpu_custom_call" | custom-call | flops 1358954496 | bytes 3538944 | tf_op jit(solution)/shard_map/feed/pallas_call | solution.py:143
  89.1 6.2 %feed.7 = (f32[128,768]{1,0:T(8,128)}, f32[128,768]{1,0:T(8,128)}) custom-call(s32[2,64]{1,0:T(2,128)} %refs_0_.7, s32[2,64]{1,0:T(2,128)} %copy-done.11, bf16[768,768]{1,0:T(8,128)(2,1)} %constant_dynamic-update-slice_fusion.refs_2_, bf16[768,768]{1,0:T(8,128)(2,1)} %collective-permute-done.1.refs_3_, bf16[64,768]{1,0:T(8,128)(2,1)} %get-tuple-element.71.refs_4_, ...), custom_call_target="tpu_custom_call" | custom-call | flops 1358954496 | bytes 3538944 | tf_op jit(solution)/shard_map/feed/pallas_call | solution.py:143
  98.2 2.4 %place.1 = (bf16[128,768]{1,0:T(8,128)(2,1)}, bf16[256,896]{1,0:T(8,128)(2,1)}) custom-call(f32[128,768]{1,0:T(8,128)} %get-tuple-element.24.acc_ref, f32[128,768]{1,0:T(8,128)} %copy-done.3, f32[128,768]{1,0:T(8,128)} %pad_maximum_fusion.4.pooled_ref, f32[1,768]{1,0:T(1,128)} %broadcast_in_dim.18.gain_ref, s32[1,128]{1,0:T(1,128)} %bitcast_add_fusion.1.slot_ref, ...), custom_call_target="tpu_custom_call" | custom-call | tf_op jit(solution)/shard_map/place/pallas_call | solution.py:279
  100.6 17.8 %all_to_all.10 = bf16[16,16,896]{2,1,0:T(8,128)(2,1)} all-to-all(bf16[16,16,896]{2,1,0:T(8,128)(2,1)} %bitcast.24), channel_id=1, replica_groups=mesh['groups'=2,'wide'=16] {'wide'}, dimensions={0} | all-to-all | bytes 917504 | tf_op jit(solution)/shard_map/all_to_all | solution.py:289
  118.5 4.5 %codes.1 = bf16[256,256]{1,0:T(8,128)(2,1)} custom-call(bf16[256,896]{1,0:T(8,128)(2,1)} %bitcast.21, bf16[8,768]{1,0:T(8,128)(2,1)} %coarse_ref.1, bf16[8,256,768]{2,1,0:T(8,128)(2,1)} %books_ref.1), custom_call_target="tpu_custom_call" | custom-call | tf_op jit(solution)/shard_map/codes/pallas_call | solution.py:290
  123.0 3.9 %all-to-all-start.1 = ((bf16[16,16,256]{2,1,0:T(8,128)(2,1)}), bf16[16,16,256]{2,1,0:T(8,128)(2,1)S(1)}, u32[]{:S(2)}, u32[]{:S(2)}) async-start(bf16[16,16,256]{2,1,0:T(8,128)(2,1)} %bitcast.22), calls=%async_computation.1 | async-start | bytes 262144 | tf_op jit(solution)/shard_map/all_to_all | solution.py:297
  126.9 7.9 %all-to-all-done.1 = bf16[16,16,256]{2,1,0:T(8,128)(2,1)S(1)} async-done(((bf16[16,16,256]{2,1,0:T(8,128)(2,1)}), bf16[16,16,256]{2,1,0:T(8,128)(2,1)S(1)}, u32[]{:S(2)}, u32[]{:S(2)}) %all-to-all-start.1) | async-done | bytes 131104 | tf_op jit(solution)/shard_map/all_to_all | solution.py:297
  134.8 0.9 fusion
  (76 shorter events, 19.0 us)
Async XLA Ops:
  0.6 8.3 %copy-start.10 = (s32[2,64]{1,0:T(2,128)S(1)}, s32[2,64]{1,0:T(2,128)}, u32[]{:S(2)}) copy-start(s32[2,64]{1,0:T(2,128)} %refs_0_.7) | copy-start | bytes 1540
  0.6 8.9 %copy-start = (bf16[2,384,768]{2,1,0:T(8,128)(2,1)S(1)}, bf16[2,384,768]{2,1,0:T(8,128)(2,1)}, u32[]{:S(2)}) copy-start(bf16[2,384,768]{2,1,0:T(8,128)(2,1)} %param.15) | copy-start | bytes 3538948
  1.9 32.4 %collective-permute-start.8 = (bf16[256,768]{1,0:T(8,128)(2,1)S(1)}, bf16[256,768]{1,0:T(8,128)(2,1)S(1)}, u32[]{:S(2)}, u32[]{:S(2)}) collective-permute-start(bf16[256,768]{1,0:T(8,128)(2,1)S(1)} %pad_maximum_fusion), channel_id=1, source_target_pairs={{0,4},{1,5},{2,6},{3,7},{4,0},{5,1},{6,2},{7,3},{8,12},{9,13},{10,... | collective-permute-start | bytes 1179656 | tf_op jit(solution)/shard_map/ppermute | solution.py:184
  4.9 29.3 %collective-permute-start.11 = (bf16[256,768]{1,0:T(8,128)(2,1)S(1)}, bf16[256,768]{1,0:T(8,128)(2,1)S(1)}, u32[]{:S(2)}, u32[]{:S(2)}) collective-permute-start(bf16[256,768]{1,0:T(8,128)(2,1)S(1)} %pad_maximum_fusion), channel_id=1, source_target_pairs={{0,2},{1,3},{2,0},{3,1},{4,6},{5,7},{6,4},{7,5},{8,10},{9,11},{10,... | collective-permute-start | bytes 1179656 | tf_op jit(solution)/shard_map/ppermute | solution.py:184
  6.5 30.7 %collective-permute-start.2 = (bf16[256,768]{1,0:T(8,128)(2,1)S(1)}, bf16[256,768]{1,0:T(8,128)(2,1)S(1)}, u32[]{:S(2)}, u32[]{:S(2)}) collective-permute-start(bf16[256,768]{1,0:T(8,128)(2,1)S(1)} %pad_maximum_fusion), channel_id=1, source_target_pairs={{0,12},{1,13},{2,14},{3,15},{4,8},{5,9},{6,10},{7,11},{8,4},{9,5},... | collective-permute-start | bytes 1179656 | tf_op jit(solution)/shard_map/ppermute | solution.py:184
  8.9 59.8 %collective-permute-start = (s32[2,64]{1,0:T(2,128)S(1)}, s32[2,64]{1,0:T(2,128)S(1)}, u32[]{:S(2)}, u32[]{:S(2)}) collective-permute-start(s32[2,64]{1,0:T(2,128)S(1)} %copy-done.10), channel_id=1, source_target_pairs={{0,1},{1,0},{2,3},{3,2},{4,5},{5,4},{6,7},{7,6},{8,9},{9,8},{10,11... | collective-permute-start | bytes 1544 | tf_op jit(solution)/shard_map/ppermute | solution.py:184
  9.6 1.7 %copy-start.7 = (f32[768]{0:T(1024)S(1)}, f32[768]{0:T(1024)}, u32[]{:S(2)}) copy-start(f32[768]{0:T(1024)} %param.24) | copy-start | bytes 9220
  21.5 9.8 %copy-start.1 = (bf16[384,768]{1,0:T(8,128)(2,1)S(1)}, bf16[384,768]{1,0:T(8,128)(2,1)}, u32[]{:S(2)}) copy-start(bf16[384,768]{1,0:T(8,128)(2,1)} %get-tuple-element.16) | copy-start | bytes 1769476
  31.3 1.3 copy-start.2
  31.3 2.6 %copy-start.9 = (s32[128,1]{0,1:T(1,128)S(1)}, s32[128,1]{0,1:T(1,128)}, u32[]{:S(2)}) copy-start(s32[128,1]{0,1:T(1,128)} %param.26) | copy-start | bytes 1540
  33.5 35.3 %collective-permute-start.1 = (bf16[768,768]{1,0:T(8,128)(2,1)}, bf16[768,768]{1,0:T(8,128)(2,1)}, u32[]{:S(2)}, u32[]{:S(2)}) collective-permute-start(bf16[768,768]{1,0:T(8,128)(2,1)} %constant_dynamic-update-slice_fusion.refs_2_), channel_id=1, source_target_pairs={{0,1},{1,0},{2,3},{3,2},{4,5},{5,4},{6,7},{7,6},{8,9},{9,8},{10,11... | collective-permute-start | bytes 3538952 | tf_op jit(solution)/shard_map/ppermute | solution.py:184
  34.3 23.5 %collective-permute-start.12 = (bf16[256,768]{1,0:T(8,128)(2,1)S(1)}, bf16[256,768]{1,0:T(8,128)(2,1)S(1)}, u32[]{:S(2)}, u32[]{:S(2)}) collective-permute-start(bf16[256,768]{1,0:T(8,128)(2,1)S(1)} %pad_maximum_fusion.3), channel_id=1, source_target_pairs={{0,16},{16,0},{1,17},{17,1},{2,18},{18,2},{3,19},{19,3},{4,20},{20... | collective-permute-start | bytes 1179656 | tf_op jit(solution)/shard_map/ppermute | solution.py:184
  35.9 10.7 %collective-permute-start.9 = (bf16[256,768]{1,0:T(8,128)(2,1)S(1)}, bf16[256,768]{1,0:T(8,128)(2,1)S(1)}, u32[]{:S(2)}, u32[]{:S(2)}) collective-permute-start(bf16[256,768]{1,0:T(8,128)(2,1)S(1)} %collective-permute-done.8), channel_id=1, source_target_pairs={{0,2},{1,3},{2,0},{3,1},{4,6},{5,7},{6,4},{7,5},{8,10},{9,11},{10,... | collective-permute-start | bytes 1179656 | tf_op jit(solution)/shard_map/ppermute | solution.py:184
  37.2 10.8 %collective-permute-start.3 = (bf16[256,768]{1,0:T(8,128)(2,1)S(1)}, bf16[256,768]{1,0:T(8,128)(2,1)S(1)}, u32[]{:S(2)}, u32[]{:S(2)}) collective-permute-start(bf16[256,768]{1,0:T(8,128)(2,1)S(1)} %collective-permute-done.2), channel_id=1, source_target_pairs={{0,4},{1,5},{2,6},{3,7},{4,0},{5,1},{6,2},{7,3},{8,12},{9,13},{10,... | collective-permute-start | bytes 1179656 | tf_op jit(solution)/shard_map/ppermute | solution.py:184
  46.6 9.9 %collective-permute-start.4 = (bf16[256,768]{1,0:T(8,128)(2,1)S(1)}, bf16[256,768]{1,0:T(8,128)(2,1)S(1)}, u32[]{:S(2)}, u32[]{:S(2)}) collective-permute-start(bf16[256,768]{1,0:T(8,128)(2,1)S(1)} %collective-permute-done.2), channel_id=1, source_target_pairs={{0,2},{1,3},{2,0},{3,1},{4,6},{5,7},{6,4},{7,5},{8,10},{9,11},{10,... | collective-permute-start | bytes 1179656 | tf_op jit(solution)/shard_map/ppermute | solution.py:184
  48.0 18.1 %collective-permute-start.10 = (bf16[256,768]{1,0:T(8,128)(2,1)S(1)}, bf16[256,768]{1,0:T(8,128)(2,1)S(1)}, u32[]{:S(2)}, u32[]{:S(2)}) collective-permute-start(bf16[256,768]{1,0:T(8,128)(2,1)S(1)} %pad_maximum_fusion.2), channel_id=1, source_target_pairs={{0,16},{16,0},{1,17},{17,1},{2,18},{18,2},{3,19},{19,3},{4,20},{20... | collective-permute-start | bytes 1179656 | tf_op jit(solution)/shard_map/ppermute | solution.py:184
  56.5 8.9 %collective-permute-start.6 = (bf16[256,768]{1,0:T(8,128)(2,1)S(1)}, bf16[256,768]{1,0:T(8,128)(2,1)S(1)}, u32[]{:S(2)}, u32[]{:S(2)}) collective-permute-start(bf16[256,768]{1,0:T(8,128)(2,1)S(1)} %collective-permute-done.3), channel_id=1, source_target_pairs={{0,2},{1,3},{2,0},{3,1},{4,6},{5,7},{6,4},{7,5},{8,10},{9,11},{10,... | collective-permute-start | bytes 1179656 | tf_op jit(solution)/shard_map/ppermute | solution.py:184
  57.9 10.1 %collective-permute-start.5 = (bf16[256,768]{1,0:T(8,128)(2,1)S(1)}, bf16[256,768]{1,0:T(8,128)(2,1)S(1)}, u32[]{:S(2)}, u32[]{:S(2)}) collective-permute-start(bf16[256,768]{1,0:T(8,128)(2,1)S(1)} %pad_maximum_fusion.1), channel_id=1, source_target_pairs={{0,16},{16,0},{1,17},{17,1},{2,18},{18,2},{3,19},{19,3},{4,20},{20... | collective-permute-start | bytes 1179656 | tf_op jit(solution)/shard_map/ppermute | solution.py:184
  65.4 23.0 %collective-permute-start.7 = (bf16[128,768]{1,0:T(8,128)(2,1)S(1)}, bf16[128,768]{1,0:T(8,128)(2,1)S(1)}, u32[]{:S(2)}, u32[]{:S(2)}) collective-permute-start(bf16[128,768]{1,0:T(8,128)(2,1)S(1)} %slice.245), channel_id=1, source_target_pairs={{0,16},{16,0},{1,17},{17,1},{2,18},{18,2},{3,19},{19,3},{4,20},{20... | collective-permute-start | bytes 589832 | tf_op jit(solution)/shard_map/ppermute | solution.py:184
  89.1 6.4 %copy-start.8 = (f32[768]{0:T(1024)S(1)}, f32[768]{0:T(1024)}, u32[]{:S(2)}) copy-start(f32[768]{0:T(1024)} %param.25) | copy-start | bytes 9220
  89.1 7.0 %copy-start.4 = (f32[64,768]{1,0:T(8,128)S(1)}, f32[64,768]{1,0:T(8,128)}, u32[]{:S(2)}) copy-start(f32[64,768]{1,0:T(8,128)} %get-tuple-element.26) | copy-start | bytes 589828
  89.1 7.0 %copy-start.5 = (f32[64,768]{1,0:T(8,128)S(1)}, f32[64,768]{1,0:T(8,128)}, u32[]{:S(2)}) copy-start(f32[64,768]{1,0:T(8,128)} %get-tuple-element.27) | copy-start | bytes 589828
  95.3 2.1 %collective-permute-start.13 = (f32[128,768]{1,0:T(8,128)}, f32[128,768]{1,0:T(8,128)S(1)}, u32[]{:S(2)}, u32[]{:S(2)}) collective-permute-start(f32[128,768]{1,0:T(8,128)} %get-tuple-element.25), channel_id=1, source_target_pairs={{0,1},{1,0},{2,3},{3,2},{4,5},{5,4},{6,7},{7,6},{8,9},{9,8},{10,11... | collective-permute-start | bytes 1179656 | tf_op jit(solution)/shard_map/ppermute | solution.py:184
  123.0 11.8 %all-to-all-start.1 = ((bf16[16,16,256]{2,1,0:T(8,128)(2,1)}), bf16[16,16,256]{2,1,0:T(8,128)(2,1)S(1)}, u32[]{:S(2)}, u32[]{:S(2)}) async-start(bf16[16,16,256]{2,1,0:T(8,128)(2,1)} %bitcast.22), calls=%async_computation.1 | async-start | bytes 262144 | tf_op jit(solution)/shard_map/all_to_all | solution.py:297
  (3 other events, 2.4 us)

commit v2 on v1

v2 whole, which is shorter than its diff:
```python
import functools

import jax
import jax.numpy as jnp
from jax import lax
from jax.experimental import pallas as pl
from jax.experimental.pallas import tpu as pltpu
from jax.sharding import PartitionSpec as P

HEADS = 12
EPS = 1e-06
VMEM_BYTES = 16 * 1024 * 1024
F32 = jnp.float32
BF16 = jnp.bfloat16


def params():
    return pltpu.CompilerParams(vmem_limit_bytes=VMEM_BYTES)


def cost():
    return pl.CostEstimate(flops=1000, bytes_accessed=1000, transcendentals=0)


def dot(a, b):
    return jnp.dot(a, b, preferred_element_type=F32)


def dot_nt(a, b):
    return lax.dot_general(a, b, (((1,), (1,)), ((), ())), preferred_element_type=F32)


def rms(values, gain):
    mean_sq = jnp.mean(values * values, axis=-1, keepdims=True)
    return values * lax.rsqrt(mean_sq + EPS) * gain


def item_rows(lengths, seq):
    items = lengths.shape[1]
    tri = (
        lax.broadcasted_iota(jnp.int32, (items, items), 0)
        <= lax.broadcasted_iota(jnp.int32, (items, items), 1)
    ).astype(F32)
    rows = jnp.broadcast_to(lengths.astype(F32), (8, items))
    ends = dot(rows.astype(BF16), tri.astype(BF16))[:1]
    starts = ends - rows[:1]
    place = lax.broadcasted_iota(jnp.int32, (seq, items), 0).astype(F32)
    return jnp.where((place < ends) & (place >= starts), 1.0, 0.0).astype(BF16)


def item_columns(lengths, seq):
    items = lengths.shape[1]
    row = lax.broadcasted_iota(jnp.int32, (items, items), 0)
    column = lax.broadcasted_iota(jnp.int32, (items, items), 1)
    rows = jnp.broadcast_to(lengths.astype(F32), (8, items)).astype(BF16)
    ends = dot_nt((column <= row).astype(F32).astype(BF16), rows)[:, :1]
    starts = dot_nt((column < row).astype(F32).astype(BF16), rows)[:, :1]
    place = lax.broadcasted_iota(jnp.int32, (items, seq), 1).astype(F32)
    return jnp.where((place < ends) & (place >= starts), 1.0, 0.0).astype(BF16)


def in_hbm(*arrays):
    return [pltpu.with_memory_space_constraint(a, pltpu.HBM) for a in arrays]


def project_kernel(
    other_ref, lengths_hbm, owner_hbm, gain_hbm, x_hbm, wq_hbm, wk_hbm, wv_hbm,
    q_ref, k_ref, v_ref, rows_ref, columns_ref, slot_ref,
    lengths_ref, owner_ref, gain_ref, x_ref, wq_ref, wk_ref, wv_ref, sems, *, wide, capacity,
):
    sources = (lengths_hbm, owner_hbm, gain_hbm, x_hbm, wq_hbm, wk_hbm, wv_hbm)
    here = (lengths_ref, owner_ref, gain_ref, x_ref, wq_ref, wk_ref, wv_ref)
    copies = [pltpu.make_async_copy(s, d, sems.at[i]) for i, (s, d) in enumerate(zip(sources, here))]
    for copy in copies:
        copy.start()
    for copy in copies[:3]:
        copy.wait()
    packs, seq, width = x_ref.shape
    per_pack = lengths_ref.shape[1]
    for pack in range(packs):
        rows_ref[pack * seq : (pack + 1) * seq] = item_rows(lengths_ref[pack : pack + 1], seq)
        for side, ref in enumerate((lengths_ref, other_ref)):
            at = (side * packs + pack) * per_pack
            columns_ref[at : at + per_pack] = item_columns(ref[pack : pack + 1], seq)
    owner = owner_ref[...]
    items = owner.shape[1]
    target = jnp.where(lax.broadcasted_iota(jnp.int32, (wide, items), 0) == owner, 1.0, 0.0)
    before = lax.broadcasted_iota(jnp.int32, (items, items), 0) < lax.broadcasted_iota(jnp.int32, (items, items), 1)
    earlier = dot(target.astype(BF16), jnp.where(before, 1.0, 0.0).astype(BF16))
    rank = jnp.sum(earlier * target, axis=0, keepdims=True)
    slot_ref[...] = owner * capacity + rank.astype(jnp.int32)
    gain = gain_ref[...]
    copies[3].wait()
    normed = [rms(x_ref[pack].astype(F32), gain).astype(BF16) for pack in range(packs)]
    normed = jnp.concatenate(normed, axis=0)
    for copy, w_ref, out_ref in zip(copies[4:], (wq_ref, wk_ref, wv_ref), (q_ref, k_ref, v_ref)):
        copy.wait()
        out_ref[...] = dot(normed, w_ref[...]).astype(BF16)


def project(lengths, other, owner, x, gain, wq, wk, wv, wide, capacity):
    packs, seq, width = x.shape
    items = lengths.shape[1]
    sources = (lengths, owner, gain, x, wq, wk, wv)
    return pl.pallas_call(
        functools.partial(project_kernel, wide=wide, capacity=capacity),
        in_specs=[pl.BlockSpec(memory_space=pltpu.VMEM)] + [pl.BlockSpec(memory_space=pltpu.HBM)] * len(sources),
        out_shape=(
            jax.ShapeDtypeStruct((packs * seq, width), BF16),
            jax.ShapeDtypeStruct((packs * seq, width), BF16),
            jax.ShapeDtypeStruct((packs * seq, width), BF16),
            jax.ShapeDtypeStruct((packs * seq, items), BF16),
            jax.ShapeDtypeStruct((2 * packs * items, seq), BF16),
            jax.ShapeDtypeStruct(owner.shape, jnp.int32),
        ),
        scratch_shapes=[pltpu.VMEM(a.shape, a.dtype) for a in sources]
        + [pltpu.SemaphoreType.DMA((len(sources),))],
        compiler_params=params(),
        cost_estimate=cost(),
        name="project",
    )(other, *in_hbm(*sources))


def hold_kernel(common, group_ref, w_in_hbm, w_down_hbm, held_ref, sems):
    half = (w_in_hbm.shape[0] - common) // 2
    start = pl.multiple_of(common + group_ref[0, 0] * half, 16)
    copies, at = [], 0
    for first, size in ((0, common), (start, half)):
        for source in (w_in_hbm, w_down_hbm):
            copies.append(
                pltpu.make_async_copy(source.at[pl.ds(first, size)], held_ref.at[pl.ds(at, size)], sems.at[len(copies)])
            )
            at += size
    for copy in copies:
        copy.start()
    for copy in copies:
        copy.wait()


def hold(w_input, w_down, common):
    rows, width = w_input.shape
    far = pl.BlockSpec(memory_space=pltpu.HBM)
    return pl.pallas_call(
        functools.partial(hold_kernel, common),
        in_specs=[pl.BlockSpec(memory_space=pltpu.SMEM), far, far],
        out_shape=jax.ShapeDtypeStruct((rows + common, width), BF16),
        scratch_shapes=[pltpu.SemaphoreType.DMA((4,))],
        compiler_params=params(),
        cost_estimate=cost(),
        name="hold",
    )(lax.axis_index("groups").astype(jnp.int32).reshape(1, 1), *in_hbm(w_input, w_down))


def attend_kernel(
    pack, q_ref, k_ref, v_ref, rows_ref, columns_ref, x_ref, wo_ref, gain_ref,
    normed2_ref, pooled_ref, ctx_ref,
):
    _, seq, width = x_ref.shape
    items = rows_ref.shape[1]
    head = width // HEADS
    base = pack * seq
    onehot = rows_ref[base : base + seq]
    block, window, lanes = 64, 128, 256
    heads = lanes // head
    lane_head = lax.broadcasted_iota(jnp.int32, (block, lanes), 1) // head
    for start in range(0, seq, block):
        first = min(max(start - (window - block) // 2, 0), seq - window)
        same = dot_nt(onehot[start : start + block], onehot[first : first + window])
        same = jnp.concatenate([same] * heads, axis=0) > 0.5
        keys = slice(base + first, base + first + window)
        for column in range(0, width, lanes):
            across = slice(column, column + lanes)
            query = q_ref[base + start : base + start + block, across]
            stacked = jnp.concatenate(
                [jnp.where(lane_head == h, query, jnp.zeros_like(query)) for h in range(heads)], axis=0
            )
            scores = jnp.where(same, dot_nt(stacked, k_ref[keys, across]), -1e30)
            expo = jnp.exp(scores - jnp.max(scores, axis=-1, keepdims=True))
            probs = (expo * (1.0 / jnp.sum(expo, axis=-1, keepdims=True))).astype(BF16)
            mixed = dot(probs, v_ref[keys, across])
            context = mixed[:block]
            for h in range(1, heads):
                context = jnp.where(lane_head == h, mixed[h * block : (h + 1) * block], context)
            ctx_ref[start : start + block, across] = context.astype(BF16)
    stream = (x_ref[pack].astype(F32) + dot(ctx_ref[...], wo_ref[...])).astype(BF16)
    normed2_ref[...] = rms(stream.astype(F32), gain_ref[...][None]).astype(BF16)
    pooled_ref[...] = dot(columns_ref[pack * items : (pack + 1) * items], stream)


def attend(pack, projected, x, wo, gain2):
    _, seq, width = x.shape
    items = projected[3].shape[1]
    return pl.pallas_call(
        functools.partial(attend_kernel, pack),
        out_shape=(
            jax.ShapeDtypeStruct((seq, width), BF16),
            jax.ShapeDtypeStruct((items, width), F32),
        ),
        scratch_shapes=[pltpu.VMEM((seq, width), BF16)],
        compiler_params=params(),
        cost_estimate=cost(),
        name="attend",
    )(*projected[:5], x, wo, gain2)


def feed_kernel(n_normed, n_held, pieces, n_base, columns_ref, *refs):
    normed_refs, refs = (refs[:n_normed], refs[n_normed : 2 * n_normed]), refs[2 * n_normed :]
    held, refs = refs[:n_held], refs[n_held:]
    bases, outs = (refs[: n_base[0]], refs[n_base[0] : sum(n_base)]), refs[sum(n_base) :]
    w_in = jnp.concatenate([held[i][r] for i, r, _, _ in pieces], axis=0)
    w_down = jnp.concatenate([held[i][r] for _, _, i, r in pieces], axis=0)
    packs = n_normed
    items = columns_ref.shape[0] // (2 * packs)
    for side in range(2):
        pooled = []
        for pack in range(packs):
            hidden = jnp.maximum(dot_nt(normed_refs[side][pack][...], w_in), 0.0).astype(BF16)
            at = (side * packs + pack) * items
            pooled.append(dot(columns_ref[at : at + items], hidden).astype(BF16))
        part = dot(jnp.concatenate(pooled, axis=0), w_down)
        if bases[side]:
            part = part + jnp.concatenate([r[...] for r in bases[side]], axis=0)
        outs[side][...] = part


def feed(columns, normed, held, pieces, bases):
    items = columns.shape[0] // 2
    width = held[0].shape[1]
    n_base = tuple(len(b) for b in bases)
    return pl.pallas_call(
        functools.partial(feed_kernel, len(normed[0]), len(held), pieces, n_base),
        out_shape=(jax.ShapeDtypeStruct((items, width), F32),) * 2,
        compiler_params=params(),
        cost_estimate=cost(),
        name="feed",
    )(columns, *normed[0], *normed[1], *held, *bases[0], *bases[1])


def place_kernel(acc_ref, other_ref, gain_ref, slot_ref, cluster_ref, embed_ref, send_ref):
    width = embed_ref.shape[1]
    embed = rms(acc_ref[...] + other_ref[...], gain_ref[...][None]).astype(BF16)
    embed_ref[...] = embed
    slots, items = send_ref.shape[0], embed.shape[0]
    placing = jnp.where(
        lax.broadcasted_iota(jnp.int32, (slots, items), 0) == slot_ref[...], 1.0, 0.0
    ).astype(BF16)
    send_ref[:, :width] = dot(placing, embed).astype(BF16)
    clusters = send_ref.shape[1] - width
    chosen = jnp.where(
        lax.broadcasted_iota(jnp.int32, (clusters, items), 0) == cluster_ref[...], 1.0, 0.0
    ).astype(BF16)
    send_ref[:, width:] = dot_nt(placing, chosen).astype(BF16)


def code_kernel(rows_ref, coarse_ref, books_ref, out_ref):
    clusters, codes, width = books_ref.shape
    slots = rows_ref.shape[0]
    spare = -clusters % 16
    coarse = jnp.concatenate([coarse_ref[...], jnp.zeros((spare, width), BF16)], axis=0)
    rows = jnp.concatenate([rows_ref[:, :width], coarse], axis=0)
    total = jnp.zeros((slots, codes), F32)
    for cluster in range(clusters):
        direct = dot_nt(rows, books_ref[cluster])
        offset = direct[slots + cluster : slots + cluster + 1]
        chosen = rows_ref[:, width + cluster : width + cluster + 1].astype(F32)
        total = total + (direct[:slots] - offset) * chosen
    out_ref[...] = total.astype(BF16)


def flip(axis_name, count, bits):
    pairs = [(i, i ^ bits) for i in range(count)]
    return lambda value: lax.ppermute(value, axis_name, pairs)


def gather_any(w_input, w_down, count):
    groups = [list(range(core, count, 2)) for core in range(2)]
    w_in = lax.all_gather(w_input, "wide", axis=0, tiled=True, axis_index_groups=groups)
    down = lax.all_gather(w_down, "wide", axis=0, tiled=True, axis_index_groups=groups)
    return w_in, down


def overlapped(w_input, w_down, tokens, encode_first, encode, sibling):
    rows = w_input.shape[0]
    common = rows // 3 // 16 * 16
    half = (rows - common) // 2
    split, both, every = 2 * common, 2 * half, 2 * (common + half)
    near, side, twin = flip("wide", 16, 4), flip("wide", 16, 2), flip("groups", 2, 1)
    line = lax.axis_index("wide") // 4
    inner = (line == 1) | (line == 2)

    def along(value, hops):
        pairs = [(4 * a + i, 4 * b + i) for a, b in hops for i in range(4)]
        return lax.ppermute(value, "wide", pairs)

    after = lax.optimization_barrier

    def blocks(i):
        return [
            (i, slice(0, common), i, slice(common, split)),
            (i, slice(split, split + half), i, slice(split + half, every)),
        ]

    def rest(i, at=0):
        return [(i, slice(at, at + half), i, slice(at + half, at + both))]

    def cat(a, b):
        return jnp.concatenate([a, b], axis=0)

    held = hold(w_input, w_down, common)
    side0, near1, middle = side(held), near(held), along(held, [(1, 2), (2, 1)])
    projected = encode_first(tokens)
    side0, near1, middle, projected = after((side0, near1, middle, projected))
    columns = projected[4]

    side1 = side(near1)
    far2 = along(jnp.where(inner, middle, held), [(1, 0), (0, 2), (2, 3), (3, 1)])
    x0 = twin(cat(side0[split:], near1[split:]))
    first = encode(0, projected, tokens)
    side1, x0, far2, first, projected = after((side1, x0, far2, first, projected))

    side2, outer = side(far2), along(far2, [(1, 0), (2, 3)])
    x1 = twin(cat(side1[split:], far2[split:]))
    other_first = sibling(first[0])
    second = encode(1, projected, tokens)
    side2, x1, outer, second, other_first = after((side2, x1, outer, second, other_first))

    far3 = jnp.where(inner, middle, outer)
    side3, x2 = side(far3), twin(cat(side2[split:], far3[split:]))
    normed = ((first[0], second[0]), (other_first, sibling(second[0])))
    own = [(0, slice(0, rows), 1, slice(0, rows))]
    pieces = own + blocks(2) + rest(3) + blocks(4) + rest(3, both) + blocks(5) + rest(6)
    acc = feed(columns, normed, [w_input, w_down, side0, x0, near1, side1, x1], pieces, ([first[1], second[1]], []))
    side3, x2, acc = after((side3, x2, acc))

    x3 = twin(side3[split:])
    pieces = blocks(0) + rest(1, both) + blocks(2) + rest(3) + blocks(4) + rest(3, both) + blocks(5)
    acc = feed(columns, normed, [far2, x1, side2, x2, far3, side3], pieces, ([acc[0]], [acc[1]]))
    x3, acc = after((x3, acc))
    acc = feed(columns, normed, [x3], rest(0), ([acc[0]], [acc[1]]))
    return acc, projected[5]


def local(
    tokens, item_lengths, w_query, w_key, w_value, w_output, w_input, w_down,
    norm_attn, norm_ffn, norm_final, owner, cluster_slot, coarse, centroids,
):
    packs, seq, width = tokens.shape
    per_pack = item_lengths.shape[1]
    wide_count = lax.axis_size("wide")
    items_dev = packs * per_pack
    capacity = max(2, 2 * items_dev // wide_count)
    slots = wide_count * capacity
    local_clusters, codes_count, _ = centroids.shape
    sibling = flip("wide", wide_count, 1)

    other_lengths = sibling(item_lengths)

    def encode_first(tokens):
        return project(
            item_lengths, other_lengths, owner.reshape(1, items_dev), tokens, norm_attn[None],
            w_query, w_key, w_value, wide_count, capacity,
        )

    def encode(pack, projected, tokens):
        return attend(pack, projected, tokens, w_output, norm_ffn)

    if wide_count == 16 and packs == 2:
        acc, slots_of = overlapped(w_input, w_down, tokens, encode_first, encode, sibling)
    else:
        projected = encode_first(tokens)
        slots_of = projected[5]
        normed, pooled = zip(*[encode(p, projected, tokens) for p in range(packs)])
        held = gather_any(w_input, w_down, wide_count)
        every = slice(0, held[0].shape[0])
        normed = (normed, [sibling(n) for n in normed])
        acc = feed(projected[4], normed, held, [(0, every, 1, every)], (pooled, []))
    other = sibling(acc[1])

    item_embed, send = pl.pallas_call(
        place_kernel,
        out_shape=(
            jax.ShapeDtypeStruct((items_dev, width), BF16),
            jax.ShapeDtypeStruct((slots, width + 128), BF16),
        ),
        compiler_params=params(),
        name="place",
    )(acc[0], other, norm_final, slots_of, cluster_slot[None])
    send = send.reshape(wide_count, capacity, width + 128)
    rows = lax.all_to_all(send, "wide", split_axis=0, concat_axis=0, tiled=True)
    codes = pl.pallas_call(
        code_kernel,
        out_shape=jax.ShapeDtypeStruct((slots, codes_count), BF16),
        compiler_params=params(),
        name="codes",
    )(rows.reshape(slots, width + 128), coarse, centroids)
    codes = codes.reshape(wide_count, capacity, codes_count)
    returned = lax.all_to_all(codes, "wide", split_axis=0, concat_axis=0, tiled=True)
    taking = (slots_of[0][:, None] == jnp.arange(slots, dtype=jnp.int32)[None, :]).astype(BF16)
    item_codes = jnp.dot(taking, returned.reshape(slots, codes_count), preferred_element_type=F32)
    return (item_embed, item_codes)


def solution(mesh):
    return jax.shard_map(
        local,
        mesh=mesh,
        in_specs=(
            P(("groups", "wide"), None, None),
            P(("groups", "wide"), None),
            P(),
            P(),
            P(),
            P(),
            P("wide", None),
            P("wide", None),
            P(),
            P(),
            P(),
            P(("groups", "wide"), None),
            P(("groups", "wide")),
            P("wide", None),
            P("wide", None, None),
        ),
        out_specs=(P(("groups", "wide"), None), P(("groups", "wide"), None)),
        check_vma=False,
    )
```

time: 136 us -> 100 us (0.74)
  Pallas kernels: 51 us -> 28.1 us
  local copies, waits for them, and re-layouts: 16.5 us -> 1.41 us
  blocking collectives: 17.8 us -> 29.8 us
  waiting for transfers between devices: 29.7 us -> 20.1 us
  other arithmetic: 1.88 us -> 0.17 us
  starting transfers between devices: 17 us -> 18.5 us
    pallas_call x6 -> x7, Pallas kernels: 44 us -> 26 us  [the longest x3 9.68 us: feed(): pl.pallas_call(functools.partial(feed_kernel, len(normed[0]), len(held),...]
    all_to_all x0 -> x1, blocking collectives: none -> 11.6 us  [local(): lax.all_to_all(codes, 'wide', split_axis=0, concat_axis=0, tiled=True)]
    slice x20 -> x7, local copies, waits for them, and re-layouts: 10.2 us -> 0.1 us  [the longest x2 0.03 us: overlapped(): side3, x2 = (side(far3), twin(cat(side2[split:], far3[split:])))]
    all_to_all x1 -> x0, waiting for transfers between devices: 7.92 us -> none  [local(): lax.all_to_all(codes, 'wide', split_axis=0, concat_axis=0, tiled=True)]
    ppermute x14 -> x13, waiting for transfers between devices: 21.8 us -> 16.7 us  [flip(): return lambda value: lax.ppermute(value, axis_name, pairs)]
    all_to_all x1 -> x0, starting transfers between devices: 3.89 us -> none  [local(): lax.all_to_all(codes, 'wide', split_axis=0, concat_axis=0, tiled=True)]
    ppermute x0 -> x3, waiting for transfers between devices: none -> 3.45 us  [along(): return lax.ppermute(value, 'wide', pairs)]
    pallas_call x1, Pallas kernels: 4.53 us -> 1.3 us  [local(): pl.pallas_call(code_kernel, out_shape=jax.ShapeDtypeStruct((slots, codes_...]
  transfers between devices with their start and end apart: 15 -> 16, of which waited for: 5 -> 12; matrix products, arithmetic and copies ran while one was open for 11% -> 1% of each run, Pallas kernels for 28% -> 23%
where the time goes in v2:
time: 100 us; the launch traced here: 99.8 us
  blocking collectives  29.8 us (30%)
  Pallas kernels  28.1 us (28%)
  waiting for transfers between devices  20.1 us (20%)
  starting transfers between devices  18.5 us (18%)
  local copies, waits for them, and re-layouts  1.41 us (1%)
    all_to_all x1, blocking collectives, local(): rows = lax.all_to_all(send, 'wide', split_axis=0, concat_axis=0, tiled=True)  18.2 us
    ppermute x13, waiting for transfers between devices, flip(): return lambda value: lax.ppermute(value, axis_name, pairs)  16.7 us
    ppermute x13, starting transfers between devices, flip(): return lambda value: lax.ppermute(value, axis_name, pairs)  16.1 us
    all_to_all x1, blocking collectives, local(): lax.all_to_all(codes, 'wide', split_axis=0, concat_axis=0, tiled=True)  11.6 us
    pallas_call x3, Pallas kernels, feed(): pl.pallas_call(functools.partial(feed_kernel, len(normed[0]), len(held),...  9.68 us
    pallas_call x2, Pallas kernels, attend(): pl.pallas_call(functools.partial(attend_kernel, pack), out_shape=(jax.Sha...  9.52 us
    pallas_call x1, Pallas kernels, project(): pl.pallas_call(functools.partial(project_kernel, wide=wide, capacity=capa...  5.68 us
    ppermute x3, waiting for transfers between devices, along(): return lax.ppermute(value, 'wide', pairs)  3.45 us
  transfers between devices with their start and end apart: 16, of which 12 were waited for; matrix products, arithmetic and copies ran while one was open for 1% of the time, Pallas kernels for 23%

profile of v2, /device:TPU:0, one launch (start us, length us, event | category | flops | bytes accessed | tf_op | source)
XLA Modules:
  0.0 99.8 jit_solution(16109241008576831750)
XLA Ops:
  2.4 5.9 %collective-permute-start.1 = (bf16[256,768]{1,0:T(8,128)(2,1)S(1)}, bf16[256,768]{1,0:T(8,128)(2,1)S(1)}, u32[]{:S(2)}, u32[]{:S(2)}) collective-permute-start(bf16[256,768]{1,0:T(8,128)(2,1)S(1)} %hold.1), channel_id=1, source_target_pairs={{0,4},{1,5},{2,6},{3,7},{4,0},{5,1},{6,2},{7,3},{8,12},{9,13},{10,... | collective-permute-start | bytes 1179656 | tf_op jit(solution)/shard_map/ppermute | solution.py:272
  8.3 1.5 %collective-permute-start = (bf16[256,768]{1,0:T(8,128)(2,1)S(1)}, bf16[256,768]{1,0:T(8,128)(2,1)S(1)}, u32[]{:S(2)}, u32[]{:S(2)}) collective-permute-start(bf16[256,768]{1,0:T(8,128)(2,1)S(1)} %hold.1), channel_id=1, source_target_pairs={{0,2},{1,3},{2,0},{3,1},{4,6},{5,7},{6,4},{7,5},{8,10},{9,11},{10,... | collective-permute-start | bytes 1179656 | tf_op jit(solution)/shard_map/ppermute | solution.py:272
  11.2 5.7 %project.1 = (bf16[768,768]{1,0:T(8,128)(2,1)S(1)}, bf16[768,768]{1,0:T(8,128)(2,1)S(1)}, bf16[768,768]{1,0:T(8,128)(2,1)S(1)}, bf16[768,64]{1,0:T(8,128)(2,1)S(...) custom-call(s32[2,64]{1,0:T(2,128)S(1)} %collective-permute-done.3.other_ref, s32[2,64]{1,0:T(2,128)} %lengths_hbm.1, ...), custom_call_target="tpu_custom_call" | custom-call | flops 1000 | bytes 1000 | tf_op jit(solution)/shard_map/project/pallas_call | solution.py:105
  17.1 1.5 %collective-permute-done.refs_6_ = bf16[256,768]{1,0:T(8,128)(2,1)S(1)} collective-permute-done((bf16[256,768]{1,0:T(8,128)(2,1)S(1)}, bf16[256,768]{1,0:T(8,128)(2,1)S(1)}, u32[]{:S(2)}, u32[]{:S(2)}) %collective-permute-start) | collective-permute-done | bytes 393248 | tf_op jit(solution)/shard_map/ppermute | solution.py:272
  18.7 1.6 %collective-permute-start.5 = (bf16[256,768]{1,0:T(8,128)(2,1)S(1)}, bf16[256,768]{1,0:T(8,128)(2,1)S(1)}, u32[]{:S(2)}, u32[]{:S(2)}) collective-permute-start(bf16[256,768]{1,0:T(8,128)(2,1)S(1)} %pad_maximum_fusion), channel_id=1, source_target_pairs={{0,16},{16,0},{1,17},{17,1},{2,18},{18,2},{3,19},{19,3},{4,20},{20... | collective-permute-start | bytes 1179656 | tf_op jit(solution)/shard_map/ppermute | solution.py:272
  20.6 1.5 %collective-permute-start.4 = (bf16[256,768]{1,0:T(8,128)(2,1)S(1)}, bf16[256,768]{1,0:T(8,128)(2,1)S(1)}, u32[]{:S(2)}, u32[]{:S(2)}) collective-permute-start(bf16[256,768]{1,0:T(8,128)(2,1)S(1)} %collective-permute-done.1.refs_8_), channel_id=1, source_target_pairs={{0,2},{1,3},{2,0},{3,1},{4,6},{5,7},{6,4},{7,5},{8,10},{9,11},{10,... | collective-permute-start | bytes 1179656 | tf_op jit(solution)/shard_map/ppermute | solution.py:272
  22.1 4.8 %attend.2 = (bf16[384,768]{1,0:T(8,128)(2,1)S(1)}, f32[64,768]{1,0:T(8,128)S(1)}) custom-call(bf16[768,768]{1,0:T(8,128)(2,1)S(1)} %get-tuple-element.73.q_ref, bf16[768,768]{1,0:T(8,128)(2,1)S(1)} %get-tuple-element.74.k_ref, bf16[768,768]{1,0:T(8,128)(2,1)S(1)} %get-tuple-element.75.v_ref, bf16[768,64]{1,0:T(8,128)(2,1)S(1)} %get-tuple-element.76.rows_ref, ...), custom_call_target="tpu_custom_call" | custom-call | flops 1000 | bytes 1000 | tf_op jit(solution)/shard_map/attend/pallas_call | solution.py:193
  26.9 1.6 %collective-permute-done.5.refs_7_ = bf16[256,768]{1,0:T(8,128)(2,1)S(1)} collective-permute-done((bf16[256,768]{1,0:T(8,128)(2,1)S(1)}, bf16[256,768]{1,0:T(8,128)(2,1)S(1)}, u32[]{:S(2)}, u32[]{:S(2)}) %collective-permute-start.5) | collective-permute-done | bytes 393248 | tf_op jit(solution)/shard_map/ppermute | solution.py:272
  28.5 1.3 %collective-permute-done.6.refs_4_ = bf16[256,768]{1,0:T(8,128)(2,1)S(1)} collective-permute-done((bf16[256,768]{1,0:T(8,128)(2,1)S(1)}, bf16[256,768]{1,0:T(8,128)(2,1)S(1)}, u32[]{:S(2)}, u32[]{:S(2)}) %collective-permute-start.6) | collective-permute-done | bytes 393248 | tf_op jit(solution)/shard_map/ppermute | solution.py:293
  30.6 1.5 %collective-permute-start.9 = (bf16[256,768]{1,0:T(8,128)(2,1)S(1)}, bf16[256,768]{1,0:T(8,128)(2,1)S(1)}, u32[]{:S(2)}, u32[]{:S(2)}) collective-permute-start(bf16[256,768]{1,0:T(8,128)(2,1)S(1)} %collective-permute-done.6.refs_4_), channel_id=1, source_target_pairs={{4,0},{5,1},{6,2},{7,3},{8,12},{9,13},{10,14},{11,15},{20,16},{21,... | collective-permute-start | bytes 1179656 | tf_op jit(solution)/shard_map/ppermute | solution.py:293
  32.1 1.4 %collective-permute-start.7 = (bf16[256,768]{1,0:T(8,128)(2,1)S(1)}, bf16[256,768]{1,0:T(8,128)(2,1)S(1)}, u32[]{:S(2)}, u32[]{:S(2)}) collective-permute-start(bf16[256,768]{1,0:T(8,128)(2,1)S(1)} %collective-permute-done.6.refs_4_), channel_id=1, source_target_pairs={{0,2},{1,3},{2,0},{3,1},{4,6},{5,7},{6,4},{7,5},{8,10},{9,11},{10,... | collective-permute-start | bytes 1179656 | tf_op jit(solution)/shard_map/ppermute | solution.py:272
  33.4 4.8 %attend.3 = (bf16[384,768]{1,0:T(8,128)(2,1)S(1)}, f32[64,768]{1,0:T(8,128)S(1)}) custom-call(bf16[768,768]{1,0:T(8,128)(2,1)S(1)} %get-tuple-element.73.q_ref, bf16[768,768]{1,0:T(8,128)(2,1)S(1)} %get-tuple-element.74.k_ref, bf16[768,768]{1,0:T(8,128)(2,1)S(1)} %get-tuple-element.75.v_ref, bf16[768,64]{1,0:T(8,128)(2,1)S(1)} %get-tuple-element.76.rows_ref, ...), custom_call_target="tpu_custom_call" | custom-call | flops 1000 | bytes 1000 | tf_op jit(solution)/shard_map/attend/pallas_call | solution.py:193
  38.2 3.4 %collective-permute-done.8.refs_10_.refs_5_ = bf16[256,768]{1,0:T(8,128)(2,1)S(1)} collective-permute-done((bf16[256,768]{1,0:T(8,128)(2,1)S(1)}, bf16[256,768]{1,0:T(8,128)(2,1)S(1)}, u32[]{:S(2)}, u32[]{:S(2)}) %collective-permute-start.8) | collective-permute-done | bytes 393248 | tf_op jit(solution)/shard_map/ppermute | solution.py:272
  41.6 2.1 %collective-permute-done.9 = bf16[256,768]{1,0:T(8,128)(2,1)S(1)} collective-permute-done((bf16[256,768]{1,0:T(8,128)(2,1)S(1)}, bf16[256,768]{1,0:T(8,128)(2,1)S(1)}, u32[]{:S(2)}, u32[]{:S(2)}) %collective-permute-start.9) | collective-permute-done | bytes 393248 | tf_op jit(solution)/shard_map/ppermute | solution.py:293
  44.0 1.6 %collective-permute-start.13 = (bf16[256,768]{1,0:T(8,128)(2,1)S(1)}, bf16[256,768]{1,0:T(8,128)(2,1)S(1)}, u32[]{:S(2)}, u32[]{:S(2)}) collective-permute-start(bf16[256,768]{1,0:T(8,128)(2,1)S(1)} %pad_maximum_fusion.2), channel_id=1, source_target_pairs={{0,16},{16,0},{1,17},{17,1},{2,18},{18,2},{3,19},{19,3},{4,20},{20... | collective-permute-start | bytes 1179656 | tf_op jit(solution)/shard_map/ppermute | solution.py:272
  45.5 1.3 %collective-permute-start.12 = (bf16[256,768]{1,0:T(8,128)(2,1)S(1)}, bf16[256,768]{1,0:T(8,128)(2,1)S(1)}, u32[]{:S(2)}, u32[]{:S(2)}) collective-permute-start(bf16[256,768]{1,0:T(8,128)(2,1)S(1)} %broadcast_select_fusion.refs_8_), channel_id=1, source_target_pairs={{0,2},{1,3},{2,0},{3,1},{4,6},{5,7},{6,4},{7,5},{8,10},{9,11},{10,... | collective-permute-start | bytes 1179656 | tf_op jit(solution)/shard_map/ppermute | solution.py:272
  46.8 3.8 %feed.3 = (f32[128,768]{1,0:T(8,128)S(1)}, f32[128,768]{1,0:T(8,128)S(1)}) custom-call(bf16[256,384]{1,0:T(8,128)(2,1)S(1)} %get-tuple-element.77.columns_ref, bf16[384,768]{1,0:T(8,128)(2,1)S(1)} %get-tuple-element.70.refs_0_, bf16[384,768]{1,0:T(8,128)(2,1)S(1)} %get-tuple-element.80.refs_1_, bf16[384,768]{1,0:T(8,128)(2,1)S(1)} %collective-permute-done.10.refs_2_, ...), custom_call_target="tpu_custom_call" | custom-call | flops 1000 | bytes 1000 | tf_op jit(solution)/shard_map/feed/pallas_call | solution.py:230
  50.6 4.9 %collective-permute-done.13.refs_7_ = bf16[256,768]{1,0:T(8,128)(2,1)S(1)} collective-permute-done((bf16[256,768]{1,0:T(8,128)(2,1)S(1)}, bf16[256,768]{1,0:T(8,128)(2,1)S(1)}, u32[]{:S(2)}, u32[]{:S(2)}) %collective-permute-start.13) | collective-permute-done | bytes 393248 | tf_op jit(solution)/shard_map/ppermute | solution.py:272
  57.4 3.7 %feed.4 = (f32[128,768]{1,0:T(8,128)S(1)}, f32[128,768]{1,0:T(8,128)S(1)}) custom-call(bf16[256,384]{1,0:T(8,128)(2,1)S(1)} %get-tuple-element.77.columns_ref, bf16[384,768]{1,0:T(8,128)(2,1)S(1)} %get-tuple-element.70.refs_0_, bf16[384,768]{1,0:T(8,128)(2,1)S(1)} %get-tuple-element.80.refs_1_, bf16[384,768]{1,0:T(8,128)(2,1)S(1)} %collective-permute-done.10.refs_2_, ...), custom_call_target="tpu_custom_call" | custom-call | flops 1000 | bytes 1000 | tf_op jit(solution)/shard_map/feed/pallas_call | solution.py:230
  61.1 1.9 %collective-permute-done.14.refs_4_ = bf16[128,768]{1,0:T(8,128)(2,1)S(1)} collective-permute-done((bf16[128,768]{1,0:T(8,128)(2,1)S(1)}, bf16[128,768]{1,0:T(8,128)(2,1)S(1)}, u32[]{:S(2)}, u32[]{:S(2)}) %collective-permute-start.14) | collective-permute-done | bytes 196640 | tf_op jit(solution)/shard_map/ppermute | solution.py:272
  63.0 2.2 %feed.5 = (f32[128,768]{1,0:T(8,128)S(1)}, f32[128,768]{1,0:T(8,128)S(1)}) custom-call(bf16[256,384]{1,0:T(8,128)(2,1)S(1)} %get-tuple-element.77.columns_ref, bf16[384,768]{1,0:T(8,128)(2,1)S(1)} %get-tuple-element.70.refs_0_, bf16[384,768]{1,0:T(8,128)(2,1)S(1)} %get-tuple-element.80.refs_1_, bf16[384,768]{1,0:T(8,128)(2,1)S(1)} %collective-permute-done.10.refs_2_, ...), custom_call_target="tpu_custom_call" | custom-call | flops 1000 | bytes 1000 | tf_op jit(solution)/shard_map/feed/pallas_call | solution.py:230
  65.3 1.7 %collective-permute-done.15.other_ref = f32[128,768]{1,0:T(8,128)S(1)} collective-permute-done((f32[128,768]{1,0:T(8,128)S(1)}, f32[128,768]{1,0:T(8,128)S(1)}, u32[]{:S(2)}, u32[]{:S(2)}) %collective-permute-start.15) | collective-permute-done | bytes 393248 | tf_op jit(solution)/shard_map/ppermute | solution.py:272
  67.8 18.2 %all_to_all.10 = bf16[16,16,896]{2,1,0:T(8,128)(2,1)S(1)} all-to-all(bf16[16,16,896]{2,1,0:T(8,128)(2,1)S(1)} %bitcast.11), channel_id=1, replica_groups=mesh['groups'=2,'wide'=16] {'wide'}, dimensions={0} | all-to-all | bytes 917504 | tf_op jit(solution)/shard_map/all_to_all | solution.py:389
  87.4 11.6 %all_to_all.11 = bf16[16,16,256]{2,1,0:T(8,128)(2,1)S(1)} all-to-all(bf16[16,16,256]{2,1,0:T(8,128)(2,1)S(1)} %bitcast.10), channel_id=1, replica_groups=mesh['groups'=2,'wide'=16] {'wide'}, dimensions={0} | all-to-all | bytes 262144 | tf_op jit(solution)/shard_map/all_to_all | solution.py:397
  (51 shorter events, 9.6 us)
Async XLA Ops:
  1.7 15.1 %collective-permute-start.2 = (bf16[256,768]{1,0:T(8,128)(2,1)S(1)}, bf16[256,768]{1,0:T(8,128)(2,1)S(1)}, u32[]{:S(2)}, u32[]{:S(2)}) collective-permute-start(bf16[256,768]{1,0:T(8,128)(2,1)S(1)} %hold.1), channel_id=1, source_target_pairs={{4,8},{5,9},{6,10},{7,11},{8,4},{9,5},{10,6},{11,7},{20,24},{21,25... | collective-permute-start | bytes 1179656 | tf_op jit(solution)/shard_map/ppermute | solution.py:293
  2.4 14.7 %collective-permute-start.1 = (bf16[256,768]{1,0:T(8,128)(2,1)S(1)}, bf16[256,768]{1,0:T(8,128)(2,1)S(1)}, u32[]{:S(2)}, u32[]{:S(2)}) collective-permute-start(bf16[256,768]{1,0:T(8,128)(2,1)S(1)} %hold.1), channel_id=1, source_target_pairs={{0,4},{1,5},{2,6},{3,7},{4,0},{5,1},{6,2},{7,3},{8,12},{9,13},{10,... | collective-permute-start | bytes 1179656 | tf_op jit(solution)/shard_map/ppermute | solution.py:272
  8.3 10.3 %collective-permute-start = (bf16[256,768]{1,0:T(8,128)(2,1)S(1)}, bf16[256,768]{1,0:T(8,128)(2,1)S(1)}, u32[]{:S(2)}, u32[]{:S(2)}) collective-permute-start(bf16[256,768]{1,0:T(8,128)(2,1)S(1)} %hold.1), channel_id=1, source_target_pairs={{0,2},{1,3},{2,0},{3,1},{4,6},{5,7},{6,4},{7,5},{8,10},{9,11},{10,... | collective-permute-start | bytes 1179656 | tf_op jit(solution)/shard_map/ppermute | solution.py:272
  9.8 1.4 %collective-permute-start.3 = (s32[2,64]{1,0:T(2,128)}, s32[2,64]{1,0:T(2,128)S(1)}, u32[]{:S(2)}, u32[]{:S(2)}) collective-permute-start(s32[2,64]{1,0:T(2,128)} %lengths_hbm.1), channel_id=1, source_target_pairs={{0,1},{1,0},{2,3},{3,2},{4,5},{5,4},{6,7},{7,6},{8,9},{9,8},{10,11... | collective-permute-start | bytes 1544 | tf_op jit(solution)/shard_map/ppermute | solution.py:272
  18.6 3.5 %copy-start.5 = (f32[768]{0:T(1024)S(1)}, f32[768]{0:T(1024)}, u32[]{:S(2)}) copy-start(f32[768]{0:T(1024)} %gain_ref.4) | copy-start | bytes 9220
  18.6 3.5 %copy-start = (bf16[2,384,768]{2,1,0:T(8,128)(2,1)S(1)}, bf16[2,384,768]{2,1,0:T(8,128)(2,1)}, u32[]{:S(2)}) copy-start(bf16[2,384,768]{2,1,0:T(8,128)(2,1)} %x_ref.3) | copy-start | bytes 3538948
  18.6 3.5 %copy-start.1 = (bf16[768,768]{1,0:T(8,128)(2,1)S(1)}, bf16[768,768]{1,0:T(8,128)(2,1)}, u32[]{:S(2)}) copy-start(bf16[768,768]{1,0:T(8,128)(2,1)} %wo_ref.3) | copy-start | bytes 3538948
  18.7 9.8 %collective-permute-start.5 = (bf16[256,768]{1,0:T(8,128)(2,1)S(1)}, bf16[256,768]{1,0:T(8,128)(2,1)S(1)}, u32[]{:S(2)}, u32[]{:S(2)}) collective-permute-start(bf16[256,768]{1,0:T(8,128)(2,1)S(1)} %pad_maximum_fusion), channel_id=1, source_target_pairs={{0,16},{16,0},{1,17},{17,1},{2,18},{18,2},{3,19},{19,3},{4,20},{20... | collective-permute-start | bytes 1179656 | tf_op jit(solution)/shard_map/ppermute | solution.py:272
  20.3 9.5 %collective-permute-start.6 = (bf16[256,768]{1,0:T(8,128)(2,1)S(1)}, bf16[256,768]{1,0:T(8,128)(2,1)S(1)}, u32[]{:S(2)}, u32[]{:S(2)}) collective-permute-start(bf16[256,768]{1,0:T(8,128)(2,1)S(1)} %broadcast_select_fusion.1), channel_id=1, source_target_pairs={{4,0},{5,1},{6,2},{7,3},{0,8},{1,9},{2,10},{3,11},{8,12},{9,13},{1... | collective-permute-start | bytes 1179656 | tf_op jit(solution)/shard_map/ppermute | solution.py:293
  20.6 9.3 %collective-permute-start.4 = (bf16[256,768]{1,0:T(8,128)(2,1)S(1)}, bf16[256,768]{1,0:T(8,128)(2,1)S(1)}, u32[]{:S(2)}, u32[]{:S(2)}) collective-permute-start(bf16[256,768]{1,0:T(8,128)(2,1)S(1)} %collective-permute-done.1.refs_8_), channel_id=1, source_target_pairs={{0,2},{1,3},{2,0},{3,1},{4,6},{5,7},{6,4},{7,5},{8,10},{9,11},{10,... | collective-permute-start | bytes 1179656 | tf_op jit(solution)/shard_map/ppermute | solution.py:272
  29.9 13.8 %collective-permute-start.10 = (bf16[384,768]{1,0:T(8,128)(2,1)S(1)}, bf16[384,768]{1,0:T(8,128)(2,1)S(1)}, u32[]{:S(2)}, u32[]{:S(2)}) collective-permute-start(bf16[384,768]{1,0:T(8,128)(2,1)S(1)} %get-tuple-element.70.refs_0_), channel_id=1, source_target_pairs={{0,1},{1,0},{2,3},{3,2},{4,5},{5,4},{6,7},{7,6},{8,9},{9,8},{10,11... | collective-permute-start | bytes 1769480 | tf_op jit(solution)/shard_map/ppermute | solution.py:272
  30.0 11.6 %collective-permute-start.8 = (bf16[256,768]{1,0:T(8,128)(2,1)S(1)}, bf16[256,768]{1,0:T(8,128)(2,1)S(1)}, u32[]{:S(2)}, u32[]{:S(2)}) collective-permute-start(bf16[256,768]{1,0:T(8,128)(2,1)S(1)} %pad_maximum_fusion.1), channel_id=1, source_target_pairs={{0,16},{16,0},{1,17},{17,1},{2,18},{18,2},{3,19},{19,3},{4,20},{20... | collective-permute-start | bytes 1179656 | tf_op jit(solution)/shard_map/ppermute | solution.py:272
  30.6 13.1 %collective-permute-start.9 = (bf16[256,768]{1,0:T(8,128)(2,1)S(1)}, bf16[256,768]{1,0:T(8,128)(2,1)S(1)}, u32[]{:S(2)}, u32[]{:S(2)}) collective-permute-start(bf16[256,768]{1,0:T(8,128)(2,1)S(1)} %collective-permute-done.6.refs_4_), channel_id=1, source_target_pairs={{4,0},{5,1},{6,2},{7,3},{8,12},{9,13},{10,14},{11,15},{20,16},{21,... | collective-permute-start | bytes 1179656 | tf_op jit(solution)/shard_map/ppermute | solution.py:293
  32.1 11.7 %collective-permute-start.7 = (bf16[256,768]{1,0:T(8,128)(2,1)S(1)}, bf16[256,768]{1,0:T(8,128)(2,1)S(1)}, u32[]{:S(2)}, u32[]{:S(2)}) collective-permute-start(bf16[256,768]{1,0:T(8,128)(2,1)S(1)} %collective-permute-done.6.refs_4_), channel_id=1, source_target_pairs={{0,2},{1,3},{2,0},{3,1},{4,6},{5,7},{6,4},{7,5},{8,10},{9,11},{10,... | collective-permute-start | bytes 1179656 | tf_op jit(solution)/shard_map/ppermute | solution.py:272
  43.7 3.1 %copy-start.3 = (bf16[192,768]{1,0:T(8,128)(2,1)S(1)}, bf16[192,768]{1,0:T(8,128)(2,1)}, u32[]{:S(2)}) copy-start(bf16[192,768]{1,0:T(8,128)(2,1)} %refs_4_.1) | copy-start | bytes 884740
  43.7 3.1 %collective-permute-start.11 = (bf16[384,768]{1,0:T(8,128)(2,1)S(1)}, bf16[384,768]{1,0:T(8,128)(2,1)S(1)}, u32[]{:S(2)}, u32[]{:S(2)}) collective-permute-start(bf16[384,768]{1,0:T(8,128)(2,1)S(1)} %get-tuple-element.80.refs_1_), channel_id=1, source_target_pairs={{0,1},{1,0},{2,3},{3,2},{4,5},{5,4},{6,7},{7,6},{8,9},{9,8},{10,11... | collective-permute-start | bytes 1769480 | tf_op jit(solution)/shard_map/ppermute | solution.py:272
  44.0 11.6 %collective-permute-start.13 = (bf16[256,768]{1,0:T(8,128)(2,1)S(1)}, bf16[256,768]{1,0:T(8,128)(2,1)S(1)}, u32[]{:S(2)}, u32[]{:S(2)}) collective-permute-start(bf16[256,768]{1,0:T(8,128)(2,1)S(1)} %pad_maximum_fusion.2), channel_id=1, source_target_pairs={{0,16},{16,0},{1,17},{17,1},{2,18},{18,2},{3,19},{19,3},{4,20},{20... | collective-permute-start | bytes 1179656 | tf_op jit(solution)/shard_map/ppermute | solution.py:272
  45.5 11.2 %collective-permute-start.12 = (bf16[256,768]{1,0:T(8,128)(2,1)S(1)}, bf16[256,768]{1,0:T(8,128)(2,1)S(1)}, u32[]{:S(2)}, u32[]{:S(2)}) collective-permute-start(bf16[256,768]{1,0:T(8,128)(2,1)S(1)} %broadcast_select_fusion.refs_8_), channel_id=1, source_target_pairs={{0,2},{1,3},{2,0},{3,1},{4,6},{5,7},{6,4},{7,5},{8,10},{9,11},{10,... | collective-permute-start | bytes 1179656 | tf_op jit(solution)/shard_map/ppermute | solution.py:272
  56.8 6.3 %collective-permute-start.14 = (bf16[128,768]{1,0:T(8,128)(2,1)S(1)}, bf16[128,768]{1,0:T(8,128)(2,1)S(1)}, u32[]{:S(2)}, u32[]{:S(2)}) collective-permute-start(bf16[128,768]{1,0:T(8,128)(2,1)S(1)} %slice.27), channel_id=1, source_target_pairs={{0,16},{16,0},{1,17},{17,1},{2,18},{18,2},{3,19},{19,3},{4,20},{20... | collective-permute-start | bytes 589832 | tf_op jit(solution)/shard_map/ppermute | solution.py:272
  63.0 4.0 %copy-start.7 = (f32[768]{0:T(1024)S(1)}, f32[768]{0:T(1024)}, u32[]{:S(2)}) copy-start(f32[768]{0:T(1024)} %gain_ref.5) | copy-start | bytes 9220
  63.0 4.0 %copy-start.8 = (s32[128]{0:T(128)S(1)}, s32[128]{0:T(128)}, u32[]{:S(2)}) copy-start(s32[128]{0:T(128)} %param.27) | copy-start | bytes 1540
  63.0 23.0 %copy-start.2 = (bf16[8,256,768]{2,1,0:T(8,128)(2,1)S(1)}, bf16[8,256,768]{2,1,0:T(8,128)(2,1)}, u32[]{:S(2)}) copy-start(bf16[8,256,768]{2,1,0:T(8,128)(2,1)} %books_ref.1) | copy-start | bytes 9437188
  65.2 20.8 %copy-start.6 = (bf16[8,768]{1,0:T(8,128)(2,1)S(1)}, bf16[8,768]{1,0:T(8,128)(2,1)}, u32[]{:S(2)}) copy-start(bf16[8,768]{1,0:T(8,128)(2,1)} %coarse_ref.1) | copy-start | bytes 36868
  65.2 1.8 %collective-permute-start.15 = (f32[128,768]{1,0:T(8,128)S(1)}, f32[128,768]{1,0:T(8,128)S(1)}, u32[]{:S(2)}, u32[]{:S(2)}) collective-permute-start(f32[128,768]{1,0:T(8,128)S(1)} %get-tuple-element.100), channel_id=1, source_target_pairs={{0,1},{1,0},{2,3},{3,2},{4,5},{5,4},{6,7},{7,6},{8,9},{9,8},{10,11... | collective-permute-start | bytes 1179656 | tf_op jit(solution)/shard_map/ppermute | solution.py:272
  (1 other events, 3.1 us)

commit v3 on v2

--- a/solution.py
+++ b/solution.py
@@ -89,7 +89,7 @@
     earlier = dot(target.astype(BF16), jnp.where(before, 1.0, 0.0).astype(BF16))
     rank = jnp.sum(earlier * target, axis=0, keepdims=True)
     slot_ref[...] = owner * capacity + rank.astype(jnp.int32)
-    gain = gain_ref[...]
+    gain = gain_ref[...][None]
     copies[3].wait()
     normed = [rms(x_ref[pack].astype(F32), gain).astype(BF16) for pack in range(packs)]
     normed = jnp.concatenate(normed, axis=0)
@@ -203,6 +203,30 @@
     )(*projected[:5], x, wo, gain2)
 
 
+def feed_side_kernel(side, n_held, pieces, columns_ref, *refs):
+    normed_refs, held, (base_ref, out_ref) = refs[: -2 - n_held], refs[-2 - n_held : -2], refs[-2:]
+    w_in = jnp.concatenate([held[i][r] for i, r, _, _ in pieces], axis=0)
+    w_down = jnp.concatenate([held[i][r] for _, _, i, r in pieces], axis=0)
+    packs = len(normed_refs)
+    items = columns_ref.shape[0] // (2 * packs)
+    pooled = []
+    for pack in range(packs):
+        hidden = jnp.maximum(dot_nt(normed_refs[pack][...], w_in), 0.0).astype(BF16)
+        at = (side * packs + pack) * items
+        pooled.append(dot(columns_ref[at : at + items], hidden).astype(BF16))
+    out_ref[...] = base_ref[...] + dot(jnp.concatenate(pooled, axis=0), w_down)
+
+
+def feed_side(side, columns, normed, held, pieces, base):
+    return pl.pallas_call(
+        functools.partial(feed_side_kernel, side, len(held), pieces),
+        out_shape=jax.ShapeDtypeStruct(base.shape, F32),
+        compiler_params=params(),
+        cost_estimate=cost(),
+        name="feed_side",
+    )(columns, *normed[side], *held, base)
+
+
 def feed_kernel(n_normed, n_held, pieces, n_base, columns_ref, *refs):
     normed_refs, refs = (refs[:n_normed], refs[n_normed : 2 * n_normed]), refs[2 * n_normed :]
     held, refs = refs[:n_held], refs[n_held:]
@@ -320,24 +344,27 @@
 
     side2, outer = side(far2), along(far2, [(1, 0), (2, 3)])
     x1 = twin(cat(side1[split:], far2[split:]))
+    last_inner = along(x0[:both], [(1, 2), (2, 1)])
     other_first = sibling(first[0])
     second = encode(1, projected, tokens)
-    side2, x1, outer, second, other_first = after((side2, x1, outer, second, other_first))
+    side2, x1, outer, last_inner, second, other_first = after((side2, x1, outer, last_inner, second, other_first))
 
     far3 = jnp.where(inner, middle, outer)
     side3, x2 = side(far3), twin(cat(side2[split:], far3[split:]))
+    last_outer = along(x1[:both], [(2, 0), (1, 3)])
     normed = ((first[0], second[0]), (other_first, sibling(second[0])))
     own = [(0, slice(0, rows), 1, slice(0, rows))]
     pieces = own + blocks(2) + rest(3) + blocks(4) + rest(3, both) + blocks(5) + rest(6)
     acc = feed(columns, normed, [w_input, w_down, side0, x0, near1, side1, x1], pieces, ([first[1], second[1]], []))
-    side3, x2, acc = after((side3, x2, acc))
-
-    x3 = twin(side3[split:])
-    pieces = blocks(0) + rest(1, both) + blocks(2) + rest(3) + blocks(4) + rest(3, both) + blocks(5)
-    acc = feed(columns, normed, [far2, x1, side2, x2, far3, side3], pieces, ([acc[0]], [acc[1]]))
-    x3, acc = after((x3, acc))
-    acc = feed(columns, normed, [x3], rest(0), ([acc[0]], [acc[1]]))
-    return acc, projected[5]
+    pieces = blocks(0) + rest(1, both) + blocks(2) + blocks(3)
+    acc = feed(columns, normed, [far2, x1, side2, far3], pieces, ([acc[0]], [acc[1]]))
+    side3, x2, last_outer, acc = after((side3, x2, last_outer, acc))
+
+    last = jnp.where(inner, last_inner, last_outer)
+    pieces = rest(0) + rest(0, both) + blocks(1) + rest(2)
+    held = [x2, side3, last]
+    there = sibling(feed_side(1, columns, normed, held, pieces, acc[1]))
+    return feed_side(0, columns, normed, held, pieces, acc[0]), there, projected[5]
 
 
 def local(
@@ -357,7 +384,7 @@
 
     def encode_first(tokens):
         return project(
-            item_lengths, other_lengths, owner.reshape(1, items_dev), tokens, norm_attn[None],
+            item_lengths, other_lengths, owner.reshape(1, items_dev), tokens, norm_attn,
             w_query, w_key, w_value, wide_count, capacity,
         )
 
@@ -365,7 +392,7 @@
         return attend(pack, projected, tokens, w_output, norm_ffn)
 
     if wide_count == 16 and packs == 2:
-        acc, slots_of = overlapped(w_input, w_down, tokens, encode_first, encode, sibling)
+        acc, other, slots_of = overlapped(w_input, w_down, tokens, encode_first, encode, sibling)
     else:
         projected = encode_first(tokens)
         slots_of = projected[5]
@@ -374,7 +401,7 @@
         every = slice(0, held[0].shape[0])
         normed = (normed, [sibling(n) for n in normed])
         acc = feed(projected[4], normed, held, [(0, every, 1, every)], (pooled, []))
-    other = sibling(acc[1])
+        acc, other = acc[0], sibling(acc[1])
 
     item_embed, send = pl.pallas_call(
         place_kernel,
@@ -384,7 +411,7 @@
         ),
         compiler_params=params(),
         name="place",
-    )(acc[0], other, norm_final, slots_of, cluster_slot[None])
+    )(acc, other, norm_final, slots_of, cluster_slot[None])
     send = send.reshape(wide_count, capacity, width + 128)
     rows = lax.all_to_all(send, "wide", split_axis=0, concat_axis=0, tiled=True)
     codes = pl.pallas_call(

time: 100 us -> 93.9 us (0.939)
  waiting for transfers between devices: 20.1 us -> 14.3 us
  starting transfers between devices: 18.5 us -> 20.9 us
  local copies, waits for them, and re-layouts: 1.41 us -> 0.16 us
  blocking collectives: 29.8 us -> 28.7 us
    ppermute x3 -> x5, starting transfers between devices: 2.44 us -> 9.91 us  [along(): return lax.ppermute(value, 'wide', pairs)]
    ppermute x13 -> x12, waiting for transfers between devices: 16.7 us -> 10.3 us  [flip(): return lambda value: lax.ppermute(value, axis_name, pairs)]
    ppermute x13 -> x12, starting transfers between devices: 16.1 us -> 11 us  [flip(): return lambda value: lax.ppermute(value, axis_name, pairs)]
    pallas_call x3 -> x2, Pallas kernels: 9.68 us -> 6.31 us  [feed(): pl.pallas_call(functools.partial(feed_kernel, len(normed[0]), len(held),...]
    pallas_call x0 -> x2, Pallas kernels: none -> 2.78 us  [feed_side(): pl.pallas_call(functools.partial(feed_side_kernel, side, len(held), piece...]
    broadcast_in_dim x1 -> x0, local copies, waits for them, and re-layouts: 1.27 us -> none  [encode_first(): norm_attn[None]]
    all_to_all x1, blocking collectives: 18.2 us -> 17 us  [local(): rows = lax.all_to_all(send, 'wide', split_axis=0, concat_axis=0, tiled=True)]
    ppermute x3 -> x5, waiting for transfers between devices: 3.45 us -> 4.03 us  [along(): return lax.ppermute(value, 'wide', pairs)]
  transfers between devices with their start and end apart: 16 -> 17, of which waited for: 12 -> 10; matrix products, arithmetic and copies ran while one was open for 1% -> 0% of each run, Pallas kernels for 23% -> 24%
where the time goes in v3:
time: 93.9 us; the launch traced here: 93.6 us
  blocking collectives  28.7 us (31%)
  Pallas kernels  27.5 us (29%)
  starting transfers between devices  20.9 us (22%)
  waiting for transfers between devices  14.3 us (15%)
  between operations  0.96 us (1%)
    all_to_all x1, blocking collectives, local(): rows = lax.all_to_all(send, 'wide', split_axis=0, concat_axis=0, tiled=True)  17 us
    all_to_all x1, blocking collectives, local(): lax.all_to_all(codes, 'wide', split_axis=0, concat_axis=0, tiled=True)  11.6 us
    ppermute x12, starting transfers between devices, flip(): return lambda value: lax.ppermute(value, axis_name, pairs)  11 us
    ppermute x12, waiting for transfers between devices, flip(): return lambda value: lax.ppermute(value, axis_name, pairs)  10.3 us
    ppermute x5, starting transfers between devices, along(): return lax.ppermute(value, 'wide', pairs)  9.91 us
    pallas_call x2, Pallas kernels, attend(): pl.pallas_call(functools.partial(attend_kernel, pack), out_shape=(jax.Sha...  9.51 us
    pallas_call x2, Pallas kernels, feed(): pl.pallas_call(functools.partial(feed_kernel, len(normed[0]), len(held),...  6.31 us
    pallas_call x1, Pallas kernels, project(): pl.pallas_call(functools.partial(project_kernel, wide=wide, capacity=capa...  5.68 us
  transfers between devices with their start and end apart: 17, of which 10 were waited for; matrix products, arithmetic and copies ran while one was open for 0% of the time, Pallas kernels for 24%

profile of v3, /device:TPU:0, one launch (start us, length us, event | category | flops | bytes accessed | tf_op | source)
XLA Modules:
  0.0 93.6 jit_solution(18030365273558840180)
XLA Ops:
  1.7 3.0 %collective-permute-start = (bf16[256,768]{1,0:T(8,128)(2,1)S(1)}, bf16[256,768]{1,0:T(8,128)(2,1)S(1)}, u32[]{:S(2)}, u32[]{:S(2)}) collective-permute-start(bf16[256,768]{1,0:T(8,128)(2,1)S(1)} %hold.1), channel_id=1, source_target_pairs={{0,2},{1,3},{2,0},{3,1},{4,6},{5,7},{6,4},{7,5},{8,10},{9,11},{10,... | collective-permute-start | bytes 1179656 | tf_op jit(solution)/shard_map/ppermute | solution.py:296
  4.7 1.6 %collective-permute-start.1 = (bf16[256,768]{1,0:T(8,128)(2,1)S(1)}, bf16[256,768]{1,0:T(8,128)(2,1)S(1)}, u32[]{:S(2)}, u32[]{:S(2)}) collective-permute-start(bf16[256,768]{1,0:T(8,128)(2,1)S(1)} %hold.1), channel_id=1, source_target_pairs={{0,4},{1,5},{2,6},{3,7},{4,0},{5,1},{6,2},{7,3},{8,12},{9,13},{10,... | collective-permute-start | bytes 1179656 | tf_op jit(solution)/shard_map/ppermute | solution.py:296
  7.1 1.3 %collective-permute-done.3.other_ref = s32[2,64]{1,0:T(2,128)S(1)} collective-permute-done((s32[2,64]{1,0:T(2,128)}, s32[2,64]{1,0:T(2,128)S(1)}, u32[]{:S(2)}, u32[]{:S(2)}) %collective-permute-start.3) | collective-permute-done | bytes 544 | tf_op jit(solution)/shard_map/ppermute | solution.py:296
  8.4 5.7 %project.1 = (bf16[768,768]{1,0:T(8,128)(2,1)S(1)}, bf16[768,768]{1,0:T(8,128)(2,1)S(1)}, bf16[768,768]{1,0:T(8,128)(2,1)S(1)}, bf16[768,64]{1,0:T(8,128)(2,1)S(...) custom-call(s32[2,64]{1,0:T(2,128)S(1)} %collective-permute-done.3.other_ref, s32[2,64]{1,0:T(2,128)} %lengths_hbm.1, ...), custom_call_target="tpu_custom_call" | custom-call | flops 1000 | bytes 1000 | tf_op jit(solution)/shard_map/project/pallas_call | solution.py:105
  15.4 5.8 %collective-permute-start.6 = (bf16[256,768]{1,0:T(8,128)(2,1)S(1)}, bf16[256,768]{1,0:T(8,128)(2,1)S(1)}, u32[]{:S(2)}, u32[]{:S(2)}) collective-permute-start(bf16[256,768]{1,0:T(8,128)(2,1)S(1)} %broadcast_select_fusion.1), channel_id=1, source_target_pairs={{4,0},{5,1},{6,2},{7,3},{0,8},{1,9},{2,10},{3,11},{8,12},{9,13},{1... | collective-permute-start | bytes 1179656 | tf_op jit(solution)/shard_map/ppermute | solution.py:317
  21.3 1.6 %collective-permute-start.5 = (bf16[256,768]{1,0:T(8,128)(2,1)S(1)}, bf16[256,768]{1,0:T(8,128)(2,1)S(1)}, u32[]{:S(2)}, u32[]{:S(2)}) collective-permute-start(bf16[256,768]{1,0:T(8,128)(2,1)S(1)} %pad_maximum_fusion), channel_id=1, source_target_pairs={{0,16},{16,0},{1,17},{17,1},{2,18},{18,2},{3,19},{19,3},{4,20},{20... | collective-permute-start | bytes 1179656 | tf_op jit(solution)/shard_map/ppermute | solution.py:296
  23.3 4.8 %attend.2 = (bf16[384,768]{1,0:T(8,128)(2,1)S(1)}, f32[64,768]{1,0:T(8,128)S(1)}) custom-call(bf16[768,768]{1,0:T(8,128)(2,1)S(1)} %get-tuple-element.71.q_ref, bf16[768,768]{1,0:T(8,128)(2,1)S(1)} %get-tuple-element.72.k_ref, bf16[768,768]{1,0:T(8,128)(2,1)S(1)} %get-tuple-element.73.v_ref, bf16[768,64]{1,0:T(8,128)(2,1)S(1)} %get-tuple-element.74.rows_ref, ...), custom_call_target="tpu_custom_call" | custom-call | flops 1000 | bytes 1000 | tf_op jit(solution)/shard_map/attend/pallas_call | solution.py:193
  28.1 2.3 %collective-permute-done.5.refs_7_ = bf16[256,768]{1,0:T(8,128)(2,1)S(1)} collective-permute-done((bf16[256,768]{1,0:T(8,128)(2,1)S(1)}, bf16[256,768]{1,0:T(8,128)(2,1)S(1)}, u32[]{:S(2)}, u32[]{:S(2)}) %collective-permute-start.5) | collective-permute-done | bytes 393248 | tf_op jit(solution)/shard_map/ppermute | solution.py:296
  30.4 1.2 %collective-permute-done.4.refs_9_ = bf16[256,768]{1,0:T(8,128)(2,1)S(1)} collective-permute-done((bf16[256,768]{1,0:T(8,128)(2,1)S(1)}, bf16[256,768]{1,0:T(8,128)(2,1)S(1)}, u32[]{:S(2)}, u32[]{:S(2)}) %collective-permute-start.4) | collective-permute-done | bytes 393248 | tf_op jit(solution)/shard_map/ppermute | solution.py:296
  32.8 1.3 %collective-permute-start.9 = (bf16[256,768]{1,0:T(8,128)(2,1)S(1)}, bf16[256,768]{1,0:T(8,128)(2,1)S(1)}, u32[]{:S(2)}, u32[]{:S(2)}) collective-permute-start(bf16[256,768]{1,0:T(8,128)(2,1)S(1)} %collective-permute-done.6.refs_4_), channel_id=1, source_target_pairs={{4,0},{5,1},{6,2},{7,3},{8,12},{9,13},{10,14},{11,15},{20,16},{21,... | collective-permute-start | bytes 1179656 | tf_op jit(solution)/shard_map/ppermute | solution.py:317
  35.0 4.8 %attend.3 = (bf16[384,768]{1,0:T(8,128)(2,1)S(1)}, f32[64,768]{1,0:T(8,128)S(1)}) custom-call(bf16[768,768]{1,0:T(8,128)(2,1)S(1)} %get-tuple-element.71.q_ref, bf16[768,768]{1,0:T(8,128)(2,1)S(1)} %get-tuple-element.72.k_ref, bf16[768,768]{1,0:T(8,128)(2,1)S(1)} %get-tuple-element.73.v_ref, bf16[768,64]{1,0:T(8,128)(2,1)S(1)} %get-tuple-element.74.rows_ref, ...), custom_call_target="tpu_custom_call" | custom-call | flops 1000 | bytes 1000 | tf_op jit(solution)/shard_map/attend/pallas_call | solution.py:193
  39.8 3.5 %collective-permute-done.8.refs_10_.refs_5_ = bf16[256,768]{1,0:T(8,128)(2,1)S(1)} collective-permute-done((bf16[256,768]{1,0:T(8,128)(2,1)S(1)}, bf16[256,768]{1,0:T(8,128)(2,1)S(1)}, u32[]{:S(2)}, u32[]{:S(2)}) %collective-permute-start.8) | collective-permute-done | bytes 393248 | tf_op jit(solution)/shard_map/ppermute | solution.py:296
  43.6 2.1 %collective-permute-done.9 = bf16[256,768]{1,0:T(8,128)(2,1)S(1)} collective-permute-done((bf16[256,768]{1,0:T(8,128)(2,1)S(1)}, bf16[256,768]{1,0:T(8,128)(2,1)S(1)}, u32[]{:S(2)}, u32[]{:S(2)}) %collective-permute-start.9) | collective-permute-done | bytes 393248 | tf_op jit(solution)/shard_map/ppermute | solution.py:317
  45.8 1.6 %collective-permute-start.13 = (bf16[256,768]{1,0:T(8,128)(2,1)S(1)}, bf16[256,768]{1,0:T(8,128)(2,1)S(1)}, u32[]{:S(2)}, u32[]{:S(2)}) collective-permute-start(bf16[256,768]{1,0:T(8,128)(2,1)S(1)} %pad_maximum_fusion.2), channel_id=1, source_target_pairs={{0,16},{16,0},{1,17},{17,1},{2,18},{18,2},{3,19},{19,3},{4,20},{20... | collective-permute-start | bytes 1179656 | tf_op jit(solution)/shard_map/ppermute | solution.py:296
  47.4 1.5 %collective-permute-start.12 = (bf16[256,768]{1,0:T(8,128)(2,1)S(1)}, bf16[256,768]{1,0:T(8,128)(2,1)S(1)}, u32[]{:S(2)}, u32[]{:S(2)}) collective-permute-start(bf16[256,768]{1,0:T(8,128)(2,1)S(1)} %broadcast_select_fusion.refs_7_), channel_id=1, source_target_pairs={{0,2},{1,3},{2,0},{3,1},{4,6},{5,7},{6,4},{7,5},{8,10},{9,11},{10,... | collective-permute-start | bytes 1179656 | tf_op jit(solution)/shard_map/ppermute | solution.py:296
  48.9 1.3 %collective-permute-start.14 = (bf16[128,768]{1,0:T(8,128)(2,1)S(1)}, bf16[128,768]{1,0:T(8,128)(2,1)S(1)}, u32[]{:S(2)}, u32[]{:S(2)}) collective-permute-start(bf16[128,768]{1,0:T(8,128)(2,1)S(1)} %slice.31), channel_id=1, source_target_pairs={{8,0},{9,1},{10,2},{11,3},{4,12},{5,13},{6,14},{7,15},{24,16},{25,... | collective-permute-start | bytes 589832 | tf_op jit(solution)/shard_map/ppermute | solution.py:317
  50.3 3.8 %feed.2 = (f32[128,768]{1,0:T(8,128)S(1)}, f32[128,768]{1,0:T(8,128)S(1)}) custom-call(bf16[256,384]{1,0:T(8,128)(2,1)S(1)} %get-tuple-element.75.columns_ref, bf16[384,768]{1,0:T(8,128)(2,1)S(1)} %get-tuple-element.67.refs_0_, bf16[384,768]{1,0:T(8,128)(2,1)S(1)} %get-tuple-element.78.refs_1_, bf16[384,768]{1,0:T(8,128)(2,1)S(1)} %collective-permute-done.11.refs_2_.refs_0_, ...), custom_call_target="tpu_custom_call" | custom-call | flops 1000 | bytes 1000 | tf_op jit(solution)/shard_map/feed/pallas_call | solution.py:254
  54.0 2.5 %feed.3 = (f32[128,768]{1,0:T(8,128)S(1)}, f32[128,768]{1,0:T(8,128)S(1)}) custom-call(bf16[256,384]{1,0:T(8,128)(2,1)S(1)} %get-tuple-element.75.columns_ref, bf16[384,768]{1,0:T(8,128)(2,1)S(1)} %get-tuple-element.67.refs_0_, bf16[384,768]{1,0:T(8,128)(2,1)S(1)} %get-tuple-element.78.refs_1_, bf16[384,768]{1,0:T(8,128)(2,1)S(1)} %collective-permute-done.11.refs_2_.refs_0_, ...), custom_call_target="tpu_custom_call" | custom-call | flops 1000 | bytes 1000 | tf_op jit(solution)/shard_map/feed/pallas_call | solution.py:254
  56.6 1.9 %collective-permute-done.14 = bf16[128,768]{1,0:T(8,128)(2,1)S(1)} collective-permute-done((bf16[128,768]{1,0:T(8,128)(2,1)S(1)}, bf16[128,768]{1,0:T(8,128)(2,1)S(1)}, u32[]{:S(2)}, u32[]{:S(2)}) %collective-permute-start.14) | collective-permute-done | bytes 196640 | tf_op jit(solution)/shard_map/ppermute | solution.py:317
  58.7 1.4 %feed_side.3 = f32[128,768]{1,0:T(8,128)S(1)} custom-call(bf16[256,384]{1,0:T(8,128)(2,1)S(1)} %get-tuple-element.75.columns_ref, bf16[384,768]{1,0:T(8,128)(2,1)S(1)} %collective-permute-done.11.refs_2_.refs_0_, bf16[384,768]{1,0:T(8,128)(2,1)S(1)} %collective-permute-done.15.refs_3_.refs_1_, bf16[256,768]{1,0:T(8,128)(2,1)S(1)} %collective-permute-done.13.refs_2_, ...), custom_call_target="tpu_custom_call" | custom-call | flops 1000 | bytes 1000 | tf_op jit(solution)/shard_map/feed_side/pallas_call | solution.py:221
  60.2 1.4 %feed_side.2.acc_ref = f32[128,768]{1,0:T(8,128)S(1)} custom-call(bf16[256,384]{1,0:T(8,128)(2,1)S(1)} %get-tuple-element.75.columns_ref, bf16[384,768]{1,0:T(8,128)(2,1)S(1)} %get-tuple-element.67.refs_0_, bf16[384,768]{1,0:T(8,128)(2,1)S(1)} %get-tuple-element.78.refs_1_, bf16[256,768]{1,0:T(8,128)(2,1)S(1)} %collective-permute-done.13.refs_2_, ...), custom_call_target="tpu_custom_call" | custom-call | flops 1000 | bytes 1000 | tf_op jit(solution)/shard_map/feed_side/pallas_call | solution.py:221
  62.7 17.0 %all_to_all.10 = bf16[16,16,896]{2,1,0:T(8,128)(2,1)S(1)} all-to-all(bf16[16,16,896]{2,1,0:T(8,128)(2,1)S(1)} %bitcast.11), channel_id=1, replica_groups=mesh['groups'=2,'wide'=16] {'wide'}, dimensions={0} | all-to-all | bytes 917504 | tf_op jit(solution)/shard_map/all_to_all | solution.py:416
  79.8 1.3 %codes.1 = bf16[256,256]{1,0:T(8,128)(2,1)S(1)} custom-call(bf16[256,896]{1,0:T(8,128)(2,1)S(1)} %bitcast.9, bf16[8,768]{1,0:T(8,128)(2,1)S(1)} %copy-done.6, bf16[8,256,768]{2,1,0:T(8,128)(2,1)S(1)} %copy-done.2), custom_call_target="tpu_custom_call" | custom-call | tf_op jit(solution)/shard_map/codes/pallas_call | solution.py:417
  81.1 11.6 %all_to_all.11 = bf16[16,16,256]{2,1,0:T(8,128)(2,1)S(1)} all-to-all(bf16[16,16,256]{2,1,0:T(8,128)(2,1)S(1)} %bitcast.10), channel_id=1, replica_groups=mesh['groups'=2,'wide'=16] {'wide'}, dimensions={0} | all-to-all | bytes 262144 | tf_op jit(solution)/shard_map/all_to_all | solution.py:424
  (55 shorter events, 8.4 us)
Async XLA Ops:
  1.7 12.4 %collective-permute-start = (bf16[256,768]{1,0:T(8,128)(2,1)S(1)}, bf16[256,768]{1,0:T(8,128)(2,1)S(1)}, u32[]{:S(2)}, u32[]{:S(2)}) collective-permute-start(bf16[256,768]{1,0:T(8,128)(2,1)S(1)} %hold.1), channel_id=1, source_target_pairs={{0,2},{1,3},{2,0},{3,1},{4,6},{5,7},{6,4},{7,5},{8,10},{9,11},{10,... | collective-permute-start | bytes 1179656 | tf_op jit(solution)/shard_map/ppermute | solution.py:296
  4.7 10.6 %collective-permute-start.1 = (bf16[256,768]{1,0:T(8,128)(2,1)S(1)}, bf16[256,768]{1,0:T(8,128)(2,1)S(1)}, u32[]{:S(2)}, u32[]{:S(2)}) collective-permute-start(bf16[256,768]{1,0:T(8,128)(2,1)S(1)} %hold.1), channel_id=1, source_target_pairs={{0,4},{1,5},{2,6},{3,7},{4,0},{5,1},{6,2},{7,3},{8,12},{9,13},{10,... | collective-permute-start | bytes 1179656 | tf_op jit(solution)/shard_map/ppermute | solution.py:296
  6.3 9.0 %collective-permute-start.2 = (bf16[256,768]{1,0:T(8,128)(2,1)S(1)}, bf16[256,768]{1,0:T(8,128)(2,1)S(1)}, u32[]{:S(2)}, u32[]{:S(2)}) collective-permute-start(bf16[256,768]{1,0:T(8,128)(2,1)S(1)} %hold.1), channel_id=1, source_target_pairs={{4,8},{5,9},{6,10},{7,11},{8,4},{9,5},{10,6},{11,7},{20,24},{21,25... | collective-permute-start | bytes 1179656 | tf_op jit(solution)/shard_map/ppermute | solution.py:317
  7.0 1.4 %collective-permute-start.3 = (s32[2,64]{1,0:T(2,128)}, s32[2,64]{1,0:T(2,128)S(1)}, u32[]{:S(2)}, u32[]{:S(2)}) collective-permute-start(s32[2,64]{1,0:T(2,128)} %lengths_hbm.1), channel_id=1, source_target_pairs={{0,1},{1,0},{2,3},{3,2},{4,5},{5,4},{6,7},{7,6},{8,9},{9,8},{10,11... | collective-permute-start | bytes 1544 | tf_op jit(solution)/shard_map/ppermute | solution.py:296
  15.3 8.0 %copy-start = (bf16[2,384,768]{2,1,0:T(8,128)(2,1)S(1)}, bf16[2,384,768]{2,1,0:T(8,128)(2,1)}, u32[]{:S(2)}) copy-start(bf16[2,384,768]{2,1,0:T(8,128)(2,1)} %x_ref.3) | copy-start | bytes 3538948
  15.3 8.0 %copy-start.1 = (bf16[768,768]{1,0:T(8,128)(2,1)S(1)}, bf16[768,768]{1,0:T(8,128)(2,1)}, u32[]{:S(2)}) copy-start(bf16[768,768]{1,0:T(8,128)(2,1)} %wo_ref.3) | copy-start | bytes 3538948
  15.3 8.0 %copy-start.5 = (f32[768]{0:T(1024)S(1)}, f32[768]{0:T(1024)}, u32[]{:S(2)}) copy-start(f32[768]{0:T(1024)} %gain_ref.4) | copy-start | bytes 9220
  15.4 12.7 %collective-permute-start.6 = (bf16[256,768]{1,0:T(8,128)(2,1)S(1)}, bf16[256,768]{1,0:T(8,128)(2,1)S(1)}, u32[]{:S(2)}, u32[]{:S(2)}) collective-permute-start(bf16[256,768]{1,0:T(8,128)(2,1)S(1)} %broadcast_select_fusion.1), channel_id=1, source_target_pairs={{4,0},{5,1},{6,2},{7,3},{0,8},{1,9},{2,10},{3,11},{8,12},{9,13},{1... | collective-permute-start | bytes 1179656 | tf_op jit(solution)/shard_map/ppermute | solution.py:317
  21.3 9.2 %collective-permute-start.5 = (bf16[256,768]{1,0:T(8,128)(2,1)S(1)}, bf16[256,768]{1,0:T(8,128)(2,1)S(1)}, u32[]{:S(2)}, u32[]{:S(2)}) collective-permute-start(bf16[256,768]{1,0:T(8,128)(2,1)S(1)} %pad_maximum_fusion), channel_id=1, source_target_pairs={{0,16},{16,0},{1,17},{17,1},{2,18},{18,2},{3,19},{19,3},{4,20},{20... | collective-permute-start | bytes 1179656 | tf_op jit(solution)/shard_map/ppermute | solution.py:296
  22.8 8.8 %collective-permute-start.4 = (bf16[256,768]{1,0:T(8,128)(2,1)S(1)}, bf16[256,768]{1,0:T(8,128)(2,1)S(1)}, u32[]{:S(2)}, u32[]{:S(2)}) collective-permute-start(bf16[256,768]{1,0:T(8,128)(2,1)S(1)} %collective-permute-done.1.refs_8_), channel_id=1, source_target_pairs={{0,2},{1,3},{2,0},{3,1},{4,6},{5,7},{6,4},{7,5},{8,10},{9,11},{10,... | collective-permute-start | bytes 1179656 | tf_op jit(solution)/shard_map/ppermute | solution.py:296
  31.6 14.0 %collective-permute-start.11 = (bf16[384,768]{1,0:T(8,128)(2,1)S(1)}, bf16[384,768]{1,0:T(8,128)(2,1)S(1)}, u32[]{:S(2)}, u32[]{:S(2)}) collective-permute-start(bf16[384,768]{1,0:T(8,128)(2,1)S(1)} %get-tuple-element.67.refs_0_), channel_id=1, source_target_pairs={{0,1},{1,0},{2,3},{3,2},{4,5},{5,4},{6,7},{7,6},{8,9},{9,8},{10,11... | collective-permute-start | bytes 1769480 | tf_op jit(solution)/shard_map/ppermute | solution.py:296
  31.7 11.6 %collective-permute-start.8 = (bf16[256,768]{1,0:T(8,128)(2,1)S(1)}, bf16[256,768]{1,0:T(8,128)(2,1)S(1)}, u32[]{:S(2)}, u32[]{:S(2)}) collective-permute-start(bf16[256,768]{1,0:T(8,128)(2,1)S(1)} %pad_maximum_fusion.1), channel_id=1, source_target_pairs={{0,16},{16,0},{1,17},{17,1},{2,18},{18,2},{3,19},{19,3},{4,20},{20... | collective-permute-start | bytes 1179656 | tf_op jit(solution)/shard_map/ppermute | solution.py:296
  32.3 11.2 %collective-permute-start.7 = (bf16[256,768]{1,0:T(8,128)(2,1)S(1)}, bf16[256,768]{1,0:T(8,128)(2,1)S(1)}, u32[]{:S(2)}, u32[]{:S(2)}) collective-permute-start(bf16[256,768]{1,0:T(8,128)(2,1)S(1)} %collective-permute-done.6.refs_4_), channel_id=1, source_target_pairs={{0,2},{1,3},{2,0},{3,1},{4,6},{5,7},{6,4},{7,5},{8,10},{9,11},{10,... | collective-permute-start | bytes 1179656 | tf_op jit(solution)/shard_map/ppermute | solution.py:296
  32.8 12.8 %collective-permute-start.9 = (bf16[256,768]{1,0:T(8,128)(2,1)S(1)}, bf16[256,768]{1,0:T(8,128)(2,1)S(1)}, u32[]{:S(2)}, u32[]{:S(2)}) collective-permute-start(bf16[256,768]{1,0:T(8,128)(2,1)S(1)} %collective-permute-done.6.refs_4_), channel_id=1, source_target_pairs={{4,0},{5,1},{6,2},{7,3},{8,12},{9,13},{10,14},{11,15},{20,16},{21,... | collective-permute-start | bytes 1179656 | tf_op jit(solution)/shard_map/ppermute | solution.py:317
  34.1 5.6 %collective-permute-start.10 = (bf16[128,768]{1,0:T(8,128)(2,1)S(1)}, bf16[128,768]{1,0:T(8,128)(2,1)S(1)}, u32[]{:S(2)}, u32[]{:S(2)}) collective-permute-start(bf16[128,768]{1,0:T(8,128)(2,1)S(1)} %slice.28), channel_id=1, source_target_pairs={{4,8},{5,9},{6,10},{7,11},{8,4},{9,5},{10,6},{11,7},{20,24},{21,25... | collective-permute-start | bytes 589832 | tf_op jit(solution)/shard_map/ppermute | solution.py:317
  45.7 4.6 %collective-permute-start.15 = (bf16[384,768]{1,0:T(8,128)(2,1)S(1)}, bf16[384,768]{1,0:T(8,128)(2,1)S(1)}, u32[]{:S(2)}, u32[]{:S(2)}) collective-permute-start(bf16[384,768]{1,0:T(8,128)(2,1)S(1)} %get-tuple-element.78.refs_1_), channel_id=1, source_target_pairs={{0,1},{1,0},{2,3},{3,2},{4,5},{5,4},{6,7},{7,6},{8,9},{9,8},{10,11... | collective-permute-start | bytes 1769480 | tf_op jit(solution)/shard_map/ppermute | solution.py:296
  45.7 4.5 %copy-start.3 = (bf16[192,768]{1,0:T(8,128)(2,1)S(1)}, bf16[192,768]{1,0:T(8,128)(2,1)}, u32[]{:S(2)}) copy-start(bf16[192,768]{1,0:T(8,128)(2,1)} %refs_4_.1) | copy-start | bytes 884740
  45.7 4.5 %copy-start.4 = (bf16[192,768]{1,0:T(8,128)(2,1)S(1)}, bf16[192,768]{1,0:T(8,128)(2,1)}, u32[]{:S(2)}) copy-start(bf16[192,768]{1,0:T(8,128)(2,1)} %refs_5_.1) | copy-start | bytes 884740
  45.8 12.6 %collective-permute-start.13 = (bf16[256,768]{1,0:T(8,128)(2,1)S(1)}, bf16[256,768]{1,0:T(8,128)(2,1)S(1)}, u32[]{:S(2)}, u32[]{:S(2)}) collective-permute-start(bf16[256,768]{1,0:T(8,128)(2,1)S(1)} %pad_maximum_fusion.2), channel_id=1, source_target_pairs={{0,16},{16,0},{1,17},{17,1},{2,18},{18,2},{3,19},{19,3},{4,20},{20... | collective-permute-start | bytes 1179656 | tf_op jit(solution)/shard_map/ppermute | solution.py:296
  47.4 11.2 %collective-permute-start.12 = (bf16[256,768]{1,0:T(8,128)(2,1)S(1)}, bf16[256,768]{1,0:T(8,128)(2,1)S(1)}, u32[]{:S(2)}, u32[]{:S(2)}) collective-permute-start(bf16[256,768]{1,0:T(8,128)(2,1)S(1)} %broadcast_select_fusion.refs_7_), channel_id=1, source_target_pairs={{0,2},{1,3},{2,0},{3,1},{4,6},{5,7},{6,4},{7,5},{8,10},{9,11},{10,... | collective-permute-start | bytes 1179656 | tf_op jit(solution)/shard_map/ppermute | solution.py:296
  48.9 9.5 %collective-permute-start.14 = (bf16[128,768]{1,0:T(8,128)(2,1)S(1)}, bf16[128,768]{1,0:T(8,128)(2,1)S(1)}, u32[]{:S(2)}, u32[]{:S(2)}) collective-permute-start(bf16[128,768]{1,0:T(8,128)(2,1)S(1)} %slice.31), channel_id=1, source_target_pairs={{8,0},{9,1},{10,2},{11,3},{4,12},{5,13},{6,14},{7,15},{24,16},{25,... | collective-permute-start | bytes 589832 | tf_op jit(solution)/shard_map/ppermute | solution.py:317
  60.1 1.8 %collective-permute-start.16 = (f32[128,768]{1,0:T(8,128)S(1)}, f32[128,768]{1,0:T(8,128)S(1)}, u32[]{:S(2)}, u32[]{:S(2)}) collective-permute-start(f32[128,768]{1,0:T(8,128)S(1)} %feed_side.3), channel_id=1, source_target_pairs={{0,1},{1,0},{2,3},{3,2},{4,5},{5,4},{6,7},{7,6},{8,9},{9,8},{10,11... | collective-permute-start | bytes 1179656 | tf_op jit(solution)/shard_map/ppermute | solution.py:296
  60.2 19.6 %copy-start.2 = (bf16[8,256,768]{2,1,0:T(8,128)(2,1)S(1)}, bf16[8,256,768]{2,1,0:T(8,128)(2,1)}, u32[]{:S(2)}) copy-start(bf16[8,256,768]{2,1,0:T(8,128)(2,1)} %books_ref.1) | copy-start | bytes 9437188
  61.6 18.2 %copy-start.6 = (bf16[8,768]{1,0:T(8,128)(2,1)S(1)}, bf16[8,768]{1,0:T(8,128)(2,1)}, u32[]{:S(2)}) copy-start(bf16[8,768]{1,0:T(8,128)(2,1)} %coarse_ref.1) | copy-start | bytes 36868
  (2 other events, 3.6 us)

commit v4 on v3

--- a/solution.py
+++ b/solution.py
@@ -316,6 +316,10 @@
         pairs = [(4 * a + i, 4 * b + i) for a, b in hops for i in range(4)]
         return lax.ppermute(value, "wide", pairs)
 
+    def amid(value):
+        pairs = [(i, i ^ 12 if i // 4 in (1, 2) else i ^ 1) for i in range(16)]
+        return lax.ppermute(value, "wide", pairs)
+
     after = lax.optimization_barrier
 
     def blocks(i):
@@ -331,7 +335,7 @@
         return jnp.concatenate([a, b], axis=0)
 
     held = hold(w_input, w_down, common)
-    side0, near1, middle = side(held), near(held), along(held, [(1, 2), (2, 1)])
+    side0, near1, middle = side(held), near(held), amid(held)
     projected = encode_first(tokens)
     side0, near1, middle, projected = after((side0, near1, middle, projected))
     columns = projected[4]
@@ -342,9 +346,9 @@
     first = encode(0, projected, tokens)
     side1, x0, far2, first, projected = after((side1, x0, far2, first, projected))
 
-    side2, outer = side(far2), along(far2, [(1, 0), (2, 3)])
+    side2, outer = side(far2), near(far2)
     x1 = twin(cat(side1[split:], far2[split:]))
-    last_inner = along(x0[:both], [(1, 2), (2, 1)])
+    last_inner = amid(x0[:both])
     other_first = sibling(first[0])
     second = encode(1, projected, tokens)
     side2, x1, outer, last_inner, second, other_first = after((side2, x1, outer, last_inner, second, other_first))

time: 93.9 us -> 90.1 us (0.960)
  starting transfers between devices: 20.9 us -> 17.1 us
    ppermute x5 -> x2, starting transfers between devices: 9.91 us -> 5.62 us  [along(): return lax.ppermute(value, 'wide', pairs)]
    ppermute x12 -> x13, waiting for transfers between devices: 10.3 us -> 12.9 us  [flip(): return lambda value: lax.ppermute(value, axis_name, pairs)]
    ppermute x5 -> x2, waiting for transfers between devices: 4.03 us -> 1.67 us  [along(): return lax.ppermute(value, 'wide', pairs)]
    ppermute x12 -> x13, starting transfers between devices: 11 us -> 11.4 us  [flip(): return lambda value: lax.ppermute(value, axis_name, pairs)]
  transfers between devices with their start and end apart: 17 -> 17, of which waited for: 10 -> 11; matrix products, arithmetic and copies ran while one was open for 0% -> 0% of each run, Pallas kernels for 24% -> 25%
where the time goes in v4:
time: 90.1 us; the launch traced here: 89.9 us
  blocking collectives  28.6 us (32%)
  Pallas kernels  27.5 us (31%)
  starting transfers between devices  17.1 us (19%)
  waiting for transfers between devices  14.5 us (16%)
  between operations  0.92 us (1%)
    all_to_all x1, blocking collectives, local(): rows = lax.all_to_all(send, 'wide', split_axis=0, concat_axis=0, tiled=True)  16.9 us
    ppermute x13, waiting for transfers between devices, flip(): return lambda value: lax.ppermute(value, axis_name, pairs)  12.9 us
    all_to_all x1, blocking collectives, local(): lax.all_to_all(codes, 'wide', split_axis=0, concat_axis=0, tiled=True)  11.6 us
    ppermute x13, starting transfers between devices, flip(): return lambda value: lax.ppermute(value, axis_name, pairs)  11.4 us
    pallas_call x2, Pallas kernels, attend(): pl.pallas_call(functools.partial(attend_kernel, pack), out_shape=(jax.Sha...  9.51 us
    pallas_call x2, Pallas kernels, feed(): pl.pallas_call(functools.partial(feed_kernel, len(normed[0]), len(held),...  6.31 us
    pallas_call x1, Pallas kernels, project(): pl.pallas_call(functools.partial(project_kernel, wide=wide, capacity=capa...  5.68 us
    ppermute x2, starting transfers between devices, along(): return lax.ppermute(value, 'wide', pairs)  5.62 us
  transfers between devices with their start and end apart: 17, of which 11 were waited for; matrix products, arithmetic and copies ran while one was open for 0% of the time, Pallas kernels for 25%

profile of v4, /device:TPU:0, one launch (start us, length us, event | category | flops | bytes accessed | tf_op | source)
XLA Modules:
  0.0 89.9 jit_solution(2777676286131371283)
XLA Ops:
  0.6 1.1 %hold.1 = bf16[256,768]{1,0:T(8,128)(2,1)S(1)} custom-call(s32[1,1]{1,0:T(1,128)} %bitcast.group_ref, bf16[192,768]{1,0:T(8,128)(2,1)} %refs_4_.1, bf16[192,768]{1,0:T(8,128)(2,1)} %refs_5_.1), custom_call_target="tpu_custom_call" | custom-call | flops 1000 | bytes 1000 | tf_op jit(solution)/shard_map/hold/pallas_call | solution.py:143
  1.7 3.0 %collective-permute-start = (bf16[256,768]{1,0:T(8,128)(2,1)S(1)}, bf16[256,768]{1,0:T(8,128)(2,1)S(1)}, u32[]{:S(2)}, u32[]{:S(2)}) collective-permute-start(bf16[256,768]{1,0:T(8,128)(2,1)S(1)} %hold.1), channel_id=1, source_target_pairs={{0,2},{1,3},{2,0},{3,1},{4,6},{5,7},{6,4},{7,5},{8,10},{9,11},{10,... | collective-permute-start | bytes 1179656 | tf_op jit(solution)/shard_map/ppermute | solution.py:296
  4.7 1.6 %collective-permute-start.1 = (bf16[256,768]{1,0:T(8,128)(2,1)S(1)}, bf16[256,768]{1,0:T(8,128)(2,1)S(1)}, u32[]{:S(2)}, u32[]{:S(2)}) collective-permute-start(bf16[256,768]{1,0:T(8,128)(2,1)S(1)} %hold.1), channel_id=1, source_target_pairs={{0,4},{1,5},{2,6},{3,7},{4,0},{5,1},{6,2},{7,3},{8,12},{9,13},{10,... | collective-permute-start | bytes 1179656 | tf_op jit(solution)/shard_map/ppermute | solution.py:296
  6.8 1.1 %collective-permute-done.3.other_ref = s32[2,64]{1,0:T(2,128)S(1)} collective-permute-done((s32[2,64]{1,0:T(2,128)}, s32[2,64]{1,0:T(2,128)S(1)}, u32[]{:S(2)}, u32[]{:S(2)}) %collective-permute-start.3) | collective-permute-done | bytes 544 | tf_op jit(solution)/shard_map/ppermute | solution.py:296
  7.9 5.7 %project.1 = (bf16[768,768]{1,0:T(8,128)(2,1)S(1)}, bf16[768,768]{1,0:T(8,128)(2,1)S(1)}, bf16[768,768]{1,0:T(8,128)(2,1)S(1)}, bf16[768,64]{1,0:T(8,128)(2,1)S(...) custom-call(s32[2,64]{1,0:T(2,128)S(1)} %collective-permute-done.3.other_ref, s32[2,64]{1,0:T(2,128)} %lengths_hbm.1, ...), custom_call_target="tpu_custom_call" | custom-call | flops 1000 | bytes 1000 | tf_op jit(solution)/shard_map/project/pallas_call | solution.py:105
  13.9 1.5 %collective-permute-done.1.refs_8_ = bf16[256,768]{1,0:T(8,128)(2,1)S(1)} collective-permute-done((bf16[256,768]{1,0:T(8,128)(2,1)S(1)}, bf16[256,768]{1,0:T(8,128)(2,1)S(1)}, u32[]{:S(2)}, u32[]{:S(2)}) %collective-permute-start.1) | collective-permute-done | bytes 393248 | tf_op jit(solution)/shard_map/ppermute | solution.py:296
  15.4 4.1 %collective-permute-start.6 = (bf16[256,768]{1,0:T(8,128)(2,1)S(1)}, bf16[256,768]{1,0:T(8,128)(2,1)S(1)}, u32[]{:S(2)}, u32[]{:S(2)}) collective-permute-start(bf16[256,768]{1,0:T(8,128)(2,1)S(1)} %broadcast_select_fusion.1), channel_id=1, source_target_pairs={{4,0},{5,1},{6,2},{7,3},{0,8},{1,9},{2,10},{3,11},{8,12},{9,13},{1... | collective-permute-start | bytes 1179656 | tf_op jit(solution)/shard_map/ppermute | solution.py:317
  19.6 1.6 %collective-permute-start.5 = (bf16[256,768]{1,0:T(8,128)(2,1)S(1)}, bf16[256,768]{1,0:T(8,128)(2,1)S(1)}, u32[]{:S(2)}, u32[]{:S(2)}) collective-permute-start(bf16[256,768]{1,0:T(8,128)(2,1)S(1)} %pad_maximum_fusion), channel_id=1, source_target_pairs={{0,16},{16,0},{1,17},{17,1},{2,18},{18,2},{3,19},{19,3},{4,20},{20... | collective-permute-start | bytes 1179656 | tf_op jit(solution)/shard_map/ppermute | solution.py:296
  21.6 4.8 %attend.2 = (bf16[384,768]{1,0:T(8,128)(2,1)S(1)}, f32[64,768]{1,0:T(8,128)S(1)}) custom-call(bf16[768,768]{1,0:T(8,128)(2,1)S(1)} %get-tuple-element.71.q_ref, bf16[768,768]{1,0:T(8,128)(2,1)S(1)} %get-tuple-element.72.k_ref, bf16[768,768]{1,0:T(8,128)(2,1)S(1)} %get-tuple-element.73.v_ref, bf16[768,64]{1,0:T(8,128)(2,1)S(1)} %get-tuple-element.74.rows_ref, ...), custom_call_target="tpu_custom_call" | custom-call | flops 1000 | bytes 1000 | tf_op jit(solution)/shard_map/attend/pallas_call | solution.py:193
  26.4 2.3 %collective-permute-done.5.refs_7_ = bf16[256,768]{1,0:T(8,128)(2,1)S(1)} collective-permute-done((bf16[256,768]{1,0:T(8,128)(2,1)S(1)}, bf16[256,768]{1,0:T(8,128)(2,1)S(1)}, u32[]{:S(2)}, u32[]{:S(2)}) %collective-permute-start.5) | collective-permute-done | bytes 393248 | tf_op jit(solution)/shard_map/ppermute | solution.py:296
  28.7 1.2 %collective-permute-done.4.refs_9_ = bf16[256,768]{1,0:T(8,128)(2,1)S(1)} collective-permute-done((bf16[256,768]{1,0:T(8,128)(2,1)S(1)}, bf16[256,768]{1,0:T(8,128)(2,1)S(1)}, u32[]{:S(2)}, u32[]{:S(2)}) %collective-permute-start.4) | collective-permute-done | bytes 393248 | tf_op jit(solution)/shard_map/ppermute | solution.py:296
  31.2 4.8 %attend.3 = (bf16[384,768]{1,0:T(8,128)(2,1)S(1)}, f32[64,768]{1,0:T(8,128)S(1)}) custom-call(bf16[768,768]{1,0:T(8,128)(2,1)S(1)} %get-tuple-element.71.q_ref, bf16[768,768]{1,0:T(8,128)(2,1)S(1)} %get-tuple-element.72.k_ref, bf16[768,768]{1,0:T(8,128)(2,1)S(1)} %get-tuple-element.73.v_ref, bf16[768,64]{1,0:T(8,128)(2,1)S(1)} %get-tuple-element.74.rows_ref, ...), custom_call_target="tpu_custom_call" | custom-call | flops 1000 | bytes 1000 | tf_op jit(solution)/shard_map/attend/pallas_call | solution.py:193
  36.0 5.6 %collective-permute-done.8.refs_10_.refs_5_ = bf16[256,768]{1,0:T(8,128)(2,1)S(1)} collective-permute-done((bf16[256,768]{1,0:T(8,128)(2,1)S(1)}, bf16[256,768]{1,0:T(8,128)(2,1)S(1)}, u32[]{:S(2)}, u32[]{:S(2)}) %collective-permute-start.8) | collective-permute-done | bytes 393248 | tf_op jit(solution)/shard_map/ppermute | solution.py:296
  42.2 1.6 %collective-permute-start.13 = (bf16[256,768]{1,0:T(8,128)(2,1)S(1)}, bf16[256,768]{1,0:T(8,128)(2,1)S(1)}, u32[]{:S(2)}, u32[]{:S(2)}) collective-permute-start(bf16[256,768]{1,0:T(8,128)(2,1)S(1)} %pad_maximum_fusion.2), channel_id=1, source_target_pairs={{0,16},{16,0},{1,17},{17,1},{2,18},{18,2},{3,19},{19,3},{4,20},{20... | collective-permute-start | bytes 1179656 | tf_op jit(solution)/shard_map/ppermute | solution.py:296
  43.8 1.5 %collective-permute-start.12 = (bf16[256,768]{1,0:T(8,128)(2,1)S(1)}, bf16[256,768]{1,0:T(8,128)(2,1)S(1)}, u32[]{:S(2)}, u32[]{:S(2)}) collective-permute-start(bf16[256,768]{1,0:T(8,128)(2,1)S(1)} %broadcast_select_fusion.refs_7_), channel_id=1, source_target_pairs={{0,2},{1,3},{2,0},{3,1},{4,6},{5,7},{6,4},{7,5},{8,10},{9,11},{10,... | collective-permute-start | bytes 1179656 | tf_op jit(solution)/shard_map/ppermute | solution.py:296
  45.3 1.5 %collective-permute-start.14 = (bf16[128,768]{1,0:T(8,128)(2,1)S(1)}, bf16[128,768]{1,0:T(8,128)(2,1)S(1)}, u32[]{:S(2)}, u32[]{:S(2)}) collective-permute-start(bf16[128,768]{1,0:T(8,128)(2,1)S(1)} %slice.31), channel_id=1, source_target_pairs={{8,0},{9,1},{10,2},{11,3},{4,12},{5,13},{6,14},{7,15},{24,16},{25,... | collective-permute-start | bytes 589832 | tf_op jit(solution)/shard_map/ppermute | solution.py:317
  46.9 3.8 %feed.2 = (f32[128,768]{1,0:T(8,128)S(1)}, f32[128,768]{1,0:T(8,128)S(1)}) custom-call(bf16[256,384]{1,0:T(8,128)(2,1)S(1)} %get-tuple-element.75.columns_ref, bf16[384,768]{1,0:T(8,128)(2,1)S(1)} %get-tuple-element.67.refs_0_, bf16[384,768]{1,0:T(8,128)(2,1)S(1)} %get-tuple-element.78.refs_1_, bf16[384,768]{1,0:T(8,128)(2,1)S(1)} %collective-permute-done.11.refs_2_.refs_0_, ...), custom_call_target="tpu_custom_call" | custom-call | flops 1000 | bytes 1000 | tf_op jit(solution)/shard_map/feed/pallas_call | solution.py:254
  50.7 2.5 %feed.3 = (f32[128,768]{1,0:T(8,128)S(1)}, f32[128,768]{1,0:T(8,128)S(1)}) custom-call(bf16[256,384]{1,0:T(8,128)(2,1)S(1)} %get-tuple-element.75.columns_ref, bf16[384,768]{1,0:T(8,128)(2,1)S(1)} %get-tuple-element.67.refs_0_, bf16[384,768]{1,0:T(8,128)(2,1)S(1)} %get-tuple-element.78.refs_1_, bf16[384,768]{1,0:T(8,128)(2,1)S(1)} %collective-permute-done.11.refs_2_.refs_0_, ...), custom_call_target="tpu_custom_call" | custom-call | flops 1000 | bytes 1000 | tf_op jit(solution)/shard_map/feed/pallas_call | solution.py:254
  53.2 1.7 %collective-permute-done.14 = bf16[128,768]{1,0:T(8,128)(2,1)S(1)} collective-permute-done((bf16[128,768]{1,0:T(8,128)(2,1)S(1)}, bf16[128,768]{1,0:T(8,128)(2,1)S(1)}, u32[]{:S(2)}, u32[]{:S(2)}) %collective-permute-start.14) | collective-permute-done | bytes 196640 | tf_op jit(solution)/shard_map/ppermute | solution.py:317
  55.1 1.4 %feed_side.3 = f32[128,768]{1,0:T(8,128)S(1)} custom-call(bf16[256,384]{1,0:T(8,128)(2,1)S(1)} %get-tuple-element.75.columns_ref, bf16[384,768]{1,0:T(8,128)(2,1)S(1)} %collective-permute-done.11.refs_2_.refs_0_, bf16[384,768]{1,0:T(8,128)(2,1)S(1)} %collective-permute-done.15.refs_3_.refs_1_, bf16[256,768]{1,0:T(8,128)(2,1)S(1)} %collective-permute-done.13.refs_2_, ...), custom_call_target="tpu_custom_call" | custom-call | flops 1000 | bytes 1000 | tf_op jit(solution)/shard_map/feed_side/pallas_call | solution.py:221
  56.6 1.4 %feed_side.2.acc_ref = f32[128,768]{1,0:T(8,128)S(1)} custom-call(bf16[256,384]{1,0:T(8,128)(2,1)S(1)} %get-tuple-element.75.columns_ref, bf16[384,768]{1,0:T(8,128)(2,1)S(1)} %get-tuple-element.67.refs_0_, bf16[384,768]{1,0:T(8,128)(2,1)S(1)} %get-tuple-element.78.refs_1_, bf16[256,768]{1,0:T(8,128)(2,1)S(1)} %collective-permute-done.13.refs_2_, ...), custom_call_target="tpu_custom_call" | custom-call | flops 1000 | bytes 1000 | tf_op jit(solution)/shard_map/feed_side/pallas_call | solution.py:221
  59.1 16.9 %all_to_all.10 = bf16[16,16,896]{2,1,0:T(8,128)(2,1)S(1)} all-to-all(bf16[16,16,896]{2,1,0:T(8,128)(2,1)S(1)} %bitcast.11), channel_id=1, replica_groups=mesh['groups'=2,'wide'=16] {'wide'}, dimensions={0} | all-to-all | bytes 917504 | tf_op jit(solution)/shard_map/all_to_all | solution.py:420
  76.1 1.3 %codes.1 = bf16[256,256]{1,0:T(8,128)(2,1)S(1)} custom-call(bf16[256,896]{1,0:T(8,128)(2,1)S(1)} %bitcast.9, bf16[8,768]{1,0:T(8,128)(2,1)S(1)} %copy-done.6, bf16[8,256,768]{2,1,0:T(8,128)(2,1)S(1)} %copy-done.2), custom_call_target="tpu_custom_call" | custom-call | tf_op jit(solution)/shard_map/codes/pallas_call | solution.py:421
  77.4 11.6 %all_to_all.11 = bf16[16,16,256]{2,1,0:T(8,128)(2,1)S(1)} all-to-all(bf16[16,16,256]{2,1,0:T(8,128)(2,1)S(1)} %bitcast.10), channel_id=1, replica_groups=mesh['groups'=2,'wide'=16] {'wide'}, dimensions={0} | all-to-all | bytes 262144 | tf_op jit(solution)/shard_map/all_to_all | solution.py:428
  (55 shorter events, 5.6 us)
Async XLA Ops:
  1.7 12.1 %collective-permute-start = (bf16[256,768]{1,0:T(8,128)(2,1)S(1)}, bf16[256,768]{1,0:T(8,128)(2,1)S(1)}, u32[]{:S(2)}, u32[]{:S(2)}) collective-permute-start(bf16[256,768]{1,0:T(8,128)(2,1)S(1)} %hold.1), channel_id=1, source_target_pairs={{0,2},{1,3},{2,0},{3,1},{4,6},{5,7},{6,4},{7,5},{8,10},{9,11},{10,... | collective-permute-start | bytes 1179656 | tf_op jit(solution)/shard_map/ppermute | solution.py:296
  4.7 10.6 %collective-permute-start.1 = (bf16[256,768]{1,0:T(8,128)(2,1)S(1)}, bf16[256,768]{1,0:T(8,128)(2,1)S(1)}, u32[]{:S(2)}, u32[]{:S(2)}) collective-permute-start(bf16[256,768]{1,0:T(8,128)(2,1)S(1)} %hold.1), channel_id=1, source_target_pairs={{0,4},{1,5},{2,6},{3,7},{4,0},{5,1},{6,2},{7,3},{8,12},{9,13},{10,... | collective-permute-start | bytes 1179656 | tf_op jit(solution)/shard_map/ppermute | solution.py:296
  6.3 9.0 %collective-permute-start.2 = (bf16[256,768]{1,0:T(8,128)(2,1)S(1)}, bf16[256,768]{1,0:T(8,128)(2,1)S(1)}, u32[]{:S(2)}, u32[]{:S(2)}) collective-permute-start(bf16[256,768]{1,0:T(8,128)(2,1)S(1)} %hold.1), channel_id=1, source_target_pairs={{0,1},{1,0},{2,3},{3,2},{4,8},{5,9},{6,10},{7,11},{8,4},{9,5},{10,... | collective-permute-start | bytes 1179656 | tf_op jit(solution)/shard_map/ppermute | solution.py:321
  6.3 1.6 %collective-permute-start.3 = (s32[2,64]{1,0:T(2,128)}, s32[2,64]{1,0:T(2,128)S(1)}, u32[]{:S(2)}, u32[]{:S(2)}) collective-permute-start(s32[2,64]{1,0:T(2,128)} %lengths_hbm.1), channel_id=1, source_target_pairs={{0,1},{1,0},{2,3},{3,2},{4,5},{5,4},{6,7},{7,6},{8,9},{9,8},{10,11... | collective-permute-start | bytes 1544 | tf_op jit(solution)/shard_map/ppermute | solution.py:296
  15.3 6.3 %copy-start = (bf16[2,384,768]{2,1,0:T(8,128)(2,1)S(1)}, bf16[2,384,768]{2,1,0:T(8,128)(2,1)}, u32[]{:S(2)}) copy-start(bf16[2,384,768]{2,1,0:T(8,128)(2,1)} %x_ref.3) | copy-start | bytes 3538948
  15.3 6.3 %copy-start.1 = (bf16[768,768]{1,0:T(8,128)(2,1)S(1)}, bf16[768,768]{1,0:T(8,128)(2,1)}, u32[]{:S(2)}) copy-start(bf16[768,768]{1,0:T(8,128)(2,1)} %wo_ref.3) | copy-start | bytes 3538948
  15.3 6.3 %copy-start.5 = (f32[768]{0:T(1024)S(1)}, f32[768]{0:T(1024)}, u32[]{:S(2)}) copy-start(f32[768]{0:T(1024)} %gain_ref.4) | copy-start | bytes 9220
  15.4 11.0 %collective-permute-start.6 = (bf16[256,768]{1,0:T(8,128)(2,1)S(1)}, bf16[256,768]{1,0:T(8,128)(2,1)S(1)}, u32[]{:S(2)}, u32[]{:S(2)}) collective-permute-start(bf16[256,768]{1,0:T(8,128)(2,1)S(1)} %broadcast_select_fusion.1), channel_id=1, source_target_pairs={{4,0},{5,1},{6,2},{7,3},{0,8},{1,9},{2,10},{3,11},{8,12},{9,13},{1... | collective-permute-start | bytes 1179656 | tf_op jit(solution)/shard_map/ppermute | solution.py:317
  19.6 9.2 %collective-permute-start.5 = (bf16[256,768]{1,0:T(8,128)(2,1)S(1)}, bf16[256,768]{1,0:T(8,128)(2,1)S(1)}, u32[]{:S(2)}, u32[]{:S(2)}) collective-permute-start(bf16[256,768]{1,0:T(8,128)(2,1)S(1)} %pad_maximum_fusion), channel_id=1, source_target_pairs={{0,16},{16,0},{1,17},{17,1},{2,18},{18,2},{3,19},{19,3},{4,20},{20... | collective-permute-start | bytes 1179656 | tf_op jit(solution)/shard_map/ppermute | solution.py:296
  21.1 8.8 %collective-permute-start.4 = (bf16[256,768]{1,0:T(8,128)(2,1)S(1)}, bf16[256,768]{1,0:T(8,128)(2,1)S(1)}, u32[]{:S(2)}, u32[]{:S(2)}) collective-permute-start(bf16[256,768]{1,0:T(8,128)(2,1)S(1)} %collective-permute-done.1.refs_8_), channel_id=1, source_target_pairs={{0,2},{1,3},{2,0},{3,1},{4,6},{5,7},{6,4},{7,5},{8,10},{9,11},{10,... | collective-permute-start | bytes 1179656 | tf_op jit(solution)/shard_map/ppermute | solution.py:296
  29.9 12.2 %collective-permute-start.11 = (bf16[384,768]{1,0:T(8,128)(2,1)S(1)}, bf16[384,768]{1,0:T(8,128)(2,1)S(1)}, u32[]{:S(2)}, u32[]{:S(2)}) collective-permute-start(bf16[384,768]{1,0:T(8,128)(2,1)S(1)} %get-tuple-element.67.refs_0_), channel_id=1, source_target_pairs={{0,1},{1,0},{2,3},{3,2},{4,5},{5,4},{6,7},{7,6},{8,9},{9,8},{10,11... | collective-permute-start | bytes 1769480 | tf_op jit(solution)/shard_map/ppermute | solution.py:296
  30.0 11.6 %collective-permute-start.8 = (bf16[256,768]{1,0:T(8,128)(2,1)S(1)}, bf16[256,768]{1,0:T(8,128)(2,1)S(1)}, u32[]{:S(2)}, u32[]{:S(2)}) collective-permute-start(bf16[256,768]{1,0:T(8,128)(2,1)S(1)} %pad_maximum_fusion.1), channel_id=1, source_target_pairs={{0,16},{16,0},{1,17},{17,1},{2,18},{18,2},{3,19},{19,3},{4,20},{20... | collective-permute-start | bytes 1179656 | tf_op jit(solution)/shard_map/ppermute | solution.py:296
  30.6 11.2 %collective-permute-start.7 = (bf16[256,768]{1,0:T(8,128)(2,1)S(1)}, bf16[256,768]{1,0:T(8,128)(2,1)S(1)}, u32[]{:S(2)}, u32[]{:S(2)}) collective-permute-start(bf16[256,768]{1,0:T(8,128)(2,1)S(1)} %collective-permute-done.6.refs_4_), channel_id=1, source_target_pairs={{0,2},{1,3},{2,0},{3,1},{4,6},{5,7},{6,4},{7,5},{8,10},{9,11},{10,... | collective-permute-start | bytes 1179656 | tf_op jit(solution)/shard_map/ppermute | solution.py:296
  31.1 11.0 %collective-permute-start.9 = (bf16[256,768]{1,0:T(8,128)(2,1)S(1)}, bf16[256,768]{1,0:T(8,128)(2,1)S(1)}, u32[]{:S(2)}, u32[]{:S(2)}) collective-permute-start(bf16[256,768]{1,0:T(8,128)(2,1)S(1)} %collective-permute-done.6.refs_4_), channel_id=1, source_target_pairs={{0,4},{1,5},{2,6},{3,7},{4,0},{5,1},{6,2},{7,3},{8,12},{9,13},{10,... | collective-permute-start | bytes 1179656 | tf_op jit(solution)/shard_map/ppermute | solution.py:296
  31.2 4.8 %collective-permute-start.10 = (bf16[128,768]{1,0:T(8,128)(2,1)S(1)}, bf16[128,768]{1,0:T(8,128)(2,1)S(1)}, u32[]{:S(2)}, u32[]{:S(2)}) collective-permute-start(bf16[128,768]{1,0:T(8,128)(2,1)S(1)} %slice.28), channel_id=1, source_target_pairs={{0,1},{1,0},{2,3},{3,2},{4,8},{5,9},{6,10},{7,11},{8,4},{9,5},{10,... | collective-permute-start | bytes 589832 | tf_op jit(solution)/shard_map/ppermute | solution.py:321
  42.1 4.8 %collective-permute-start.15 = (bf16[384,768]{1,0:T(8,128)(2,1)S(1)}, bf16[384,768]{1,0:T(8,128)(2,1)S(1)}, u32[]{:S(2)}, u32[]{:S(2)}) collective-permute-start(bf16[384,768]{1,0:T(8,128)(2,1)S(1)} %get-tuple-element.78.refs_1_), channel_id=1, source_target_pairs={{0,1},{1,0},{2,3},{3,2},{4,5},{5,4},{6,7},{7,6},{8,9},{9,8},{10,11... | collective-permute-start | bytes 1769480 | tf_op jit(solution)/shard_map/ppermute | solution.py:296
  42.1 4.7 %copy-start.3 = (bf16[192,768]{1,0:T(8,128)(2,1)S(1)}, bf16[192,768]{1,0:T(8,128)(2,1)}, u32[]{:S(2)}) copy-start(bf16[192,768]{1,0:T(8,128)(2,1)} %refs_4_.1) | copy-start | bytes 884740
  42.2 4.7 %copy-start.4 = (bf16[192,768]{1,0:T(8,128)(2,1)S(1)}, bf16[192,768]{1,0:T(8,128)(2,1)}, u32[]{:S(2)}) copy-start(bf16[192,768]{1,0:T(8,128)(2,1)} %refs_5_.1) | copy-start | bytes 884740
  42.2 12.6 %collective-permute-start.13 = (bf16[256,768]{1,0:T(8,128)(2,1)S(1)}, bf16[256,768]{1,0:T(8,128)(2,1)S(1)}, u32[]{:S(2)}, u32[]{:S(2)}) collective-permute-start(bf16[256,768]{1,0:T(8,128)(2,1)S(1)} %pad_maximum_fusion.2), channel_id=1, source_target_pairs={{0,16},{16,0},{1,17},{17,1},{2,18},{18,2},{3,19},{19,3},{4,20},{20... | collective-permute-start | bytes 1179656 | tf_op jit(solution)/shard_map/ppermute | solution.py:296
  43.8 11.2 %collective-permute-start.12 = (bf16[256,768]{1,0:T(8,128)(2,1)S(1)}, bf16[256,768]{1,0:T(8,128)(2,1)S(1)}, u32[]{:S(2)}, u32[]{:S(2)}) collective-permute-start(bf16[256,768]{1,0:T(8,128)(2,1)S(1)} %broadcast_select_fusion.refs_7_), channel_id=1, source_target_pairs={{0,2},{1,3},{2,0},{3,1},{4,6},{5,7},{6,4},{7,5},{8,10},{9,11},{10,... | collective-permute-start | bytes 1179656 | tf_op jit(solution)/shard_map/ppermute | solution.py:296
  45.3 9.5 %collective-permute-start.14 = (bf16[128,768]{1,0:T(8,128)(2,1)S(1)}, bf16[128,768]{1,0:T(8,128)(2,1)S(1)}, u32[]{:S(2)}, u32[]{:S(2)}) collective-permute-start(bf16[128,768]{1,0:T(8,128)(2,1)S(1)} %slice.31), channel_id=1, source_target_pairs={{8,0},{9,1},{10,2},{11,3},{4,12},{5,13},{6,14},{7,15},{24,16},{25,... | collective-permute-start | bytes 589832 | tf_op jit(solution)/shard_map/ppermute | solution.py:317
  56.5 1.8 %collective-permute-start.16 = (f32[128,768]{1,0:T(8,128)S(1)}, f32[128,768]{1,0:T(8,128)S(1)}, u32[]{:S(2)}, u32[]{:S(2)}) collective-permute-start(f32[128,768]{1,0:T(8,128)S(1)} %feed_side.3), channel_id=1, source_target_pairs={{0,1},{1,0},{2,3},{3,2},{4,5},{5,4},{6,7},{7,6},{8,9},{9,8},{10,11... | collective-permute-start | bytes 1179656 | tf_op jit(solution)/shard_map/ppermute | solution.py:296
  56.6 19.5 %copy-start.2 = (bf16[8,256,768]{2,1,0:T(8,128)(2,1)S(1)}, bf16[8,256,768]{2,1,0:T(8,128)(2,1)}, u32[]{:S(2)}) copy-start(bf16[8,256,768]{2,1,0:T(8,128)(2,1)} %books_ref.1) | copy-start | bytes 9437188
  58.0 18.1 %copy-start.6 = (bf16[8,768]{1,0:T(8,128)(2,1)S(1)}, bf16[8,768]{1,0:T(8,128)(2,1)}, u32[]{:S(2)}) copy-start(bf16[8,768]{1,0:T(8,128)(2,1)} %coarse_ref.1) | copy-start | bytes 36868
  (2 other events, 3.6 us)

commit v5 on v4

--- a/solution.py
+++ b/solution.py
@@ -349,14 +349,13 @@
     side2, outer = side(far2), near(far2)
     x1 = twin(cat(side1[split:], far2[split:]))
     last_inner = amid(x0[:both])
-    other_first = sibling(first[0])
     second = encode(1, projected, tokens)
-    side2, x1, outer, last_inner, second, other_first = after((side2, x1, outer, last_inner, second, other_first))
+    side2, x1, outer, last_inner, second = after((side2, x1, outer, last_inner, second))
 
     far3 = jnp.where(inner, middle, outer)
     side3, x2 = side(far3), twin(cat(side2[split:], far3[split:]))
     last_outer = along(x1[:both], [(2, 0), (1, 3)])
-    normed = ((first[0], second[0]), (other_first, sibling(second[0])))
+    normed = ((first[0], second[0]), (sibling(first[0]), sibling(second[0])))
     own = [(0, slice(0, rows), 1, slice(0, rows))]
     pieces = own + blocks(2) + rest(3) + blocks(4) + rest(3, both) + blocks(5) + rest(6)
     acc = feed(columns, normed, [w_input, w_down, side0, x0, near1, side1, x1], pieces, ([first[1], second[1]], []))

time: 90.1 us -> 86.9 us (0.964)
  waiting for transfers between devices: 14.5 us -> 10.9 us
    ppermute x13, waiting for transfers between devices: 12.9 us -> 9.23 us  [flip(): return lambda value: lax.ppermute(value, axis_name, pairs)]
  transfers between devices with their start and end apart: 17 -> 17, of which waited for: 11 -> 11; matrix products, arithmetic and copies ran while one was open for 0% -> 0% of each run, Pallas kernels for 25% -> 26%
where the time goes in v5:
time: 86.9 us; the launch traced here: 86.7 us
  blocking collectives  28.5 us (33%)
  Pallas kernels  27.5 us (32%)
  starting transfers between devices  17.6 us (20%)
  waiting for transfers between devices  10.9 us (13%)
  between operations  0.92 us (1%)
    all_to_all x1, blocking collectives, local(): rows = lax.all_to_all(send, 'wide', split_axis=0, concat_axis=0, tiled=True)  16.9 us
    ppermute x13, starting transfers between devices, flip(): return lambda value: lax.ppermute(value, axis_name, pairs)  11.9 us
    all_to_all x1, blocking collectives, local(): lax.all_to_all(codes, 'wide', split_axis=0, concat_axis=0, tiled=True)  11.6 us
    pallas_call x2, Pallas kernels, attend(): pl.pallas_call(functools.partial(attend_kernel, pack), out_shape=(jax.Sha...  9.51 us
    ppermute x13, waiting for transfers between devices, flip(): return lambda value: lax.ppermute(value, axis_name, pairs)  9.23 us
    pallas_call x2, Pallas kernels, feed(): pl.pallas_call(functools.partial(feed_kernel, len(normed[0]), len(held),...  6.32 us
    pallas_call x1, Pallas kernels, project(): pl.pallas_call(functools.partial(project_kernel, wide=wide, capacity=capa...  5.68 us
    ppermute x2, starting transfers between devices, along(): return lax.ppermute(value, 'wide', pairs)  5.62 us
  transfers between devices with their start and end apart: 17, of which 11 were waited for; matrix products, arithmetic and copies ran while one was open for 0% of the time, Pallas kernels for 26%

profile of v5, /device:TPU:0, one launch (start us, length us, event | category | flops | bytes accessed | tf_op | source)
XLA Modules:
  0.0 86.7 jit_solution(4459684957781776992)
XLA Ops:
  0.6 1.1 %hold.1 = bf16[256,768]{1,0:T(8,128)(2,1)S(1)} custom-call(s32[1,1]{1,0:T(1,128)} %bitcast.group_ref, bf16[192,768]{1,0:T(8,128)(2,1)} %refs_4_.1, bf16[192,768]{1,0:T(8,128)(2,1)} %refs_5_.1), custom_call_target="tpu_custom_call" | custom-call | flops 1000 | bytes 1000 | tf_op jit(solution)/shard_map/hold/pallas_call | solution.py:143
  1.7 3.0 %collective-permute-start = (bf16[256,768]{1,0:T(8,128)(2,1)S(1)}, bf16[256,768]{1,0:T(8,128)(2,1)S(1)}, u32[]{:S(2)}, u32[]{:S(2)}) collective-permute-start(bf16[256,768]{1,0:T(8,128)(2,1)S(1)} %hold.1), channel_id=1, source_target_pairs={{0,2},{1,3},{2,0},{3,1},{4,6},{5,7},{6,4},{7,5},{8,10},{9,11},{10,... | collective-permute-start | bytes 1179656 | tf_op jit(solution)/shard_map/ppermute | solution.py:296
  4.7 1.6 %collective-permute-start.1 = (bf16[256,768]{1,0:T(8,128)(2,1)S(1)}, bf16[256,768]{1,0:T(8,128)(2,1)S(1)}, u32[]{:S(2)}, u32[]{:S(2)}) collective-permute-start(bf16[256,768]{1,0:T(8,128)(2,1)S(1)} %hold.1), channel_id=1, source_target_pairs={{0,4},{1,5},{2,6},{3,7},{4,0},{5,1},{6,2},{7,3},{8,12},{9,13},{10,... | collective-permute-start | bytes 1179656 | tf_op jit(solution)/shard_map/ppermute | solution.py:296
  6.8 1.1 %collective-permute-done.3.other_ref = s32[2,64]{1,0:T(2,128)S(1)} collective-permute-done((s32[2,64]{1,0:T(2,128)}, s32[2,64]{1,0:T(2,128)S(1)}, u32[]{:S(2)}, u32[]{:S(2)}) %collective-permute-start.3) | collective-permute-done | bytes 544 | tf_op jit(solution)/shard_map/ppermute | solution.py:296
  7.9 5.7 %project.1 = (bf16[768,768]{1,0:T(8,128)(2,1)S(1)}, bf16[768,768]{1,0:T(8,128)(2,1)S(1)}, bf16[768,768]{1,0:T(8,128)(2,1)S(1)}, bf16[768,64]{1,0:T(8,128)(2,1)S(...) custom-call(s32[2,64]{1,0:T(2,128)S(1)} %collective-permute-done.3.other_ref, s32[2,64]{1,0:T(2,128)} %lengths_hbm.1, ...), custom_call_target="tpu_custom_call" | custom-call | flops 1000 | bytes 1000 | tf_op jit(solution)/shard_map/project/pallas_call | solution.py:105
  13.9 1.5 %collective-permute-done.1.refs_8_ = bf16[256,768]{1,0:T(8,128)(2,1)S(1)} collective-permute-done((bf16[256,768]{1,0:T(8,128)(2,1)S(1)}, bf16[256,768]{1,0:T(8,128)(2,1)S(1)}, u32[]{:S(2)}, u32[]{:S(2)}) %collective-permute-start.1) | collective-permute-done | bytes 393248 | tf_op jit(solution)/shard_map/ppermute | solution.py:296
  15.4 4.1 %collective-permute-start.6 = (bf16[256,768]{1,0:T(8,128)(2,1)S(1)}, bf16[256,768]{1,0:T(8,128)(2,1)S(1)}, u32[]{:S(2)}, u32[]{:S(2)}) collective-permute-start(bf16[256,768]{1,0:T(8,128)(2,1)S(1)} %broadcast_select_fusion.1), channel_id=1, source_target_pairs={{4,0},{5,1},{6,2},{7,3},{0,8},{1,9},{2,10},{3,11},{8,12},{9,13},{1... | collective-permute-start | bytes 1179656 | tf_op jit(solution)/shard_map/ppermute | solution.py:317
  19.6 1.6 %collective-permute-start.5 = (bf16[256,768]{1,0:T(8,128)(2,1)S(1)}, bf16[256,768]{1,0:T(8,128)(2,1)S(1)}, u32[]{:S(2)}, u32[]{:S(2)}) collective-permute-start(bf16[256,768]{1,0:T(8,128)(2,1)S(1)} %pad_maximum_fusion), channel_id=1, source_target_pairs={{0,16},{16,0},{1,17},{17,1},{2,18},{18,2},{3,19},{19,3},{4,20},{20... | collective-permute-start | bytes 1179656 | tf_op jit(solution)/shard_map/ppermute | solution.py:296
  21.6 4.8 %attend.2 = (bf16[384,768]{1,0:T(8,128)(2,1)S(1)}, f32[64,768]{1,0:T(8,128)S(1)}) custom-call(bf16[768,768]{1,0:T(8,128)(2,1)S(1)} %get-tuple-element.70.q_ref, bf16[768,768]{1,0:T(8,128)(2,1)S(1)} %get-tuple-element.71.k_ref, bf16[768,768]{1,0:T(8,128)(2,1)S(1)} %get-tuple-element.72.v_ref, bf16[768,64]{1,0:T(8,128)(2,1)S(1)} %get-tuple-element.73.rows_ref, ...), custom_call_target="tpu_custom_call" | custom-call | flops 1000 | bytes 1000 | tf_op jit(solution)/shard_map/attend/pallas_call | solution.py:193
  26.4 2.3 %collective-permute-done.5.refs_7_ = bf16[256,768]{1,0:T(8,128)(2,1)S(1)} collective-permute-done((bf16[256,768]{1,0:T(8,128)(2,1)S(1)}, bf16[256,768]{1,0:T(8,128)(2,1)S(1)}, u32[]{:S(2)}, u32[]{:S(2)}) %collective-permute-start.5) | collective-permute-done | bytes 393248 | tf_op jit(solution)/shard_map/ppermute | solution.py:296
  28.7 1.3 %collective-permute-done.4.refs_9_ = bf16[256,768]{1,0:T(8,128)(2,1)S(1)} collective-permute-done((bf16[256,768]{1,0:T(8,128)(2,1)S(1)}, bf16[256,768]{1,0:T(8,128)(2,1)S(1)}, u32[]{:S(2)}, u32[]{:S(2)}) %collective-permute-start.4) | collective-permute-done | bytes 393248 | tf_op jit(solution)/shard_map/ppermute | solution.py:296
  31.7 4.8 %attend.3 = (bf16[384,768]{1,0:T(8,128)(2,1)S(1)}, f32[64,768]{1,0:T(8,128)S(1)}) custom-call(bf16[768,768]{1,0:T(8,128)(2,1)S(1)} %get-tuple-element.70.q_ref, bf16[768,768]{1,0:T(8,128)(2,1)S(1)} %get-tuple-element.71.k_ref, bf16[768,768]{1,0:T(8,128)(2,1)S(1)} %get-tuple-element.72.v_ref, bf16[768,64]{1,0:T(8,128)(2,1)S(1)} %get-tuple-element.73.rows_ref, ...), custom_call_target="tpu_custom_call" | custom-call | flops 1000 | bytes 1000 | tf_op jit(solution)/shard_map/attend/pallas_call | solution.py:193
  36.5 1.5 %collective-permute-done.8.refs_10_.refs_5_ = bf16[256,768]{1,0:T(8,128)(2,1)S(1)} collective-permute-done((bf16[256,768]{1,0:T(8,128)(2,1)S(1)}, bf16[256,768]{1,0:T(8,128)(2,1)S(1)}, u32[]{:S(2)}, u32[]{:S(2)}) %collective-permute-start.8) | collective-permute-done | bytes 393248 | tf_op jit(solution)/shard_map/ppermute | solution.py:296
  39.1 1.6 %collective-permute-start.12 = (bf16[256,768]{1,0:T(8,128)(2,1)S(1)}, bf16[256,768]{1,0:T(8,128)(2,1)S(1)}, u32[]{:S(2)}, u32[]{:S(2)}) collective-permute-start(bf16[256,768]{1,0:T(8,128)(2,1)S(1)} %pad_maximum_fusion.2), channel_id=1, source_target_pairs={{0,16},{16,0},{1,17},{17,1},{2,18},{18,2},{3,19},{19,3},{4,20},{20... | collective-permute-start | bytes 1179656 | tf_op jit(solution)/shard_map/ppermute | solution.py:296
  40.7 1.5 %collective-permute-start.11 = (bf16[256,768]{1,0:T(8,128)(2,1)S(1)}, bf16[256,768]{1,0:T(8,128)(2,1)S(1)}, u32[]{:S(2)}, u32[]{:S(2)}) collective-permute-start(bf16[256,768]{1,0:T(8,128)(2,1)S(1)} %broadcast_select_fusion.refs_7_), channel_id=1, source_target_pairs={{0,2},{1,3},{2,0},{3,1},{4,6},{5,7},{6,4},{7,5},{8,10},{9,11},{10,... | collective-permute-start | bytes 1179656 | tf_op jit(solution)/shard_map/ppermute | solution.py:296
  42.2 1.5 %collective-permute-start.13 = (bf16[128,768]{1,0:T(8,128)(2,1)S(1)}, bf16[128,768]{1,0:T(8,128)(2,1)S(1)}, u32[]{:S(2)}, u32[]{:S(2)}) collective-permute-start(bf16[128,768]{1,0:T(8,128)(2,1)S(1)} %slice.31), channel_id=1, source_target_pairs={{8,0},{9,1},{10,2},{11,3},{4,12},{5,13},{6,14},{7,15},{24,16},{25,... | collective-permute-start | bytes 589832 | tf_op jit(solution)/shard_map/ppermute | solution.py:317
  43.8 3.8 %feed.2 = (f32[128,768]{1,0:T(8,128)S(1)}, f32[128,768]{1,0:T(8,128)S(1)}) custom-call(bf16[256,384]{1,0:T(8,128)(2,1)S(1)} %get-tuple-element.74.columns_ref, bf16[384,768]{1,0:T(8,128)(2,1)S(1)} %get-tuple-element.66.refs_0_, bf16[384,768]{1,0:T(8,128)(2,1)S(1)} %get-tuple-element.77.refs_1_, bf16[384,768]{1,0:T(8,128)(2,1)S(1)} %collective-permute-done.14.refs_2_.refs_0_, ...), custom_call_target="tpu_custom_call" | custom-call | flops 1000 | bytes 1000 | tf_op jit(solution)/shard_map/feed/pallas_call | solution.py:254
  47.5 2.5 %feed.3 = (f32[128,768]{1,0:T(8,128)S(1)}, f32[128,768]{1,0:T(8,128)S(1)}) custom-call(bf16[256,384]{1,0:T(8,128)(2,1)S(1)} %get-tuple-element.74.columns_ref, bf16[384,768]{1,0:T(8,128)(2,1)S(1)} %get-tuple-element.66.refs_0_, bf16[384,768]{1,0:T(8,128)(2,1)S(1)} %get-tuple-element.77.refs_1_, bf16[384,768]{1,0:T(8,128)(2,1)S(1)} %collective-permute-done.14.refs_2_.refs_0_, ...), custom_call_target="tpu_custom_call" | custom-call | flops 1000 | bytes 1000 | tf_op jit(solution)/shard_map/feed/pallas_call | solution.py:254
  50.1 1.7 %collective-permute-done.13 = bf16[128,768]{1,0:T(8,128)(2,1)S(1)} collective-permute-done((bf16[128,768]{1,0:T(8,128)(2,1)S(1)}, bf16[128,768]{1,0:T(8,128)(2,1)S(1)}, u32[]{:S(2)}, u32[]{:S(2)}) %collective-permute-start.13) | collective-permute-done | bytes 196640 | tf_op jit(solution)/shard_map/ppermute | solution.py:317
  51.9 1.4 %feed_side.3 = f32[128,768]{1,0:T(8,128)S(1)} custom-call(bf16[256,384]{1,0:T(8,128)(2,1)S(1)} %get-tuple-element.74.columns_ref, bf16[384,768]{1,0:T(8,128)(2,1)S(1)} %collective-permute-done.14.refs_2_.refs_0_, bf16[384,768]{1,0:T(8,128)(2,1)S(1)} %collective-permute-done.15.refs_3_.refs_1_, bf16[256,768]{1,0:T(8,128)(2,1)S(1)} %collective-permute-done.12.refs_2_, ...), custom_call_target="tpu_custom_call" | custom-call | flops 1000 | bytes 1000 | tf_op jit(solution)/shard_map/feed_side/pallas_call | solution.py:221
  53.4 1.4 %feed_side.2.acc_ref = f32[128,768]{1,0:T(8,128)S(1)} custom-call(bf16[256,384]{1,0:T(8,128)(2,1)S(1)} %get-tuple-element.74.columns_ref, bf16[384,768]{1,0:T(8,128)(2,1)S(1)} %get-tuple-element.66.refs_0_, bf16[384,768]{1,0:T(8,128)(2,1)S(1)} %get-tuple-element.77.refs_1_, bf16[256,768]{1,0:T(8,128)(2,1)S(1)} %collective-permute-done.12.refs_2_, ...), custom_call_target="tpu_custom_call" | custom-call | flops 1000 | bytes 1000 | tf_op jit(solution)/shard_map/feed_side/pallas_call | solution.py:221
  56.0 16.9 %all_to_all.10 = bf16[16,16,896]{2,1,0:T(8,128)(2,1)S(1)} all-to-all(bf16[16,16,896]{2,1,0:T(8,128)(2,1)S(1)} %bitcast.11), channel_id=1, replica_groups=mesh['groups'=2,'wide'=16] {'wide'}, dimensions={0} | all-to-all | bytes 917504 | tf_op jit(solution)/shard_map/all_to_all | solution.py:419
  72.9 1.3 %codes.1 = bf16[256,256]{1,0:T(8,128)(2,1)S(1)} custom-call(bf16[256,896]{1,0:T(8,128)(2,1)S(1)} %bitcast.9, bf16[8,768]{1,0:T(8,128)(2,1)S(1)} %copy-done.6, bf16[8,256,768]{2,1,0:T(8,128)(2,1)S(1)} %copy-done.2), custom_call_target="tpu_custom_call" | custom-call | tf_op jit(solution)/shard_map/codes/pallas_call | solution.py:420
  74.2 11.6 %all_to_all.11 = bf16[16,16,256]{2,1,0:T(8,128)(2,1)S(1)} all-to-all(bf16[16,16,256]{2,1,0:T(8,128)(2,1)S(1)} %bitcast.10), channel_id=1, replica_groups=mesh['groups'=2,'wide'=16] {'wide'}, dimensions={0} | all-to-all | bytes 262144 | tf_op jit(solution)/shard_map/all_to_all | solution.py:427
  (55 shorter events, 6.5 us)
Async XLA Ops:
  1.7 12.1 %collective-permute-start = (bf16[256,768]{1,0:T(8,128)(2,1)S(1)}, bf16[256,768]{1,0:T(8,128)(2,1)S(1)}, u32[]{:S(2)}, u32[]{:S(2)}) collective-permute-start(bf16[256,768]{1,0:T(8,128)(2,1)S(1)} %hold.1), channel_id=1, source_target_pairs={{0,2},{1,3},{2,0},{3,1},{4,6},{5,7},{6,4},{7,5},{8,10},{9,11},{10,... | collective-permute-start | bytes 1179656 | tf_op jit(solution)/shard_map/ppermute | solution.py:296
  4.7 10.6 %collective-permute-start.1 = (bf16[256,768]{1,0:T(8,128)(2,1)S(1)}, bf16[256,768]{1,0:T(8,128)(2,1)S(1)}, u32[]{:S(2)}, u32[]{:S(2)}) collective-permute-start(bf16[256,768]{1,0:T(8,128)(2,1)S(1)} %hold.1), channel_id=1, source_target_pairs={{0,4},{1,5},{2,6},{3,7},{4,0},{5,1},{6,2},{7,3},{8,12},{9,13},{10,... | collective-permute-start | bytes 1179656 | tf_op jit(solution)/shard_map/ppermute | solution.py:296
  6.3 9.0 %collective-permute-start.2 = (bf16[256,768]{1,0:T(8,128)(2,1)S(1)}, bf16[256,768]{1,0:T(8,128)(2,1)S(1)}, u32[]{:S(2)}, u32[]{:S(2)}) collective-permute-start(bf16[256,768]{1,0:T(8,128)(2,1)S(1)} %hold.1), channel_id=1, source_target_pairs={{0,1},{1,0},{2,3},{3,2},{4,8},{5,9},{6,10},{7,11},{8,4},{9,5},{10,... | collective-permute-start | bytes 1179656 | tf_op jit(solution)/shard_map/ppermute | solution.py:321
  6.3 1.6 %collective-permute-start.3 = (s32[2,64]{1,0:T(2,128)}, s32[2,64]{1,0:T(2,128)S(1)}, u32[]{:S(2)}, u32[]{:S(2)}) collective-permute-start(s32[2,64]{1,0:T(2,128)} %lengths_hbm.1), channel_id=1, source_target_pairs={{0,1},{1,0},{2,3},{3,2},{4,5},{5,4},{6,7},{7,6},{8,9},{9,8},{10,11... | collective-permute-start | bytes 1544 | tf_op jit(solution)/shard_map/ppermute | solution.py:296
  15.3 6.3 %copy-start = (bf16[2,384,768]{2,1,0:T(8,128)(2,1)S(1)}, bf16[2,384,768]{2,1,0:T(8,128)(2,1)}, u32[]{:S(2)}) copy-start(bf16[2,384,768]{2,1,0:T(8,128)(2,1)} %x_ref.3) | copy-start | bytes 3538948
  15.3 6.3 %copy-start.1 = (bf16[768,768]{1,0:T(8,128)(2,1)S(1)}, bf16[768,768]{1,0:T(8,128)(2,1)}, u32[]{:S(2)}) copy-start(bf16[768,768]{1,0:T(8,128)(2,1)} %wo_ref.3) | copy-start | bytes 3538948
  15.3 6.3 %copy-start.5 = (f32[768]{0:T(1024)S(1)}, f32[768]{0:T(1024)}, u32[]{:S(2)}) copy-start(f32[768]{0:T(1024)} %gain_ref.4) | copy-start | bytes 9220
  15.4 11.0 %collective-permute-start.6 = (bf16[256,768]{1,0:T(8,128)(2,1)S(1)}, bf16[256,768]{1,0:T(8,128)(2,1)S(1)}, u32[]{:S(2)}, u32[]{:S(2)}) collective-permute-start(bf16[256,768]{1,0:T(8,128)(2,1)S(1)} %broadcast_select_fusion.1), channel_id=1, source_target_pairs={{4,0},{5,1},{6,2},{7,3},{0,8},{1,9},{2,10},{3,11},{8,12},{9,13},{1... | collective-permute-start | bytes 1179656 | tf_op jit(solution)/shard_map/ppermute | solution.py:317
  19.6 9.2 %collective-permute-start.5 = (bf16[256,768]{1,0:T(8,128)(2,1)S(1)}, bf16[256,768]{1,0:T(8,128)(2,1)S(1)}, u32[]{:S(2)}, u32[]{:S(2)}) collective-permute-start(bf16[256,768]{1,0:T(8,128)(2,1)S(1)} %pad_maximum_fusion), channel_id=1, source_target_pairs={{0,16},{16,0},{1,17},{17,1},{2,18},{18,2},{3,19},{19,3},{4,20},{20... | collective-permute-start | bytes 1179656 | tf_op jit(solution)/shard_map/ppermute | solution.py:296
  21.1 8.9 %collective-permute-start.4 = (bf16[256,768]{1,0:T(8,128)(2,1)S(1)}, bf16[256,768]{1,0:T(8,128)(2,1)S(1)}, u32[]{:S(2)}, u32[]{:S(2)}) collective-permute-start(bf16[256,768]{1,0:T(8,128)(2,1)S(1)} %collective-permute-done.1.refs_8_), channel_id=1, source_target_pairs={{0,2},{1,3},{2,0},{3,1},{4,6},{5,7},{6,4},{7,5},{8,10},{9,11},{10,... | collective-permute-start | bytes 1179656 | tf_op jit(solution)/shard_map/ppermute | solution.py:296
  30.1 7.9 %collective-permute-start.8 = (bf16[256,768]{1,0:T(8,128)(2,1)S(1)}, bf16[256,768]{1,0:T(8,128)(2,1)S(1)}, u32[]{:S(2)}, u32[]{:S(2)}) collective-permute-start(bf16[256,768]{1,0:T(8,128)(2,1)S(1)} %pad_maximum_fusion.1), channel_id=1, source_target_pairs={{0,16},{16,0},{1,17},{17,1},{2,18},{18,2},{3,19},{19,3},{4,20},{20... | collective-permute-start | bytes 1179656 | tf_op jit(solution)/shard_map/ppermute | solution.py:296
  30.6 7.8 %collective-permute-start.7 = (bf16[256,768]{1,0:T(8,128)(2,1)S(1)}, bf16[256,768]{1,0:T(8,128)(2,1)S(1)}, u32[]{:S(2)}, u32[]{:S(2)}) collective-permute-start(bf16[256,768]{1,0:T(8,128)(2,1)S(1)} %collective-permute-done.6.refs_4_), channel_id=1, source_target_pairs={{0,2},{1,3},{2,0},{3,1},{4,6},{5,7},{6,4},{7,5},{8,10},{9,11},{10,... | collective-permute-start | bytes 1179656 | tf_op jit(solution)/shard_map/ppermute | solution.py:296
  31.1 7.8 %collective-permute-start.9 = (bf16[256,768]{1,0:T(8,128)(2,1)S(1)}, bf16[256,768]{1,0:T(8,128)(2,1)S(1)}, u32[]{:S(2)}, u32[]{:S(2)}) collective-permute-start(bf16[256,768]{1,0:T(8,128)(2,1)S(1)} %collective-permute-done.6.refs_4_), channel_id=1, source_target_pairs={{0,4},{1,5},{2,6},{3,7},{4,0},{5,1},{6,2},{7,3},{8,12},{9,13},{10,... | collective-permute-start | bytes 1179656 | tf_op jit(solution)/shard_map/ppermute | solution.py:296
  31.1 5.3 %collective-permute-start.10 = (bf16[128,768]{1,0:T(8,128)(2,1)S(1)}, bf16[128,768]{1,0:T(8,128)(2,1)S(1)}, u32[]{:S(2)}, u32[]{:S(2)}) collective-permute-start(bf16[128,768]{1,0:T(8,128)(2,1)S(1)} %slice.28), channel_id=1, source_target_pairs={{0,1},{1,0},{2,3},{3,2},{4,8},{5,9},{6,10},{7,11},{8,4},{9,5},{10,... | collective-permute-start | bytes 589832 | tf_op jit(solution)/shard_map/ppermute | solution.py:321
  31.2 12.5 %collective-permute-start.14 = (bf16[384,768]{1,0:T(8,128)(2,1)S(1)}, bf16[384,768]{1,0:T(8,128)(2,1)S(1)}, u32[]{:S(2)}, u32[]{:S(2)}) collective-permute-start(bf16[384,768]{1,0:T(8,128)(2,1)S(1)} %get-tuple-element.66.refs_0_), channel_id=1, source_target_pairs={{0,1},{1,0},{2,3},{3,2},{4,5},{5,4},{6,7},{7,6},{8,9},{9,8},{10,11... | collective-permute-start | bytes 1769480 | tf_op jit(solution)/shard_map/ppermute | solution.py:296
  38.9 4.8 %collective-permute-start.15 = (bf16[384,768]{1,0:T(8,128)(2,1)S(1)}, bf16[384,768]{1,0:T(8,128)(2,1)S(1)}, u32[]{:S(2)}, u32[]{:S(2)}) collective-permute-start(bf16[384,768]{1,0:T(8,128)(2,1)S(1)} %get-tuple-element.77.refs_1_), channel_id=1, source_target_pairs={{0,1},{1,0},{2,3},{3,2},{4,5},{5,4},{6,7},{7,6},{8,9},{9,8},{10,11... | collective-permute-start | bytes 1769480 | tf_op jit(solution)/shard_map/ppermute | solution.py:296
  38.9 4.8 %copy-start.3 = (bf16[192,768]{1,0:T(8,128)(2,1)S(1)}, bf16[192,768]{1,0:T(8,128)(2,1)}, u32[]{:S(2)}) copy-start(bf16[192,768]{1,0:T(8,128)(2,1)} %refs_4_.1) | copy-start | bytes 884740
  39.0 4.8 %copy-start.4 = (bf16[192,768]{1,0:T(8,128)(2,1)S(1)}, bf16[192,768]{1,0:T(8,128)(2,1)}, u32[]{:S(2)}) copy-start(bf16[192,768]{1,0:T(8,128)(2,1)} %refs_5_.1) | copy-start | bytes 884740
  39.1 12.7 %collective-permute-start.12 = (bf16[256,768]{1,0:T(8,128)(2,1)S(1)}, bf16[256,768]{1,0:T(8,128)(2,1)S(1)}, u32[]{:S(2)}, u32[]{:S(2)}) collective-permute-start(bf16[256,768]{1,0:T(8,128)(2,1)S(1)} %pad_maximum_fusion.2), channel_id=1, source_target_pairs={{0,16},{16,0},{1,17},{17,1},{2,18},{18,2},{3,19},{19,3},{4,20},{20... | collective-permute-start | bytes 1179656 | tf_op jit(solution)/shard_map/ppermute | solution.py:296
  40.7 11.2 %collective-permute-start.11 = (bf16[256,768]{1,0:T(8,128)(2,1)S(1)}, bf16[256,768]{1,0:T(8,128)(2,1)S(1)}, u32[]{:S(2)}, u32[]{:S(2)}) collective-permute-start(bf16[256,768]{1,0:T(8,128)(2,1)S(1)} %broadcast_select_fusion.refs_7_), channel_id=1, source_target_pairs={{0,2},{1,3},{2,0},{3,1},{4,6},{5,7},{6,4},{7,5},{8,10},{9,11},{10,... | collective-permute-start | bytes 1179656 | tf_op jit(solution)/shard_map/ppermute | solution.py:296
  42.2 9.5 %collective-permute-start.13 = (bf16[128,768]{1,0:T(8,128)(2,1)S(1)}, bf16[128,768]{1,0:T(8,128)(2,1)S(1)}, u32[]{:S(2)}, u32[]{:S(2)}) collective-permute-start(bf16[128,768]{1,0:T(8,128)(2,1)S(1)} %slice.31), channel_id=1, source_target_pairs={{8,0},{9,1},{10,2},{11,3},{4,12},{5,13},{6,14},{7,15},{24,16},{25,... | collective-permute-start | bytes 589832 | tf_op jit(solution)/shard_map/ppermute | solution.py:317
  53.3 1.8 %collective-permute-start.16 = (f32[128,768]{1,0:T(8,128)S(1)}, f32[128,768]{1,0:T(8,128)S(1)}, u32[]{:S(2)}, u32[]{:S(2)}) collective-permute-start(f32[128,768]{1,0:T(8,128)S(1)} %feed_side.3), channel_id=1, source_target_pairs={{0,1},{1,0},{2,3},{3,2},{4,5},{5,4},{6,7},{7,6},{8,9},{9,8},{10,11... | collective-permute-start | bytes 1179656 | tf_op jit(solution)/shard_map/ppermute | solution.py:296
  53.4 19.5 %copy-start.2 = (bf16[8,256,768]{2,1,0:T(8,128)(2,1)S(1)}, bf16[8,256,768]{2,1,0:T(8,128)(2,1)}, u32[]{:S(2)}) copy-start(bf16[8,256,768]{2,1,0:T(8,128)(2,1)} %books_ref.1) | copy-start | bytes 9437188
  54.8 18.0 %copy-start.6 = (bf16[8,768]{1,0:T(8,128)(2,1)S(1)}, bf16[8,768]{1,0:T(8,128)(2,1)}, u32[]{:S(2)}) copy-start(bf16[8,768]{1,0:T(8,128)(2,1)} %coarse_ref.1) | copy-start | bytes 36868
  (2 other events, 3.6 us)

commit v6 on v5

--- a/solution.py
+++ b/solution.py
@@ -19,7 +19,7 @@
 
 
 def cost():
-    return pl.CostEstimate(flops=1000, bytes_accessed=1000, transcendentals=0)
+    return pl.CostEstimate(flops=2000000000, bytes_accessed=5000000, transcendentals=0)
 
 
 def dot(a, b):
@@ -335,7 +335,7 @@
         return jnp.concatenate([a, b], axis=0)
 
     held = hold(w_input, w_down, common)
-    side0, near1, middle = side(held), near(held), amid(held)
+    middle, near1, side0 = amid(held), near(held), side(held)
     projected = encode_first(tokens)
     side0, near1, middle, projected = after((side0, near1, middle, projected))
     columns = projected[4]
@@ -344,9 +344,10 @@
     far2 = along(jnp.where(inner, middle, held), [(1, 0), (0, 2), (2, 3), (3, 1)])
     x0 = twin(cat(side0[split:], near1[split:]))
     first = encode(0, projected, tokens)
-    side1, x0, far2, first, projected = after((side1, x0, far2, first, projected))
+    side1, far2, first, projected = after((side1, far2, first, projected))
 
     side2, outer = side(far2), near(far2)
+    x0, projected = after((x0, projected))
     x1 = twin(cat(side1[split:], far2[split:]))
     last_inner = amid(x0[:both])
     second = encode(1, projected, tokens)
@@ -354,7 +355,7 @@
 
     far3 = jnp.where(inner, middle, outer)
     side3, x2 = side(far3), twin(cat(side2[split:], far3[split:]))
-    last_outer = along(x1[:both], [(2, 0), (1, 3)])
+    last_outer = along(x1[:both], [(2, 0), (0, 1), (1, 3), (3, 2)])
     normed = ((first[0], second[0]), (sibling(first[0]), sibling(second[0])))
     own = [(0, slice(0, rows), 1, slice(0, rows))]
     pieces = own + blocks(2) + rest(3) + blocks(4) + rest(3, both) + blocks(5) + rest(6)

time: 86.9 us -> 85.6 us (0.985)
  waiting for transfers between devices: 10.9 us -> 9.75 us
    ppermute x2, waiting for transfers between devices: 1.66 us -> 0.59 us  [along(): return lax.ppermute(value, 'wide', pairs)]
  transfers between devices with their start and end apart: 17 -> 17, of which waited for: 11 -> 11; matrix products, arithmetic and copies ran while one was open for 0% -> 0% of each run, Pallas kernels for 26% -> 27%
where the time goes in v6:
time: 85.6 us; the launch traced here: 85.4 us
  blocking collectives  28.6 us (33%)
  Pallas kernels  27.5 us (32%)
  starting transfers between devices  17.4 us (20%)
  waiting for transfers between devices  9.75 us (11%)
  between operations  0.91 us (1%)
  matrix products  0.87 us (1%)
    all_to_all x1, blocking collectives, local(): rows = lax.all_to_all(send, 'wide', split_axis=0, concat_axis=0, tiled=True)  17 us
    ppermute x13, starting transfers between devices, flip(): return lambda value: lax.ppermute(value, axis_name, pairs)  12.2 us
    all_to_all x1, blocking collectives, local(): lax.all_to_all(codes, 'wide', split_axis=0, concat_axis=0, tiled=True)  11.6 us
    pallas_call x2, Pallas kernels, attend(): pl.pallas_call(functools.partial(attend_kernel, pack), out_shape=(jax.Sha...  9.51 us
    ppermute x13, waiting for transfers between devices, flip(): return lambda value: lax.ppermute(value, axis_name, pairs)  9.15 us
    pallas_call x2, Pallas kernels, feed(): pl.pallas_call(functools.partial(feed_kernel, len(normed[0]), len(held),...  6.33 us
    pallas_call x1, Pallas kernels, project(): pl.pallas_call(functools.partial(project_kernel, wide=wide, capacity=capa...  5.68 us
    ppermute x2, starting transfers between devices, along(): return lax.ppermute(value, 'wide', pairs)  5.08 us
  transfers between devices with their start and end apart: 17, of which 11 were waited for; matrix products, arithmetic and copies ran while one was open for 0% of the time, Pallas kernels for 27%

profile of v6, /device:TPU:0, one launch (start us, length us, event | category | flops | bytes accessed | tf_op | source)
XLA Modules:
  0.0 85.4 jit_solution(12157483739889064773)
XLA Ops:
  0.6 1.1 %hold.1 = bf16[256,768]{1,0:T(8,128)(2,1)S(1)} custom-call(s32[1,1]{1,0:T(1,128)} %bitcast.group_ref, bf16[192,768]{1,0:T(8,128)(2,1)} %refs_4_.1, bf16[192,768]{1,0:T(8,128)(2,1)} %refs_5_.1), custom_call_target="tpu_custom_call" | custom-call | flops 2000000000 | bytes 5000000 | tf_op jit(solution)/shard_map/hold/pallas_call | solution.py:143
  1.7 3.0 %collective-permute-start = (bf16[256,768]{1,0:T(8,128)(2,1)S(1)}, bf16[256,768]{1,0:T(8,128)(2,1)S(1)}, u32[]{:S(2)}, u32[]{:S(2)}) collective-permute-start(bf16[256,768]{1,0:T(8,128)(2,1)S(1)} %hold.1), channel_id=1, source_target_pairs={{0,2},{1,3},{2,0},{3,1},{4,6},{5,7},{6,4},{7,5},{8,10},{9,11},{10,... | collective-permute-start | bytes 1179656 | tf_op jit(solution)/shard_map/ppermute | solution.py:296
  4.8 1.6 %collective-permute-start.1 = (bf16[256,768]{1,0:T(8,128)(2,1)S(1)}, bf16[256,768]{1,0:T(8,128)(2,1)S(1)}, u32[]{:S(2)}, u32[]{:S(2)}) collective-permute-start(bf16[256,768]{1,0:T(8,128)(2,1)S(1)} %hold.1), channel_id=1, source_target_pairs={{0,4},{1,5},{2,6},{3,7},{4,0},{5,1},{6,2},{7,3},{8,12},{9,13},{10,... | collective-permute-start | bytes 1179656 | tf_op jit(solution)/shard_map/ppermute | solution.py:296
  6.9 1.2 %collective-permute-done.3.other_ref = s32[2,64]{1,0:T(2,128)S(1)} collective-permute-done((s32[2,64]{1,0:T(2,128)S(1)}, s32[2,64]{1,0:T(2,128)S(1)}, u32[]{:S(2)}, u32[]{:S(2)}) %collective-permute-start.3) | collective-permute-done | bytes 544 | tf_op jit(solution)/shard_map/ppermute | solution.py:296
  8.1 5.7 %project.1 = (bf16[768,768]{1,0:T(8,128)(2,1)S(1)}, bf16[768,768]{1,0:T(8,128)(2,1)S(1)}, bf16[768,768]{1,0:T(8,128)(2,1)S(1)}, bf16[768,64]{1,0:T(8,128)(2,1)S(...) custom-call(s32[2,64]{1,0:T(2,128)S(1)} %collective-permute-done.3.other_ref, s32[2,64]{1,0:T(2,128)} %lengths_hbm.1, ...), custom_call_target="tpu_custom_call" | custom-call | flops 2000000000 | bytes 5000000 | tf_op jit(solution)/shard_map/project/pallas_call | solution.py:105
  13.9 1.5 %collective-permute-done.1.refs_8_ = bf16[256,768]{1,0:T(8,128)(2,1)S(1)} collective-permute-done((bf16[256,768]{1,0:T(8,128)(2,1)S(1)}, bf16[256,768]{1,0:T(8,128)(2,1)S(1)}, u32[]{:S(2)}, u32[]{:S(2)}) %collective-permute-start.1) | collective-permute-done | bytes 393248 | tf_op jit(solution)/shard_map/ppermute | solution.py:296
  15.4 4.1 %collective-permute-start.5 = (bf16[256,768]{1,0:T(8,128)(2,1)S(1)}, bf16[256,768]{1,0:T(8,128)(2,1)S(1)}, u32[]{:S(2)}, u32[]{:S(2)}) collective-permute-start(bf16[256,768]{1,0:T(8,128)(2,1)S(1)} %broadcast_select_fusion.1), channel_id=1, source_target_pairs={{4,0},{5,1},{6,2},{7,3},{0,8},{1,9},{2,10},{3,11},{8,12},{9,13},{1... | collective-permute-start | bytes 1179656 | tf_op jit(solution)/shard_map/ppermute | solution.py:317
  20.1 1.6 %collective-permute-start.9 = (bf16[256,768]{1,0:T(8,128)(2,1)S(1)}, bf16[256,768]{1,0:T(8,128)(2,1)S(1)}, u32[]{:S(2)}, u32[]{:S(2)}) collective-permute-start(bf16[256,768]{1,0:T(8,128)(2,1)S(1)} %pad_maximum_fusion.1), channel_id=1, source_target_pairs={{0,16},{16,0},{1,17},{17,1},{2,18},{18,2},{3,19},{19,3},{4,20},{20... | collective-permute-start | bytes 1179656 | tf_op jit(solution)/shard_map/ppermute | solution.py:296
  21.7 4.8 %attend.2 = (bf16[384,768]{1,0:T(8,128)(2,1)S(1)}, f32[64,768]{1,0:T(8,128)S(1)}) custom-call(bf16[768,768]{1,0:T(8,128)(2,1)S(1)} %get-tuple-element.82.q_ref, bf16[768,768]{1,0:T(8,128)(2,1)S(1)} %get-tuple-element.83.k_ref, bf16[768,768]{1,0:T(8,128)(2,1)S(1)} %get-tuple-element.84.v_ref, bf16[768,64]{1,0:T(8,128)(2,1)S(1)} %get-tuple-element.85.rows_ref, ...), custom_call_target="tpu_custom_call" | custom-call | flops 2000000000 | bytes 5000000 | tf_op jit(solution)/shard_map/attend/pallas_call | solution.py:193
  26.4 2.2 %collective-permute-done.4.refs_9_ = bf16[256,768]{1,0:T(8,128)(2,1)S(1)} collective-permute-done((bf16[256,768]{1,0:T(8,128)(2,1)S(1)}, bf16[256,768]{1,0:T(8,128)(2,1)S(1)}, u32[]{:S(2)}, u32[]{:S(2)}) %collective-permute-start.4) | collective-permute-done | bytes 393248 | tf_op jit(solution)/shard_map/ppermute | solution.py:296
  28.7 1.6 %collective-permute-start.7 = (bf16[256,768]{1,0:T(8,128)(2,1)S(1)}, bf16[256,768]{1,0:T(8,128)(2,1)S(1)}, u32[]{:S(2)}, u32[]{:S(2)}) collective-permute-start(bf16[256,768]{1,0:T(8,128)(2,1)S(1)} %pad_maximum_fusion), channel_id=1, source_target_pairs={{0,16},{16,0},{1,17},{17,1},{2,18},{18,2},{3,19},{19,3},{4,20},{20... | collective-permute-start | bytes 1179656 | tf_op jit(solution)/shard_map/ppermute | solution.py:296
  31.6 4.8 %attend.3 = (bf16[384,768]{1,0:T(8,128)(2,1)S(1)}, f32[64,768]{1,0:T(8,128)S(1)}) custom-call(bf16[768,768]{1,0:T(8,128)(2,1)S(1)} %get-tuple-element.82.q_ref, bf16[768,768]{1,0:T(8,128)(2,1)S(1)} %get-tuple-element.83.k_ref, bf16[768,768]{1,0:T(8,128)(2,1)S(1)} %get-tuple-element.84.v_ref, bf16[768,64]{1,0:T(8,128)(2,1)S(1)} %get-tuple-element.85.rows_ref, ...), custom_call_target="tpu_custom_call" | custom-call | flops 2000000000 | bytes 5000000 | tf_op jit(solution)/shard_map/attend/pallas_call | solution.py:193
  36.4 1.0 %collective-permute-done.7.refs_10_.refs_5_ = bf16[256,768]{1,0:T(8,128)(2,1)S(1)} collective-permute-done((bf16[256,768]{1,0:T(8,128)(2,1)S(1)}, bf16[256,768]{1,0:T(8,128)(2,1)S(1)}, u32[]{:S(2)}, u32[]{:S(2)}) %collective-permute-start.7) | collective-permute-done | bytes 393248 | tf_op jit(solution)/shard_map/ppermute | solution.py:296
  39.3 1.5 %collective-permute-start.11 = (bf16[256,768]{1,0:T(8,128)(2,1)S(1)}, bf16[256,768]{1,0:T(8,128)(2,1)S(1)}, u32[]{:S(2)}, u32[]{:S(2)}) collective-permute-start(bf16[256,768]{1,0:T(8,128)(2,1)S(1)} %broadcast_select_fusion.refs_7_), channel_id=1, source_target_pairs={{0,2},{1,3},{2,0},{3,1},{4,6},{5,7},{6,4},{7,5},{8,10},{9,11},{10,... | collective-permute-start | bytes 1179656 | tf_op jit(solution)/shard_map/ppermute | solution.py:296
  40.8 1.0 %collective-permute-start.13 = (bf16[128,768]{1,0:T(8,128)(2,1)S(1)}, bf16[128,768]{1,0:T(8,128)(2,1)S(1)}, u32[]{:S(2)}, u32[]{:S(2)}) collective-permute-start(bf16[128,768]{1,0:T(8,128)(2,1)S(1)} %slice.31), channel_id=1, source_target_pairs={{8,0},{9,1},{10,2},{11,3},{0,4},{1,5},{2,6},{3,7},{4,12},{5,13},{6... | collective-permute-start | bytes 589832 | tf_op jit(solution)/shard_map/ppermute | solution.py:317
  41.8 3.8 %feed.2 = (f32[128,768]{1,0:T(8,128)S(1)}, f32[128,768]{1,0:T(8,128)S(1)}) custom-call(bf16[256,384]{1,0:T(8,128)(2,1)S(1)} %get-tuple-element.86.columns_ref, bf16[384,768]{1,0:T(8,128)(2,1)S(1)} %get-tuple-element.71.refs_0_, bf16[384,768]{1,0:T(8,128)(2,1)S(1)} %get-tuple-element.89.refs_1_, bf16[384,768]{1,0:T(8,128)(2,1)S(1)} %collective-permute-done.14.refs_2_.refs_0_, ...), custom_call_target="tpu_custom_call" | custom-call | flops 2000000000 | bytes 5000000 | tf_op jit(solution)/shard_map/feed/pallas_call | solution.py:254
  45.6 2.5 %feed.3 = (f32[128,768]{1,0:T(8,128)S(1)}, f32[128,768]{1,0:T(8,128)S(1)}) custom-call(bf16[256,384]{1,0:T(8,128)(2,1)S(1)} %get-tuple-element.86.columns_ref, bf16[384,768]{1,0:T(8,128)(2,1)S(1)} %get-tuple-element.71.refs_0_, bf16[384,768]{1,0:T(8,128)(2,1)S(1)} %get-tuple-element.89.refs_1_, bf16[384,768]{1,0:T(8,128)(2,1)S(1)} %collective-permute-done.14.refs_2_.refs_0_, ...), custom_call_target="tpu_custom_call" | custom-call | flops 2000000000 | bytes 5000000 | tf_op jit(solution)/shard_map/feed/pallas_call | solution.py:254
  48.7 1.5 %collective-permute-done.12.refs_2_ = bf16[256,768]{1,0:T(8,128)(2,1)S(1)} collective-permute-done((bf16[256,768]{1,0:T(8,128)(2,1)S(1)}, bf16[256,768]{1,0:T(8,128)(2,1)S(1)}, u32[]{:S(2)}, u32[]{:S(2)}) %collective-permute-start.12) | collective-permute-done | bytes 393248 | tf_op jit(solution)/shard_map/ppermute | solution.py:296
  50.5 1.4 %feed_side.3 = f32[128,768]{1,0:T(8,128)S(1)} custom-call(bf16[256,384]{1,0:T(8,128)(2,1)S(1)} %get-tuple-element.86.columns_ref, bf16[384,768]{1,0:T(8,128)(2,1)S(1)} %collective-permute-done.14.refs_2_.refs_0_, bf16[384,768]{1,0:T(8,128)(2,1)S(1)} %collective-permute-done.15.refs_3_.refs_1_, bf16[256,768]{1,0:T(8,128)(2,1)S(1)} %collective-permute-done.12.refs_2_, ...), custom_call_target="tpu_custom_call" | custom-call | flops 2000000000 | bytes 5000000 | tf_op jit(solution)/shard_map/feed_side/pallas_call | solution.py:221
  52.1 1.4 %feed_side.2.acc_ref = f32[128,768]{1,0:T(8,128)S(1)} custom-call(bf16[256,384]{1,0:T(8,128)(2,1)S(1)} %get-tuple-element.86.columns_ref, bf16[384,768]{1,0:T(8,128)(2,1)S(1)} %get-tuple-element.71.refs_0_, bf16[384,768]{1,0:T(8,128)(2,1)S(1)} %get-tuple-element.89.refs_1_, bf16[256,768]{1,0:T(8,128)(2,1)S(1)} %collective-permute-done.12.refs_2_, ...), custom_call_target="tpu_custom_call" | custom-call | flops 2000000000 | bytes 5000000 | tf_op jit(solution)/shard_map/feed_side/pallas_call | solution.py:221
  54.6 17.0 %all_to_all.10 = bf16[16,16,896]{2,1,0:T(8,128)(2,1)S(1)} all-to-all(bf16[16,16,896]{2,1,0:T(8,128)(2,1)S(1)} %bitcast.11), channel_id=1, replica_groups=mesh['groups'=2,'wide'=16] {'wide'}, dimensions={0} | all-to-all | bytes 917504 | tf_op jit(solution)/shard_map/all_to_all | solution.py:420
  71.6 1.3 %codes.1 = bf16[256,256]{1,0:T(8,128)(2,1)S(1)} custom-call(bf16[256,896]{1,0:T(8,128)(2,1)S(1)} %bitcast.9, bf16[8,768]{1,0:T(8,128)(2,1)S(1)} %copy-done.1, bf16[8,256,768]{2,1,0:T(8,128)(2,1)S(1)} %copy-done), custom_call_target="tpu_custom_call" | custom-call | tf_op jit(solution)/shard_map/codes/pallas_call | solution.py:421
  72.9 11.6 %all_to_all.11 = bf16[16,16,256]{2,1,0:T(8,128)(2,1)S(1)} all-to-all(bf16[16,16,256]{2,1,0:T(8,128)(2,1)S(1)} %bitcast.10), channel_id=1, replica_groups=mesh['groups'=2,'wide'=16] {'wide'}, dimensions={0} | all-to-all | bytes 262144 | tf_op jit(solution)/shard_map/all_to_all | solution.py:428
  84.5 0.9 %fusion = f32[128,256]{1,0:T(8,128)} fusion(bf16[256,256]{1,0:T(8,128)(2,1)S(1)} %bitcast.14, s32[128]{0:T(128)S(1)} %bitcast.12), kind=kOutput, calls=%fused_computation.7 | convolution fusion | flops 16809984 | bytes 262656 | tf_op jit(solution)/shard_map/dot_general | solution.py:430
  (57 shorter events, 6.6 us)
Async XLA Ops:
  0.6 5.7 %copy-start.9 = (s32[2,64]{1,0:T(2,128)S(1)}, s32[2,64]{1,0:T(2,128)}, u32[]{:S(2)}) copy-start(s32[2,64]{1,0:T(2,128)} %lengths_hbm.1) | copy-start | bytes 1540
  1.7 12.1 %collective-permute-start = (bf16[256,768]{1,0:T(8,128)(2,1)S(1)}, bf16[256,768]{1,0:T(8,128)(2,1)S(1)}, u32[]{:S(2)}, u32[]{:S(2)}) collective-permute-start(bf16[256,768]{1,0:T(8,128)(2,1)S(1)} %hold.1), channel_id=1, source_target_pairs={{0,2},{1,3},{2,0},{3,1},{4,6},{5,7},{6,4},{7,5},{8,10},{9,11},{10,... | collective-permute-start | bytes 1179656 | tf_op jit(solution)/shard_map/ppermute | solution.py:296
  4.8 10.6 %collective-permute-start.1 = (bf16[256,768]{1,0:T(8,128)(2,1)S(1)}, bf16[256,768]{1,0:T(8,128)(2,1)S(1)}, u32[]{:S(2)}, u32[]{:S(2)}) collective-permute-start(bf16[256,768]{1,0:T(8,128)(2,1)S(1)} %hold.1), channel_id=1, source_target_pairs={{0,4},{1,5},{2,6},{3,7},{4,0},{5,1},{6,2},{7,3},{8,12},{9,13},{10,... | collective-permute-start | bytes 1179656 | tf_op jit(solution)/shard_map/ppermute | solution.py:296
  6.3 9.0 %collective-permute-start.2 = (bf16[256,768]{1,0:T(8,128)(2,1)S(1)}, bf16[256,768]{1,0:T(8,128)(2,1)S(1)}, u32[]{:S(2)}, u32[]{:S(2)}) collective-permute-start(bf16[256,768]{1,0:T(8,128)(2,1)S(1)} %hold.1), channel_id=1, source_target_pairs={{0,1},{1,0},{2,3},{3,2},{4,8},{5,9},{6,10},{7,11},{8,4},{9,5},{10,... | collective-permute-start | bytes 1179656 | tf_op jit(solution)/shard_map/ppermute | solution.py:321
  6.3 1.7 %collective-permute-start.3 = (s32[2,64]{1,0:T(2,128)S(1)}, s32[2,64]{1,0:T(2,128)S(1)}, u32[]{:S(2)}, u32[]{:S(2)}) collective-permute-start(s32[2,64]{1,0:T(2,128)S(1)} %copy-done.9), channel_id=1, source_target_pairs={{0,1},{1,0},{2,3},{3,2},{4,5},{5,4},{6,7},{7,6},{8,9},{9,8},{10,11... | collective-permute-start | bytes 1544 | tf_op jit(solution)/shard_map/ppermute | solution.py:296
  15.3 6.3 %copy-start.4 = (bf16[2,384,768]{2,1,0:T(8,128)(2,1)S(1)}, bf16[2,384,768]{2,1,0:T(8,128)(2,1)}, u32[]{:S(2)}) copy-start(bf16[2,384,768]{2,1,0:T(8,128)(2,1)} %x_ref.3) | copy-start | bytes 3538948
  15.3 6.3 %copy-start.5 = (bf16[768,768]{1,0:T(8,128)(2,1)S(1)}, bf16[768,768]{1,0:T(8,128)(2,1)}, u32[]{:S(2)}) copy-start(bf16[768,768]{1,0:T(8,128)(2,1)} %wo_ref.3) | copy-start | bytes 3538948
  15.3 6.3 %copy-start.8 = (f32[768]{0:T(1024)S(1)}, f32[768]{0:T(1024)}, u32[]{:S(2)}) copy-start(f32[768]{0:T(1024)} %gain_ref.4) | copy-start | bytes 9220
  15.4 11.0 %collective-permute-start.5 = (bf16[256,768]{1,0:T(8,128)(2,1)S(1)}, bf16[256,768]{1,0:T(8,128)(2,1)S(1)}, u32[]{:S(2)}, u32[]{:S(2)}) collective-permute-start(bf16[256,768]{1,0:T(8,128)(2,1)S(1)} %broadcast_select_fusion.1), channel_id=1, source_target_pairs={{4,0},{5,1},{6,2},{7,3},{0,8},{1,9},{2,10},{3,11},{8,12},{9,13},{1... | collective-permute-start | bytes 1179656 | tf_op jit(solution)/shard_map/ppermute | solution.py:317
  19.5 9.1 %collective-permute-start.4 = (bf16[256,768]{1,0:T(8,128)(2,1)S(1)}, bf16[256,768]{1,0:T(8,128)(2,1)S(1)}, u32[]{:S(2)}, u32[]{:S(2)}) collective-permute-start(bf16[256,768]{1,0:T(8,128)(2,1)S(1)} %collective-permute-done.1.refs_8_), channel_id=1, source_target_pairs={{0,2},{1,3},{2,0},{3,1},{4,6},{5,7},{6,4},{7,5},{8,10},{9,11},{10,... | collective-permute-start | bytes 1179656 | tf_op jit(solution)/shard_map/ppermute | solution.py:296
  20.1 10.9 %collective-permute-start.9 = (bf16[256,768]{1,0:T(8,128)(2,1)S(1)}, bf16[256,768]{1,0:T(8,128)(2,1)S(1)}, u32[]{:S(2)}, u32[]{:S(2)}) collective-permute-start(bf16[256,768]{1,0:T(8,128)(2,1)S(1)} %pad_maximum_fusion.1), channel_id=1, source_target_pairs={{0,16},{16,0},{1,17},{17,1},{2,18},{18,2},{3,19},{19,3},{4,20},{20... | collective-permute-start | bytes 1179656 | tf_op jit(solution)/shard_map/ppermute | solution.py:296
  28.7 8.7 %collective-permute-start.7 = (bf16[256,768]{1,0:T(8,128)(2,1)S(1)}, bf16[256,768]{1,0:T(8,128)(2,1)S(1)}, u32[]{:S(2)}, u32[]{:S(2)}) collective-permute-start(bf16[256,768]{1,0:T(8,128)(2,1)S(1)} %pad_maximum_fusion), channel_id=1, source_target_pairs={{0,16},{16,0},{1,17},{17,1},{2,18},{18,2},{3,19},{19,3},{4,20},{20... | collective-permute-start | bytes 1179656 | tf_op jit(solution)/shard_map/ppermute | solution.py:296
  30.2 7.9 %collective-permute-start.6 = (bf16[256,768]{1,0:T(8,128)(2,1)S(1)}, bf16[256,768]{1,0:T(8,128)(2,1)S(1)}, u32[]{:S(2)}, u32[]{:S(2)}) collective-permute-start(bf16[256,768]{1,0:T(8,128)(2,1)S(1)} %collective-permute-done.5.refs_4_), channel_id=1, source_target_pairs={{0,2},{1,3},{2,0},{3,1},{4,6},{5,7},{6,4},{7,5},{8,10},{9,11},{10,... | collective-permute-start | bytes 1179656 | tf_op jit(solution)/shard_map/ppermute | solution.py:296
  30.7 7.8 %collective-permute-start.8 = (bf16[256,768]{1,0:T(8,128)(2,1)S(1)}, bf16[256,768]{1,0:T(8,128)(2,1)S(1)}, u32[]{:S(2)}, u32[]{:S(2)}) collective-permute-start(bf16[256,768]{1,0:T(8,128)(2,1)S(1)} %collective-permute-done.5.refs_4_), channel_id=1, source_target_pairs={{0,4},{1,5},{2,6},{3,7},{4,0},{5,1},{6,2},{7,3},{8,12},{9,13},{10,... | collective-permute-start | bytes 1179656 | tf_op jit(solution)/shard_map/ppermute | solution.py:296
  31.1 5.3 %collective-permute-start.10 = (bf16[128,768]{1,0:T(8,128)(2,1)S(1)}, bf16[128,768]{1,0:T(8,128)(2,1)S(1)}, u32[]{:S(2)}, u32[]{:S(2)}) collective-permute-start(bf16[128,768]{1,0:T(8,128)(2,1)S(1)} %slice.28), channel_id=1, source_target_pairs={{0,1},{1,0},{2,3},{3,2},{4,8},{5,9},{6,10},{7,11},{8,4},{9,5},{10,... | collective-permute-start | bytes 589832 | tf_op jit(solution)/shard_map/ppermute | solution.py:321
  31.1 10.7 %collective-permute-start.14 = (bf16[384,768]{1,0:T(8,128)(2,1)S(1)}, bf16[384,768]{1,0:T(8,128)(2,1)S(1)}, u32[]{:S(2)}, u32[]{:S(2)}) collective-permute-start(bf16[384,768]{1,0:T(8,128)(2,1)S(1)} %get-tuple-element.71.refs_0_), channel_id=1, source_target_pairs={{0,1},{1,0},{2,3},{3,2},{4,5},{5,4},{6,7},{7,6},{8,9},{9,8},{10,11... | collective-permute-start | bytes 1769480 | tf_op jit(solution)/shard_map/ppermute | solution.py:296
  38.5 3.3 %collective-permute-start.15 = (bf16[384,768]{1,0:T(8,128)(2,1)S(1)}, bf16[384,768]{1,0:T(8,128)(2,1)S(1)}, u32[]{:S(2)}, u32[]{:S(2)}) collective-permute-start(bf16[384,768]{1,0:T(8,128)(2,1)S(1)} %get-tuple-element.89.refs_1_), channel_id=1, source_target_pairs={{0,1},{1,0},{2,3},{3,2},{4,5},{5,4},{6,7},{7,6},{8,9},{9,8},{10,11... | collective-permute-start | bytes 1769480 | tf_op jit(solution)/shard_map/ppermute | solution.py:296
  38.6 3.2 %copy-start.6 = (bf16[192,768]{1,0:T(8,128)(2,1)S(1)}, bf16[192,768]{1,0:T(8,128)(2,1)}, u32[]{:S(2)}) copy-start(bf16[192,768]{1,0:T(8,128)(2,1)} %refs_4_.1) | copy-start | bytes 884740
  38.7 11.6 %collective-permute-start.12 = (bf16[256,768]{1,0:T(8,128)(2,1)S(1)}, bf16[256,768]{1,0:T(8,128)(2,1)S(1)}, u32[]{:S(2)}, u32[]{:S(2)}) collective-permute-start(bf16[256,768]{1,0:T(8,128)(2,1)S(1)} %pad_maximum_fusion.2), channel_id=1, source_target_pairs={{0,16},{16,0},{1,17},{17,1},{2,18},{18,2},{3,19},{19,3},{4,20},{20... | collective-permute-start | bytes 1179656 | tf_op jit(solution)/shard_map/ppermute | solution.py:296
  39.3 11.2 %collective-permute-start.11 = (bf16[256,768]{1,0:T(8,128)(2,1)S(1)}, bf16[256,768]{1,0:T(8,128)(2,1)S(1)}, u32[]{:S(2)}, u32[]{:S(2)}) collective-permute-start(bf16[256,768]{1,0:T(8,128)(2,1)S(1)} %broadcast_select_fusion.refs_7_), channel_id=1, source_target_pairs={{0,2},{1,3},{2,0},{3,1},{4,6},{5,7},{6,4},{7,5},{8,10},{9,11},{10,... | collective-permute-start | bytes 1179656 | tf_op jit(solution)/shard_map/ppermute | solution.py:296
  40.8 7.9 %collective-permute-start.13 = (bf16[128,768]{1,0:T(8,128)(2,1)S(1)}, bf16[128,768]{1,0:T(8,128)(2,1)S(1)}, u32[]{:S(2)}, u32[]{:S(2)}) collective-permute-start(bf16[128,768]{1,0:T(8,128)(2,1)S(1)} %slice.31), channel_id=1, source_target_pairs={{8,0},{9,1},{10,2},{11,3},{0,4},{1,5},{2,6},{3,7},{4,12},{5,13},{6... | collective-permute-start | bytes 589832 | tf_op jit(solution)/shard_map/ppermute | solution.py:317
  52.0 1.8 %collective-permute-start.16 = (f32[128,768]{1,0:T(8,128)S(1)}, f32[128,768]{1,0:T(8,128)S(1)}, u32[]{:S(2)}, u32[]{:S(2)}) collective-permute-start(f32[128,768]{1,0:T(8,128)S(1)} %feed_side.3), channel_id=1, source_target_pairs={{0,1},{1,0},{2,3},{3,2},{4,5},{5,4},{6,7},{7,6},{8,9},{9,8},{10,11... | collective-permute-start | bytes 1179656 | tf_op jit(solution)/shard_map/ppermute | solution.py:296
  52.0 19.5 %copy-start = (bf16[8,256,768]{2,1,0:T(8,128)(2,1)S(1)}, bf16[8,256,768]{2,1,0:T(8,128)(2,1)}, u32[]{:S(2)}) copy-start(bf16[8,256,768]{2,1,0:T(8,128)(2,1)} %books_ref.1) | copy-start | bytes 9437188
  53.5 18.1 %copy-start.1 = (bf16[8,768]{1,0:T(8,128)(2,1)S(1)}, bf16[8,768]{1,0:T(8,128)(2,1)}, u32[]{:S(2)}) copy-start(bf16[8,768]{1,0:T(8,128)(2,1)} %coarse_ref.1) | copy-start | bytes 36868
  (3 other events, 6.8 us)

commit v7 on v6

--- a/solution.py
+++ b/solution.py
@@ -214,13 +214,14 @@
         hidden = jnp.maximum(dot_nt(normed_refs[pack][...], w_in), 0.0).astype(BF16)
         at = (side * packs + pack) * items
         pooled.append(dot(columns_ref[at : at + items], hidden).astype(BF16))
-    out_ref[...] = base_ref[...] + dot(jnp.concatenate(pooled, axis=0), w_down)
-
-
-def feed_side(side, columns, normed, held, pieces, base):
+    total = base_ref[...] + dot(jnp.concatenate(pooled, axis=0), w_down)
+    out_ref[...] = total.astype(out_ref.dtype)
+
+
+def feed_side(side, columns, normed, held, pieces, base, dtype=F32):
     return pl.pallas_call(
         functools.partial(feed_side_kernel, side, len(held), pieces),
-        out_shape=jax.ShapeDtypeStruct(base.shape, F32),
+        out_shape=jax.ShapeDtypeStruct(base.shape, dtype),
         compiler_params=params(),
         cost_estimate=cost(),
         name="feed_side",
@@ -262,7 +263,7 @@
 
 def place_kernel(acc_ref, other_ref, gain_ref, slot_ref, cluster_ref, embed_ref, send_ref):
     width = embed_ref.shape[1]
-    embed = rms(acc_ref[...] + other_ref[...], gain_ref[...][None]).astype(BF16)
+    embed = rms(acc_ref[...] + other_ref[...].astype(F32), gain_ref[...][None]).astype(BF16)
     embed_ref[...] = embed
     slots, items = send_ref.shape[0], embed.shape[0]
     placing = jnp.where(
@@ -340,9 +341,9 @@
     side0, near1, middle, projected = after((side0, near1, middle, projected))
     columns = projected[4]
 
-    side1 = side(near1)
     far2 = along(jnp.where(inner, middle, held), [(1, 0), (0, 2), (2, 3), (3, 1)])
     x0 = twin(cat(side0[split:], near1[split:]))
+    side1 = side(near1)
     first = encode(0, projected, tokens)
     side1, far2, first, projected = after((side1, far2, first, projected))
 
@@ -367,7 +368,7 @@
     last = jnp.where(inner, last_inner, last_outer)
     pieces = rest(0) + rest(0, both) + blocks(1) + rest(2)
     held = [x2, side3, last]
-    there = sibling(feed_side(1, columns, normed, held, pieces, acc[1]))
+    there = sibling(feed_side(1, columns, normed, held, pieces, acc[1], BF16))
     return feed_side(0, columns, normed, held, pieces, acc[0]), there, projected[5]
 
 

time: 85.6 us -> 85.4 us (level)
  transfers between devices with their start and end apart: 17 -> 17, of which waited for: 11 -> 10; matrix products, arithmetic and copies ran while one was open for 0% -> 0% of each run, Pallas kernels for 27% -> 27%
where the time goes in v7:
time: 85.4 us; the launch traced here: 85.2 us
  blocking collectives  28.7 us (34%)
  Pallas kernels  27.5 us (32%)
  starting transfers between devices  17.4 us (20%)
  waiting for transfers between devices  9.47 us (11%)
  between operations  0.93 us (1%)
  matrix products  0.87 us (1%)
    all_to_all x1, blocking collectives, local(): rows = lax.all_to_all(send, 'wide', split_axis=0, concat_axis=0, tiled=True)  17.1 us
    ppermute x13, starting transfers between devices, flip(): return lambda value: lax.ppermute(value, axis_name, pairs)  12.2 us
    all_to_all x1, blocking collectives, local(): lax.all_to_all(codes, 'wide', split_axis=0, concat_axis=0, tiled=True)  11.6 us
    pallas_call x2, Pallas kernels, attend(): pl.pallas_call(functools.partial(attend_kernel, pack), out_shape=(jax.Sha...  9.51 us
    ppermute x13, waiting for transfers between devices, flip(): return lambda value: lax.ppermute(value, axis_name, pairs)  8.87 us
    pallas_call x2, Pallas kernels, feed(): pl.pallas_call(functools.partial(feed_kernel, len(normed[0]), len(held),...  6.33 us
    pallas_call x1, Pallas kernels, project(): pl.pallas_call(functools.partial(project_kernel, wide=wide, capacity=capa...  5.68 us
    ppermute x2, starting transfers between devices, along(): return lax.ppermute(value, 'wide', pairs)  5.08 us
  transfers between devices with their start and end apart: 17, of which 10 were waited for; matrix products, arithmetic and copies ran while one was open for 0% of the time, Pallas kernels for 27%

profile of v7, /device:TPU:0, one launch (start us, length us, event | category | flops | bytes accessed | tf_op | source)
XLA Modules:
  0.0 85.2 jit_solution(11811675499090184277)
XLA Ops:
  0.6 1.1 %hold.1 = bf16[256,768]{1,0:T(8,128)(2,1)S(1)} custom-call(s32[1,1]{1,0:T(1,128)} %bitcast.group_ref, bf16[192,768]{1,0:T(8,128)(2,1)} %refs_4_.1, bf16[192,768]{1,0:T(8,128)(2,1)} %refs_5_.1), custom_call_target="tpu_custom_call" | custom-call | flops 2000000000 | bytes 5000000 | tf_op jit(solution)/shard_map/hold/pallas_call | solution.py:143
  1.7 3.0 %collective-permute-start = (bf16[256,768]{1,0:T(8,128)(2,1)S(1)}, bf16[256,768]{1,0:T(8,128)(2,1)S(1)}, u32[]{:S(2)}, u32[]{:S(2)}) collective-permute-start(bf16[256,768]{1,0:T(8,128)(2,1)S(1)} %hold.1), channel_id=1, source_target_pairs={{0,2},{1,3},{2,0},{3,1},{4,6},{5,7},{6,4},{7,5},{8,10},{9,11},{10,... | collective-permute-start | bytes 1179656 | tf_op jit(solution)/shard_map/ppermute | solution.py:297
  4.8 1.6 %collective-permute-start.1 = (bf16[256,768]{1,0:T(8,128)(2,1)S(1)}, bf16[256,768]{1,0:T(8,128)(2,1)S(1)}, u32[]{:S(2)}, u32[]{:S(2)}) collective-permute-start(bf16[256,768]{1,0:T(8,128)(2,1)S(1)} %hold.1), channel_id=1, source_target_pairs={{0,4},{1,5},{2,6},{3,7},{4,0},{5,1},{6,2},{7,3},{8,12},{9,13},{10,... | collective-permute-start | bytes 1179656 | tf_op jit(solution)/shard_map/ppermute | solution.py:297
  6.9 1.2 %collective-permute-done.3.other_ref = s32[2,64]{1,0:T(2,128)S(1)} collective-permute-done((s32[2,64]{1,0:T(2,128)S(1)}, s32[2,64]{1,0:T(2,128)S(1)}, u32[]{:S(2)}, u32[]{:S(2)}) %collective-permute-start.3) | collective-permute-done | bytes 544 | tf_op jit(solution)/shard_map/ppermute | solution.py:297
  8.1 5.7 %project.1 = (bf16[768,768]{1,0:T(8,128)(2,1)S(1)}, bf16[768,768]{1,0:T(8,128)(2,1)S(1)}, bf16[768,768]{1,0:T(8,128)(2,1)S(1)}, bf16[768,64]{1,0:T(8,128)(2,1)S(...) custom-call(s32[2,64]{1,0:T(2,128)S(1)} %collective-permute-done.3.other_ref, s32[2,64]{1,0:T(2,128)} %lengths_hbm.1, ...), custom_call_target="tpu_custom_call" | custom-call | flops 2000000000 | bytes 5000000 | tf_op jit(solution)/shard_map/project/pallas_call | solution.py:105
  13.9 1.5 %collective-permute-done.1.refs_8_ = bf16[256,768]{1,0:T(8,128)(2,1)S(1)} collective-permute-done((bf16[256,768]{1,0:T(8,128)(2,1)S(1)}, bf16[256,768]{1,0:T(8,128)(2,1)S(1)}, u32[]{:S(2)}, u32[]{:S(2)}) %collective-permute-start.1) | collective-permute-done | bytes 393248 | tf_op jit(solution)/shard_map/ppermute | solution.py:297
  15.4 4.1 %collective-permute-start.5 = (bf16[256,768]{1,0:T(8,128)(2,1)S(1)}, bf16[256,768]{1,0:T(8,128)(2,1)S(1)}, u32[]{:S(2)}, u32[]{:S(2)}) collective-permute-start(bf16[256,768]{1,0:T(8,128)(2,1)S(1)} %broadcast_select_fusion.1), channel_id=1, source_target_pairs={{4,0},{5,1},{6,2},{7,3},{0,8},{1,9},{2,10},{3,11},{8,12},{9,13},{1... | collective-permute-start | bytes 1179656 | tf_op jit(solution)/shard_map/ppermute | solution.py:318
  20.1 1.6 %collective-permute-start.9 = (bf16[256,768]{1,0:T(8,128)(2,1)S(1)}, bf16[256,768]{1,0:T(8,128)(2,1)S(1)}, u32[]{:S(2)}, u32[]{:S(2)}) collective-permute-start(bf16[256,768]{1,0:T(8,128)(2,1)S(1)} %pad_maximum_fusion.1), channel_id=1, source_target_pairs={{0,16},{16,0},{1,17},{17,1},{2,18},{18,2},{3,19},{19,3},{4,20},{20... | collective-permute-start | bytes 1179656 | tf_op jit(solution)/shard_map/ppermute | solution.py:297
  21.7 4.8 %attend.2 = (bf16[384,768]{1,0:T(8,128)(2,1)S(1)}, f32[64,768]{1,0:T(8,128)S(1)}) custom-call(bf16[768,768]{1,0:T(8,128)(2,1)S(1)} %get-tuple-element.82.q_ref, bf16[768,768]{1,0:T(8,128)(2,1)S(1)} %get-tuple-element.83.k_ref, bf16[768,768]{1,0:T(8,128)(2,1)S(1)} %get-tuple-element.84.v_ref, bf16[768,64]{1,0:T(8,128)(2,1)S(1)} %get-tuple-element.85.rows_ref, ...), custom_call_target="tpu_custom_call" | custom-call | flops 2000000000 | bytes 5000000 | tf_op jit(solution)/shard_map/attend/pallas_call | solution.py:193
  26.4 2.2 %collective-permute-done.4.refs_9_ = bf16[256,768]{1,0:T(8,128)(2,1)S(1)} collective-permute-done((bf16[256,768]{1,0:T(8,128)(2,1)S(1)}, bf16[256,768]{1,0:T(8,128)(2,1)S(1)}, u32[]{:S(2)}, u32[]{:S(2)}) %collective-permute-start.4) | collective-permute-done | bytes 393248 | tf_op jit(solution)/shard_map/ppermute | solution.py:297
  28.7 1.6 %collective-permute-start.7 = (bf16[256,768]{1,0:T(8,128)(2,1)S(1)}, bf16[256,768]{1,0:T(8,128)(2,1)S(1)}, u32[]{:S(2)}, u32[]{:S(2)}) collective-permute-start(bf16[256,768]{1,0:T(8,128)(2,1)S(1)} %pad_maximum_fusion), channel_id=1, source_target_pairs={{0,16},{16,0},{1,17},{17,1},{2,18},{18,2},{3,19},{19,3},{4,20},{20... | collective-permute-start | bytes 1179656 | tf_op jit(solution)/shard_map/ppermute | solution.py:297
  31.6 4.8 %attend.3 = (bf16[384,768]{1,0:T(8,128)(2,1)S(1)}, f32[64,768]{1,0:T(8,128)S(1)}) custom-call(bf16[768,768]{1,0:T(8,128)(2,1)S(1)} %get-tuple-element.82.q_ref, bf16[768,768]{1,0:T(8,128)(2,1)S(1)} %get-tuple-element.83.k_ref, bf16[768,768]{1,0:T(8,128)(2,1)S(1)} %get-tuple-element.84.v_ref, bf16[768,64]{1,0:T(8,128)(2,1)S(1)} %get-tuple-element.85.rows_ref, ...), custom_call_target="tpu_custom_call" | custom-call | flops 2000000000 | bytes 5000000 | tf_op jit(solution)/shard_map/attend/pallas_call | solution.py:193
  36.4 1.0 %collective-permute-done.7.refs_10_.refs_5_ = bf16[256,768]{1,0:T(8,128)(2,1)S(1)} collective-permute-done((bf16[256,768]{1,0:T(8,128)(2,1)S(1)}, bf16[256,768]{1,0:T(8,128)(2,1)S(1)}, u32[]{:S(2)}, u32[]{:S(2)}) %collective-permute-start.7) | collective-permute-done | bytes 393248 | tf_op jit(solution)/shard_map/ppermute | solution.py:297
  39.3 1.5 %collective-permute-start.11 = (bf16[256,768]{1,0:T(8,128)(2,1)S(1)}, bf16[256,768]{1,0:T(8,128)(2,1)S(1)}, u32[]{:S(2)}, u32[]{:S(2)}) collective-permute-start(bf16[256,768]{1,0:T(8,128)(2,1)S(1)} %broadcast_select_fusion.refs_7_), channel_id=1, source_target_pairs={{0,2},{1,3},{2,0},{3,1},{4,6},{5,7},{6,4},{7,5},{8,10},{9,11},{10,... | collective-permute-start | bytes 1179656 | tf_op jit(solution)/shard_map/ppermute | solution.py:297
  40.8 1.0 %collective-permute-start.13 = (bf16[128,768]{1,0:T(8,128)(2,1)S(1)}, bf16[128,768]{1,0:T(8,128)(2,1)S(1)}, u32[]{:S(2)}, u32[]{:S(2)}) collective-permute-start(bf16[128,768]{1,0:T(8,128)(2,1)S(1)} %slice.31), channel_id=1, source_target_pairs={{8,0},{9,1},{10,2},{11,3},{0,4},{1,5},{2,6},{3,7},{4,12},{5,13},{6... | collective-permute-start | bytes 589832 | tf_op jit(solution)/shard_map/ppermute | solution.py:318
  41.8 3.8 %feed.2 = (f32[128,768]{1,0:T(8,128)S(1)}, f32[128,768]{1,0:T(8,128)S(1)}) custom-call(bf16[256,384]{1,0:T(8,128)(2,1)S(1)} %get-tuple-element.86.columns_ref, bf16[384,768]{1,0:T(8,128)(2,1)S(1)} %get-tuple-element.71.refs_0_, bf16[384,768]{1,0:T(8,128)(2,1)S(1)} %get-tuple-element.89.refs_1_, bf16[384,768]{1,0:T(8,128)(2,1)S(1)} %collective-permute-done.14.refs_2_.refs_0_, ...), custom_call_target="tpu_custom_call" | custom-call | flops 2000000000 | bytes 5000000 | tf_op jit(solution)/shard_map/feed/pallas_call | solution.py:255
  45.6 2.5 %feed.3 = (f32[128,768]{1,0:T(8,128)S(1)}, f32[128,768]{1,0:T(8,128)S(1)}) custom-call(bf16[256,384]{1,0:T(8,128)(2,1)S(1)} %get-tuple-element.86.columns_ref, bf16[384,768]{1,0:T(8,128)(2,1)S(1)} %get-tuple-element.71.refs_0_, bf16[384,768]{1,0:T(8,128)(2,1)S(1)} %get-tuple-element.89.refs_1_, bf16[384,768]{1,0:T(8,128)(2,1)S(1)} %collective-permute-done.14.refs_2_.refs_0_, ...), custom_call_target="tpu_custom_call" | custom-call | flops 2000000000 | bytes 5000000 | tf_op jit(solution)/shard_map/feed/pallas_call | solution.py:255
  48.7 1.5 %collective-permute-done.12.refs_2_ = bf16[256,768]{1,0:T(8,128)(2,1)S(1)} collective-permute-done((bf16[256,768]{1,0:T(8,128)(2,1)S(1)}, bf16[256,768]{1,0:T(8,128)(2,1)S(1)}, u32[]{:S(2)}, u32[]{:S(2)}) %collective-permute-start.12) | collective-permute-done | bytes 393248 | tf_op jit(solution)/shard_map/ppermute | solution.py:297
  50.5 1.4 %feed_side.3 = bf16[128,768]{1,0:T(8,128)(2,1)S(1)} custom-call(bf16[256,384]{1,0:T(8,128)(2,1)S(1)} %get-tuple-element.86.columns_ref, bf16[384,768]{1,0:T(8,128)(2,1)S(1)} %collective-permute-done.14.refs_2_.refs_0_, bf16[384,768]{1,0:T(8,128)(2,1)S(1)} %collective-permute-done.15.refs_3_.refs_1_, bf16[256,768]{1,0:T(8,128)(2,1)S(1)} %collective-permute-done.12.refs_2_, ...), custom_call_target="tpu_custom_call" | custom-call | flops 2000000000 | bytes 5000000 | tf_op jit(solution)/shard_map/feed_side/pallas_call | solution.py:222
  52.1 1.4 %feed_side.2.acc_ref = f32[128,768]{1,0:T(8,128)S(1)} custom-call(bf16[256,384]{1,0:T(8,128)(2,1)S(1)} %get-tuple-element.86.columns_ref, bf16[384,768]{1,0:T(8,128)(2,1)S(1)} %get-tuple-element.71.refs_0_, bf16[384,768]{1,0:T(8,128)(2,1)S(1)} %get-tuple-element.89.refs_1_, bf16[256,768]{1,0:T(8,128)(2,1)S(1)} %collective-permute-done.12.refs_2_, ...), custom_call_target="tpu_custom_call" | custom-call | flops 2000000000 | bytes 5000000 | tf_op jit(solution)/shard_map/feed_side/pallas_call | solution.py:222
  54.3 17.1 %all_to_all.10 = bf16[16,16,896]{2,1,0:T(8,128)(2,1)S(1)} all-to-all(bf16[16,16,896]{2,1,0:T(8,128)(2,1)S(1)} %bitcast.11), channel_id=1, replica_groups=mesh['groups'=2,'wide'=16] {'wide'}, dimensions={0} | all-to-all | bytes 917504 | tf_op jit(solution)/shard_map/all_to_all | solution.py:421
  71.4 1.3 %codes.1 = bf16[256,256]{1,0:T(8,128)(2,1)S(1)} custom-call(bf16[256,896]{1,0:T(8,128)(2,1)S(1)} %bitcast.9, bf16[8,768]{1,0:T(8,128)(2,1)S(1)} %copy-done.1, bf16[8,256,768]{2,1,0:T(8,128)(2,1)S(1)} %copy-done), custom_call_target="tpu_custom_call" | custom-call | tf_op jit(solution)/shard_map/codes/pallas_call | solution.py:422
  72.7 11.6 %all_to_all.11 = bf16[16,16,256]{2,1,0:T(8,128)(2,1)S(1)} all-to-all(bf16[16,16,256]{2,1,0:T(8,128)(2,1)S(1)} %bitcast.10), channel_id=1, replica_groups=mesh['groups'=2,'wide'=16] {'wide'}, dimensions={0} | all-to-all | bytes 262144 | tf_op jit(solution)/shard_map/all_to_all | solution.py:429
  84.3 0.9 %fusion = f32[128,256]{1,0:T(8,128)} fusion(bf16[256,256]{1,0:T(8,128)(2,1)S(1)} %bitcast.14, s32[128]{0:T(128)S(1)} %bitcast.12), kind=kOutput, calls=%fused_computation.7 | convolution fusion | flops 16809984 | bytes 262656 | tf_op jit(solution)/shard_map/dot_general | solution.py:431
  (57 shorter events, 6.4 us)
Async XLA Ops:
  0.6 5.7 %copy-start.9 = (s32[2,64]{1,0:T(2,128)S(1)}, s32[2,64]{1,0:T(2,128)}, u32[]{:S(2)}) copy-start(s32[2,64]{1,0:T(2,128)} %lengths_hbm.1) | copy-start | bytes 1540
  1.7 12.1 %collective-permute-start = (bf16[256,768]{1,0:T(8,128)(2,1)S(1)}, bf16[256,768]{1,0:T(8,128)(2,1)S(1)}, u32[]{:S(2)}, u32[]{:S(2)}) collective-permute-start(bf16[256,768]{1,0:T(8,128)(2,1)S(1)} %hold.1), channel_id=1, source_target_pairs={{0,2},{1,3},{2,0},{3,1},{4,6},{5,7},{6,4},{7,5},{8,10},{9,11},{10,... | collective-permute-start | bytes 1179656 | tf_op jit(solution)/shard_map/ppermute | solution.py:297
  4.8 10.6 %collective-permute-start.1 = (bf16[256,768]{1,0:T(8,128)(2,1)S(1)}, bf16[256,768]{1,0:T(8,128)(2,1)S(1)}, u32[]{:S(2)}, u32[]{:S(2)}) collective-permute-start(bf16[256,768]{1,0:T(8,128)(2,1)S(1)} %hold.1), channel_id=1, source_target_pairs={{0,4},{1,5},{2,6},{3,7},{4,0},{5,1},{6,2},{7,3},{8,12},{9,13},{10,... | collective-permute-start | bytes 1179656 | tf_op jit(solution)/shard_map/ppermute | solution.py:297
  6.3 9.0 %collective-permute-start.2 = (bf16[256,768]{1,0:T(8,128)(2,1)S(1)}, bf16[256,768]{1,0:T(8,128)(2,1)S(1)}, u32[]{:S(2)}, u32[]{:S(2)}) collective-permute-start(bf16[256,768]{1,0:T(8,128)(2,1)S(1)} %hold.1), channel_id=1, source_target_pairs={{0,1},{1,0},{2,3},{3,2},{4,8},{5,9},{6,10},{7,11},{8,4},{9,5},{10,... | collective-permute-start | bytes 1179656 | tf_op jit(solution)/shard_map/ppermute | solution.py:322
  6.3 1.7 %collective-permute-start.3 = (s32[2,64]{1,0:T(2,128)S(1)}, s32[2,64]{1,0:T(2,128)S(1)}, u32[]{:S(2)}, u32[]{:S(2)}) collective-permute-start(s32[2,64]{1,0:T(2,128)S(1)} %copy-done.9), channel_id=1, source_target_pairs={{0,1},{1,0},{2,3},{3,2},{4,5},{5,4},{6,7},{7,6},{8,9},{9,8},{10,11... | collective-permute-start | bytes 1544 | tf_op jit(solution)/shard_map/ppermute | solution.py:297
  15.3 6.3 %copy-start.4 = (bf16[2,384,768]{2,1,0:T(8,128)(2,1)S(1)}, bf16[2,384,768]{2,1,0:T(8,128)(2,1)}, u32[]{:S(2)}) copy-start(bf16[2,384,768]{2,1,0:T(8,128)(2,1)} %x_ref.3) | copy-start | bytes 3538948
  15.3 6.3 %copy-start.5 = (bf16[768,768]{1,0:T(8,128)(2,1)S(1)}, bf16[768,768]{1,0:T(8,128)(2,1)}, u32[]{:S(2)}) copy-start(bf16[768,768]{1,0:T(8,128)(2,1)} %wo_ref.3) | copy-start | bytes 3538948
  15.3 6.3 %copy-start.8 = (f32[768]{0:T(1024)S(1)}, f32[768]{0:T(1024)}, u32[]{:S(2)}) copy-start(f32[768]{0:T(1024)} %gain_ref.4) | copy-start | bytes 9220
  15.4 11.0 %collective-permute-start.5 = (bf16[256,768]{1,0:T(8,128)(2,1)S(1)}, bf16[256,768]{1,0:T(8,128)(2,1)S(1)}, u32[]{:S(2)}, u32[]{:S(2)}) collective-permute-start(bf16[256,768]{1,0:T(8,128)(2,1)S(1)} %broadcast_select_fusion.1), channel_id=1, source_target_pairs={{4,0},{5,1},{6,2},{7,3},{0,8},{1,9},{2,10},{3,11},{8,12},{9,13},{1... | collective-permute-start | bytes 1179656 | tf_op jit(solution)/shard_map/ppermute | solution.py:318
  19.5 9.1 %collective-permute-start.4 = (bf16[256,768]{1,0:T(8,128)(2,1)S(1)}, bf16[256,768]{1,0:T(8,128)(2,1)S(1)}, u32[]{:S(2)}, u32[]{:S(2)}) collective-permute-start(bf16[256,768]{1,0:T(8,128)(2,1)S(1)} %collective-permute-done.1.refs_8_), channel_id=1, source_target_pairs={{0,2},{1,3},{2,0},{3,1},{4,6},{5,7},{6,4},{7,5},{8,10},{9,11},{10,... | collective-permute-start | bytes 1179656 | tf_op jit(solution)/shard_map/ppermute | solution.py:297
  20.1 10.9 %collective-permute-start.9 = (bf16[256,768]{1,0:T(8,128)(2,1)S(1)}, bf16[256,768]{1,0:T(8,128)(2,1)S(1)}, u32[]{:S(2)}, u32[]{:S(2)}) collective-permute-start(bf16[256,768]{1,0:T(8,128)(2,1)S(1)} %pad_maximum_fusion.1), channel_id=1, source_target_pairs={{0,16},{16,0},{1,17},{17,1},{2,18},{18,2},{3,19},{19,3},{4,20},{20... | collective-permute-start | bytes 1179656 | tf_op jit(solution)/shard_map/ppermute | solution.py:297
  28.7 8.7 %collective-permute-start.7 = (bf16[256,768]{1,0:T(8,128)(2,1)S(1)}, bf16[256,768]{1,0:T(8,128)(2,1)S(1)}, u32[]{:S(2)}, u32[]{:S(2)}) collective-permute-start(bf16[256,768]{1,0:T(8,128)(2,1)S(1)} %pad_maximum_fusion), channel_id=1, source_target_pairs={{0,16},{16,0},{1,17},{17,1},{2,18},{18,2},{3,19},{19,3},{4,20},{20... | collective-permute-start | bytes 1179656 | tf_op jit(solution)/shard_map/ppermute | solution.py:297
  30.2 7.9 %collective-permute-start.6 = (bf16[256,768]{1,0:T(8,128)(2,1)S(1)}, bf16[256,768]{1,0:T(8,128)(2,1)S(1)}, u32[]{:S(2)}, u32[]{:S(2)}) collective-permute-start(bf16[256,768]{1,0:T(8,128)(2,1)S(1)} %collective-permute-done.5.refs_4_), channel_id=1, source_target_pairs={{0,2},{1,3},{2,0},{3,1},{4,6},{5,7},{6,4},{7,5},{8,10},{9,11},{10,... | collective-permute-start | bytes 1179656 | tf_op jit(solution)/shard_map/ppermute | solution.py:297
  30.7 7.8 %collective-permute-start.8 = (bf16[256,768]{1,0:T(8,128)(2,1)S(1)}, bf16[256,768]{1,0:T(8,128)(2,1)S(1)}, u32[]{:S(2)}, u32[]{:S(2)}) collective-permute-start(bf16[256,768]{1,0:T(8,128)(2,1)S(1)} %collective-permute-done.5.refs_4_), channel_id=1, source_target_pairs={{0,4},{1,5},{2,6},{3,7},{4,0},{5,1},{6,2},{7,3},{8,12},{9,13},{10,... | collective-permute-start | bytes 1179656 | tf_op jit(solution)/shard_map/ppermute | solution.py:297
  31.1 5.3 %collective-permute-start.10 = (bf16[128,768]{1,0:T(8,128)(2,1)S(1)}, bf16[128,768]{1,0:T(8,128)(2,1)S(1)}, u32[]{:S(2)}, u32[]{:S(2)}) collective-permute-start(bf16[128,768]{1,0:T(8,128)(2,1)S(1)} %slice.28), channel_id=1, source_target_pairs={{0,1},{1,0},{2,3},{3,2},{4,8},{5,9},{6,10},{7,11},{8,4},{9,5},{10,... | collective-permute-start | bytes 589832 | tf_op jit(solution)/shard_map/ppermute | solution.py:322
  31.1 10.7 %collective-permute-start.14 = (bf16[384,768]{1,0:T(8,128)(2,1)S(1)}, bf16[384,768]{1,0:T(8,128)(2,1)S(1)}, u32[]{:S(2)}, u32[]{:S(2)}) collective-permute-start(bf16[384,768]{1,0:T(8,128)(2,1)S(1)} %get-tuple-element.71.refs_0_), channel_id=1, source_target_pairs={{0,1},{1,0},{2,3},{3,2},{4,5},{5,4},{6,7},{7,6},{8,9},{9,8},{10,11... | collective-permute-start | bytes 1769480 | tf_op jit(solution)/shard_map/ppermute | solution.py:297
  38.5 3.3 %collective-permute-start.15 = (bf16[384,768]{1,0:T(8,128)(2,1)S(1)}, bf16[384,768]{1,0:T(8,128)(2,1)S(1)}, u32[]{:S(2)}, u32[]{:S(2)}) collective-permute-start(bf16[384,768]{1,0:T(8,128)(2,1)S(1)} %get-tuple-element.89.refs_1_), channel_id=1, source_target_pairs={{0,1},{1,0},{2,3},{3,2},{4,5},{5,4},{6,7},{7,6},{8,9},{9,8},{10,11... | collective-permute-start | bytes 1769480 | tf_op jit(solution)/shard_map/ppermute | solution.py:297
  38.6 3.2 %copy-start.6 = (bf16[192,768]{1,0:T(8,128)(2,1)S(1)}, bf16[192,768]{1,0:T(8,128)(2,1)}, u32[]{:S(2)}) copy-start(bf16[192,768]{1,0:T(8,128)(2,1)} %refs_4_.1) | copy-start | bytes 884740
  38.7 11.6 %collective-permute-start.12 = (bf16[256,768]{1,0:T(8,128)(2,1)S(1)}, bf16[256,768]{1,0:T(8,128)(2,1)S(1)}, u32[]{:S(2)}, u32[]{:S(2)}) collective-permute-start(bf16[256,768]{1,0:T(8,128)(2,1)S(1)} %pad_maximum_fusion.2), channel_id=1, source_target_pairs={{0,16},{16,0},{1,17},{17,1},{2,18},{18,2},{3,19},{19,3},{4,20},{20... | collective-permute-start | bytes 1179656 | tf_op jit(solution)/shard_map/ppermute | solution.py:297
  39.3 11.2 %collective-permute-start.11 = (bf16[256,768]{1,0:T(8,128)(2,1)S(1)}, bf16[256,768]{1,0:T(8,128)(2,1)S(1)}, u32[]{:S(2)}, u32[]{:S(2)}) collective-permute-start(bf16[256,768]{1,0:T(8,128)(2,1)S(1)} %broadcast_select_fusion.refs_7_), channel_id=1, source_target_pairs={{0,2},{1,3},{2,0},{3,1},{4,6},{5,7},{6,4},{7,5},{8,10},{9,11},{10,... | collective-permute-start | bytes 1179656 | tf_op jit(solution)/shard_map/ppermute | solution.py:297
  40.8 7.9 %collective-permute-start.13 = (bf16[128,768]{1,0:T(8,128)(2,1)S(1)}, bf16[128,768]{1,0:T(8,128)(2,1)S(1)}, u32[]{:S(2)}, u32[]{:S(2)}) collective-permute-start(bf16[128,768]{1,0:T(8,128)(2,1)S(1)} %slice.31), channel_id=1, source_target_pairs={{8,0},{9,1},{10,2},{11,3},{0,4},{1,5},{2,6},{3,7},{4,12},{5,13},{6... | collective-permute-start | bytes 589832 | tf_op jit(solution)/shard_map/ppermute | solution.py:318
  52.0 1.5 %collective-permute-start.16 = (bf16[128,768]{1,0:T(8,128)(2,1)S(1)}, bf16[128,768]{1,0:T(8,128)(2,1)S(1)}, u32[]{:S(2)}, u32[]{:S(2)}) collective-permute-start(bf16[128,768]{1,0:T(8,128)(2,1)S(1)} %feed_side.3), channel_id=1, source_target_pairs={{0,1},{1,0},{2,3},{3,2},{4,5},{5,4},{6,7},{7,6},{8,9},{9,8},{10,11... | collective-permute-start | bytes 589832 | tf_op jit(solution)/shard_map/ppermute | solution.py:297
  52.0 19.3 %copy-start = (bf16[8,256,768]{2,1,0:T(8,128)(2,1)S(1)}, bf16[8,256,768]{2,1,0:T(8,128)(2,1)}, u32[]{:S(2)}) copy-start(bf16[8,256,768]{2,1,0:T(8,128)(2,1)} %books_ref.1) | copy-start | bytes 9437188
  53.5 17.9 %copy-start.1 = (bf16[8,768]{1,0:T(8,128)(2,1)S(1)}, bf16[8,768]{1,0:T(8,128)(2,1)}, u32[]{:S(2)}) copy-start(bf16[8,768]{1,0:T(8,128)(2,1)} %coarse_ref.1) | copy-start | bytes 36868
  (3 other events, 6.3 us)

commit v8 on v6

--- a/solution.py
+++ b/solution.py
@@ -291,6 +291,16 @@
     out_ref[...] = total.astype(BF16)
 
 
+def take_kernel(slot_ref, codes_ref, out_ref):
+    slots, items = codes_ref.shape[0], slot_ref.shape[1]
+    placing = jnp.where(
+        lax.broadcasted_iota(jnp.int32, (slots, items), 0) == slot_ref[...], 1.0, 0.0
+    ).astype(BF16)
+    out_ref[...] = lax.dot_general(
+        placing, codes_ref[...], (((0,), (0,)), ((), ())), preferred_element_type=F32
+    )
+
+
 def flip(axis_name, count, bits):
     pairs = [(i, i ^ bits) for i in range(count)]
     return lambda value: lax.ppermute(value, axis_name, pairs)
@@ -340,9 +350,9 @@
     side0, near1, middle, projected = after((side0, near1, middle, projected))
     columns = projected[4]
 
-    side1 = side(near1)
     far2 = along(jnp.where(inner, middle, held), [(1, 0), (0, 2), (2, 3), (3, 1)])
     x0 = twin(cat(side0[split:], near1[split:]))
+    side1 = side(near1)
     first = encode(0, projected, tokens)
     side1, far2, first, projected = after((side1, far2, first, projected))
 
@@ -426,8 +436,13 @@
     )(rows.reshape(slots, width + 128), coarse, centroids)
     codes = codes.reshape(wide_count, capacity, codes_count)
     returned = lax.all_to_all(codes, "wide", split_axis=0, concat_axis=0, tiled=True)
-    taking = (slots_of[0][:, None] == jnp.arange(slots, dtype=jnp.int32)[None, :]).astype(BF16)
-    item_codes = jnp.dot(taking, returned.reshape(slots, codes_count), preferred_element_type=F32)
+    item_codes = pl.pallas_call(
+        take_kernel,
+        out_shape=jax.ShapeDtypeStruct((items_dev, codes_count), F32),
+        compiler_params=params(),
+        cost_estimate=cost(),
+        name="take",
+    )(slots_of, returned.reshape(slots, codes_count))
     return (item_embed, item_codes)
 
 

time: 85.6 us -> 85.6 us (level)
  matrix products: 0.87 us -> 0 us
    dot_general x1 -> x0, matrix products: 0.87 us -> none  [local(): jnp.dot(taking, returned.reshape(slots, codes_count), preferred_element_t...]
    pallas_call x0 -> x1, Pallas kernels: none -> 0.86 us  [local(): pl.pallas_call(take_kernel, out_shape=jax.ShapeDtypeStruct((items_dev, co...]
where the time goes in v8:
time: 85.6 us; the launch traced here: 85.4 us
  blocking collectives  28.6 us (33%)
  Pallas kernels  28.3 us (33%)
  starting transfers between devices  17.4 us (20%)
  waiting for transfers between devices  9.75 us (11%)
  between operations  0.91 us (1%)
    all_to_all x1, blocking collectives, local(): rows = lax.all_to_all(send, 'wide', split_axis=0, concat_axis=0, tiled=True)  17 us
    ppermute x13, starting transfers between devices, flip(): return lambda value: lax.ppermute(value, axis_name, pairs)  12.2 us
    all_to_all x1, blocking collectives, local(): lax.all_to_all(codes, 'wide', split_axis=0, concat_axis=0, tiled=True)  11.6 us
    pallas_call x2, Pallas kernels, attend(): pl.pallas_call(functools.partial(attend_kernel, pack), out_shape=(jax.Sha...  9.51 us
    ppermute x13, waiting for transfers between devices, flip(): return lambda value: lax.ppermute(value, axis_name, pairs)  9.15 us
    pallas_call x2, Pallas kernels, feed(): pl.pallas_call(functools.partial(feed_kernel, len(normed[0]), len(held),...  6.33 us
    pallas_call x1, Pallas kernels, project(): pl.pallas_call(functools.partial(project_kernel, wide=wide, capacity=capa...  5.68 us
    ppermute x2, starting transfers between devices, along(): return lax.ppermute(value, 'wide', pairs)  5.08 us
  transfers between devices with their start and end apart: 17, of which 11 were waited for; matrix products, arithmetic and copies ran while one was open for 0% of the time, Pallas kernels for 27%

profile of v8, /device:TPU:0, one launch (start us, length us, event | category | flops | bytes accessed | tf_op | source)
XLA Modules:
  0.0 85.4 jit_solution(2628630842018994892)
XLA Ops:
  0.6 1.1 %hold.1 = bf16[256,768]{1,0:T(8,128)(2,1)S(1)} custom-call(s32[1,1]{1,0:T(1,128)} %bitcast.group_ref, bf16[192,768]{1,0:T(8,128)(2,1)} %refs_4_.1, bf16[192,768]{1,0:T(8,128)(2,1)} %refs_5_.1), custom_call_target="tpu_custom_call" | custom-call | flops 2000000000 | bytes 5000000 | tf_op jit(solution)/shard_map/hold/pallas_call | solution.py:143
  1.7 3.0 %collective-permute-start = (bf16[256,768]{1,0:T(8,128)(2,1)S(1)}, bf16[256,768]{1,0:T(8,128)(2,1)S(1)}, u32[]{:S(2)}, u32[]{:S(2)}) collective-permute-start(bf16[256,768]{1,0:T(8,128)(2,1)S(1)} %hold.1), channel_id=1, source_target_pairs={{0,2},{1,3},{2,0},{3,1},{4,6},{5,7},{6,4},{7,5},{8,10},{9,11},{10,... | collective-permute-start | bytes 1179656 | tf_op jit(solution)/shard_map/ppermute | solution.py:306
  4.8 1.6 %collective-permute-start.1 = (bf16[256,768]{1,0:T(8,128)(2,1)S(1)}, bf16[256,768]{1,0:T(8,128)(2,1)S(1)}, u32[]{:S(2)}, u32[]{:S(2)}) collective-permute-start(bf16[256,768]{1,0:T(8,128)(2,1)S(1)} %hold.1), channel_id=1, source_target_pairs={{0,4},{1,5},{2,6},{3,7},{4,0},{5,1},{6,2},{7,3},{8,12},{9,13},{10,... | collective-permute-start | bytes 1179656 | tf_op jit(solution)/shard_map/ppermute | solution.py:306
  6.9 1.2 %collective-permute-done.3.other_ref = s32[2,64]{1,0:T(2,128)S(1)} collective-permute-done((s32[2,64]{1,0:T(2,128)S(1)}, s32[2,64]{1,0:T(2,128)S(1)}, u32[]{:S(2)}, u32[]{:S(2)}) %collective-permute-start.3) | collective-permute-done | bytes 544 | tf_op jit(solution)/shard_map/ppermute | solution.py:306
  8.1 5.7 %project.1 = (bf16[768,768]{1,0:T(8,128)(2,1)S(1)}, bf16[768,768]{1,0:T(8,128)(2,1)S(1)}, bf16[768,768]{1,0:T(8,128)(2,1)S(1)}, bf16[768,64]{1,0:T(8,128)(2,1)S(...) custom-call(s32[2,64]{1,0:T(2,128)S(1)} %collective-permute-done.3.other_ref, s32[2,64]{1,0:T(2,128)} %lengths_hbm.1, ...), custom_call_target="tpu_custom_call" | custom-call | flops 2000000000 | bytes 5000000 | tf_op jit(solution)/shard_map/project/pallas_call | solution.py:105
  13.9 1.5 %collective-permute-done.1.refs_8_ = bf16[256,768]{1,0:T(8,128)(2,1)S(1)} collective-permute-done((bf16[256,768]{1,0:T(8,128)(2,1)S(1)}, bf16[256,768]{1,0:T(8,128)(2,1)S(1)}, u32[]{:S(2)}, u32[]{:S(2)}) %collective-permute-start.1) | collective-permute-done | bytes 393248 | tf_op jit(solution)/shard_map/ppermute | solution.py:306
  15.4 4.1 %collective-permute-start.5 = (bf16[256,768]{1,0:T(8,128)(2,1)S(1)}, bf16[256,768]{1,0:T(8,128)(2,1)S(1)}, u32[]{:S(2)}, u32[]{:S(2)}) collective-permute-start(bf16[256,768]{1,0:T(8,128)(2,1)S(1)} %broadcast_select_fusion.1), channel_id=1, source_target_pairs={{4,0},{5,1},{6,2},{7,3},{0,8},{1,9},{2,10},{3,11},{8,12},{9,13},{1... | collective-permute-start | bytes 1179656 | tf_op jit(solution)/shard_map/ppermute | solution.py:327
  20.1 1.6 %collective-permute-start.9 = (bf16[256,768]{1,0:T(8,128)(2,1)S(1)}, bf16[256,768]{1,0:T(8,128)(2,1)S(1)}, u32[]{:S(2)}, u32[]{:S(2)}) collective-permute-start(bf16[256,768]{1,0:T(8,128)(2,1)S(1)} %pad_maximum_fusion.1), channel_id=1, source_target_pairs={{0,16},{16,0},{1,17},{17,1},{2,18},{18,2},{3,19},{19,3},{4,20},{20... | collective-permute-start | bytes 1179656 | tf_op jit(solution)/shard_map/ppermute | solution.py:306
  21.7 4.8 %attend.2 = (bf16[384,768]{1,0:T(8,128)(2,1)S(1)}, f32[64,768]{1,0:T(8,128)S(1)}) custom-call(bf16[768,768]{1,0:T(8,128)(2,1)S(1)} %get-tuple-element.82.q_ref, bf16[768,768]{1,0:T(8,128)(2,1)S(1)} %get-tuple-element.83.k_ref, bf16[768,768]{1,0:T(8,128)(2,1)S(1)} %get-tuple-element.84.v_ref, bf16[768,64]{1,0:T(8,128)(2,1)S(1)} %get-tuple-element.85.rows_ref, ...), custom_call_target="tpu_custom_call" | custom-call | flops 2000000000 | bytes 5000000 | tf_op jit(solution)/shard_map/attend/pallas_call | solution.py:193
  26.4 2.2 %collective-permute-done.4.refs_9_ = bf16[256,768]{1,0:T(8,128)(2,1)S(1)} collective-permute-done((bf16[256,768]{1,0:T(8,128)(2,1)S(1)}, bf16[256,768]{1,0:T(8,128)(2,1)S(1)}, u32[]{:S(2)}, u32[]{:S(2)}) %collective-permute-start.4) | collective-permute-done | bytes 393248 | tf_op jit(solution)/shard_map/ppermute | solution.py:306
  28.7 1.6 %collective-permute-start.7 = (bf16[256,768]{1,0:T(8,128)(2,1)S(1)}, bf16[256,768]{1,0:T(8,128)(2,1)S(1)}, u32[]{:S(2)}, u32[]{:S(2)}) collective-permute-start(bf16[256,768]{1,0:T(8,128)(2,1)S(1)} %pad_maximum_fusion), channel_id=1, source_target_pairs={{0,16},{16,0},{1,17},{17,1},{2,18},{18,2},{3,19},{19,3},{4,20},{20... | collective-permute-start | bytes 1179656 | tf_op jit(solution)/shard_map/ppermute | solution.py:306
  31.6 4.8 %attend.3 = (bf16[384,768]{1,0:T(8,128)(2,1)S(1)}, f32[64,768]{1,0:T(8,128)S(1)}) custom-call(bf16[768,768]{1,0:T(8,128)(2,1)S(1)} %get-tuple-element.82.q_ref, bf16[768,768]{1,0:T(8,128)(2,1)S(1)} %get-tuple-element.83.k_ref, bf16[768,768]{1,0:T(8,128)(2,1)S(1)} %get-tuple-element.84.v_ref, bf16[768,64]{1,0:T(8,128)(2,1)S(1)} %get-tuple-element.85.rows_ref, ...), custom_call_target="tpu_custom_call" | custom-call | flops 2000000000 | bytes 5000000 | tf_op jit(solution)/shard_map/attend/pallas_call | solution.py:193
  36.4 1.0 %collective-permute-done.7.refs_10_.refs_5_ = bf16[256,768]{1,0:T(8,128)(2,1)S(1)} collective-permute-done((bf16[256,768]{1,0:T(8,128)(2,1)S(1)}, bf16[256,768]{1,0:T(8,128)(2,1)S(1)}, u32[]{:S(2)}, u32[]{:S(2)}) %collective-permute-start.7) | collective-permute-done | bytes 393248 | tf_op jit(solution)/shard_map/ppermute | solution.py:306
  39.3 1.5 %collective-permute-start.11 = (bf16[256,768]{1,0:T(8,128)(2,1)S(1)}, bf16[256,768]{1,0:T(8,128)(2,1)S(1)}, u32[]{:S(2)}, u32[]{:S(2)}) collective-permute-start(bf16[256,768]{1,0:T(8,128)(2,1)S(1)} %broadcast_select_fusion.refs_7_), channel_id=1, source_target_pairs={{0,2},{1,3},{2,0},{3,1},{4,6},{5,7},{6,4},{7,5},{8,10},{9,11},{10,... | collective-permute-start | bytes 1179656 | tf_op jit(solution)/shard_map/ppermute | solution.py:306
  40.8 1.0 %collective-permute-start.13 = (bf16[128,768]{1,0:T(8,128)(2,1)S(1)}, bf16[128,768]{1,0:T(8,128)(2,1)S(1)}, u32[]{:S(2)}, u32[]{:S(2)}) collective-permute-start(bf16[128,768]{1,0:T(8,128)(2,1)S(1)} %slice.31), channel_id=1, source_target_pairs={{8,0},{9,1},{10,2},{11,3},{0,4},{1,5},{2,6},{3,7},{4,12},{5,13},{6... | collective-permute-start | bytes 589832 | tf_op jit(solution)/shard_map/ppermute | solution.py:327
  41.8 3.8 %feed.2 = (f32[128,768]{1,0:T(8,128)S(1)}, f32[128,768]{1,0:T(8,128)S(1)}) custom-call(bf16[256,384]{1,0:T(8,128)(2,1)S(1)} %get-tuple-element.86.columns_ref, bf16[384,768]{1,0:T(8,128)(2,1)S(1)} %get-tuple-element.71.refs_0_, bf16[384,768]{1,0:T(8,128)(2,1)S(1)} %get-tuple-element.89.refs_1_, bf16[384,768]{1,0:T(8,128)(2,1)S(1)} %collective-permute-done.14.refs_2_.refs_0_, ...), custom_call_target="tpu_custom_call" | custom-call | flops 2000000000 | bytes 5000000 | tf_op jit(solution)/shard_map/feed/pallas_call | solution.py:254
  45.6 2.5 %feed.3 = (f32[128,768]{1,0:T(8,128)S(1)}, f32[128,768]{1,0:T(8,128)S(1)}) custom-call(bf16[256,384]{1,0:T(8,128)(2,1)S(1)} %get-tuple-element.86.columns_ref, bf16[384,768]{1,0:T(8,128)(2,1)S(1)} %get-tuple-element.71.refs_0_, bf16[384,768]{1,0:T(8,128)(2,1)S(1)} %get-tuple-element.89.refs_1_, bf16[384,768]{1,0:T(8,128)(2,1)S(1)} %collective-permute-done.14.refs_2_.refs_0_, ...), custom_call_target="tpu_custom_call" | custom-call | flops 2000000000 | bytes 5000000 | tf_op jit(solution)/shard_map/feed/pallas_call | solution.py:254
  48.7 1.5 %collective-permute-done.12.refs_2_ = bf16[256,768]{1,0:T(8,128)(2,1)S(1)} collective-permute-done((bf16[256,768]{1,0:T(8,128)(2,1)S(1)}, bf16[256,768]{1,0:T(8,128)(2,1)S(1)}, u32[]{:S(2)}, u32[]{:S(2)}) %collective-permute-start.12) | collective-permute-done | bytes 393248 | tf_op jit(solution)/shard_map/ppermute | solution.py:306
  50.5 1.4 %feed_side.3 = f32[128,768]{1,0:T(8,128)S(1)} custom-call(bf16[256,384]{1,0:T(8,128)(2,1)S(1)} %get-tuple-element.86.columns_ref, bf16[384,768]{1,0:T(8,128)(2,1)S(1)} %collective-permute-done.14.refs_2_.refs_0_, bf16[384,768]{1,0:T(8,128)(2,1)S(1)} %collective-permute-done.15.refs_3_.refs_1_, bf16[256,768]{1,0:T(8,128)(2,1)S(1)} %collective-permute-done.12.refs_2_, ...), custom_call_target="tpu_custom_call" | custom-call | flops 2000000000 | bytes 5000000 | tf_op jit(solution)/shard_map/feed_side/pallas_call | solution.py:221
  52.1 1.4 %feed_side.2.acc_ref = f32[128,768]{1,0:T(8,128)S(1)} custom-call(bf16[256,384]{1,0:T(8,128)(2,1)S(1)} %get-tuple-element.86.columns_ref, bf16[384,768]{1,0:T(8,128)(2,1)S(1)} %get-tuple-element.71.refs_0_, bf16[384,768]{1,0:T(8,128)(2,1)S(1)} %get-tuple-element.89.refs_1_, bf16[256,768]{1,0:T(8,128)(2,1)S(1)} %collective-permute-done.12.refs_2_, ...), custom_call_target="tpu_custom_call" | custom-call | flops 2000000000 | bytes 5000000 | tf_op jit(solution)/shard_map/feed_side/pallas_call | solution.py:221
  54.6 17.0 %all_to_all.10 = bf16[16,16,896]{2,1,0:T(8,128)(2,1)S(1)} all-to-all(bf16[16,16,896]{2,1,0:T(8,128)(2,1)S(1)} %bitcast.9), channel_id=1, replica_groups=mesh['groups'=2,'wide'=16] {'wide'}, dimensions={0} | all-to-all | bytes 917504 | tf_op jit(solution)/shard_map/all_to_all | solution.py:430
  71.6 1.3 %codes.1 = bf16[256,256]{1,0:T(8,128)(2,1)S(1)} custom-call(bf16[256,896]{1,0:T(8,128)(2,1)S(1)} %bitcast.7, bf16[8,768]{1,0:T(8,128)(2,1)S(1)} %copy-done.1, bf16[8,256,768]{2,1,0:T(8,128)(2,1)S(1)} %copy-done), custom_call_target="tpu_custom_call" | custom-call | tf_op jit(solution)/shard_map/codes/pallas_call | solution.py:431
  72.9 11.6 %all_to_all.11 = bf16[16,16,256]{2,1,0:T(8,128)(2,1)S(1)} all-to-all(bf16[16,16,256]{2,1,0:T(8,128)(2,1)S(1)} %bitcast.8), channel_id=1, replica_groups=mesh['groups'=2,'wide'=16] {'wide'}, dimensions={0} | all-to-all | bytes 262144 | tf_op jit(solution)/shard_map/all_to_all | solution.py:438
  84.5 0.9 %take.1 = f32[128,256]{1,0:T(8,128)} custom-call(s32[1,128]{1,0:T(1,128)S(1)} %get-tuple-element.105.slot_ref, bf16[256,256]{1,0:T(8,128)(2,1)S(1)} %bitcast.10), custom_call_target="tpu_custom_call" | custom-call | flops 2000000000 | bytes 5000000 | tf_op jit(solution)/shard_map/take/pallas_call | solution.py:439
  (57 shorter events, 6.6 us)
Async XLA Ops:
  0.6 5.7 %copy-start.9 = (s32[2,64]{1,0:T(2,128)S(1)}, s32[2,64]{1,0:T(2,128)}, u32[]{:S(2)}) copy-start(s32[2,64]{1,0:T(2,128)} %lengths_hbm.1) | copy-start | bytes 1540
  1.7 12.1 %collective-permute-start = (bf16[256,768]{1,0:T(8,128)(2,1)S(1)}, bf16[256,768]{1,0:T(8,128)(2,1)S(1)}, u32[]{:S(2)}, u32[]{:S(2)}) collective-permute-start(bf16[256,768]{1,0:T(8,128)(2,1)S(1)} %hold.1), channel_id=1, source_target_pairs={{0,2},{1,3},{2,0},{3,1},{4,6},{5,7},{6,4},{7,5},{8,10},{9,11},{10,... | collective-permute-start | bytes 1179656 | tf_op jit(solution)/shard_map/ppermute | solution.py:306
  4.8 10.6 %collective-permute-start.1 = (bf16[256,768]{1,0:T(8,128)(2,1)S(1)}, bf16[256,768]{1,0:T(8,128)(2,1)S(1)}, u32[]{:S(2)}, u32[]{:S(2)}) collective-permute-start(bf16[256,768]{1,0:T(8,128)(2,1)S(1)} %hold.1), channel_id=1, source_target_pairs={{0,4},{1,5},{2,6},{3,7},{4,0},{5,1},{6,2},{7,3},{8,12},{9,13},{10,... | collective-permute-start | bytes 1179656 | tf_op jit(solution)/shard_map/ppermute | solution.py:306
  6.3 9.0 %collective-permute-start.2 = (bf16[256,768]{1,0:T(8,128)(2,1)S(1)}, bf16[256,768]{1,0:T(8,128)(2,1)S(1)}, u32[]{:S(2)}, u32[]{:S(2)}) collective-permute-start(bf16[256,768]{1,0:T(8,128)(2,1)S(1)} %hold.1), channel_id=1, source_target_pairs={{0,1},{1,0},{2,3},{3,2},{4,8},{5,9},{6,10},{7,11},{8,4},{9,5},{10,... | collective-permute-start | bytes 1179656 | tf_op jit(solution)/shard_map/ppermute | solution.py:331
  6.3 1.7 %collective-permute-start.3 = (s32[2,64]{1,0:T(2,128)S(1)}, s32[2,64]{1,0:T(2,128)S(1)}, u32[]{:S(2)}, u32[]{:S(2)}) collective-permute-start(s32[2,64]{1,0:T(2,128)S(1)} %copy-done.9), channel_id=1, source_target_pairs={{0,1},{1,0},{2,3},{3,2},{4,5},{5,4},{6,7},{7,6},{8,9},{9,8},{10,11... | collective-permute-start | bytes 1544 | tf_op jit(solution)/shard_map/ppermute | solution.py:306
  15.3 6.3 %copy-start.4 = (bf16[2,384,768]{2,1,0:T(8,128)(2,1)S(1)}, bf16[2,384,768]{2,1,0:T(8,128)(2,1)}, u32[]{:S(2)}) copy-start(bf16[2,384,768]{2,1,0:T(8,128)(2,1)} %x_ref.3) | copy-start | bytes 3538948
  15.3 6.3 %copy-start.5 = (bf16[768,768]{1,0:T(8,128)(2,1)S(1)}, bf16[768,768]{1,0:T(8,128)(2,1)}, u32[]{:S(2)}) copy-start(bf16[768,768]{1,0:T(8,128)(2,1)} %wo_ref.3) | copy-start | bytes 3538948
  15.3 6.3 %copy-start.8 = (f32[768]{0:T(1024)S(1)}, f32[768]{0:T(1024)}, u32[]{:S(2)}) copy-start(f32[768]{0:T(1024)} %gain_ref.4) | copy-start | bytes 9220
  15.4 11.0 %collective-permute-start.5 = (bf16[256,768]{1,0:T(8,128)(2,1)S(1)}, bf16[256,768]{1,0:T(8,128)(2,1)S(1)}, u32[]{:S(2)}, u32[]{:S(2)}) collective-permute-start(bf16[256,768]{1,0:T(8,128)(2,1)S(1)} %broadcast_select_fusion.1), channel_id=1, source_target_pairs={{4,0},{5,1},{6,2},{7,3},{0,8},{1,9},{2,10},{3,11},{8,12},{9,13},{1... | collective-permute-start | bytes 1179656 | tf_op jit(solution)/shard_map/ppermute | solution.py:327
  19.5 9.1 %collective-permute-start.4 = (bf16[256,768]{1,0:T(8,128)(2,1)S(1)}, bf16[256,768]{1,0:T(8,128)(2,1)S(1)}, u32[]{:S(2)}, u32[]{:S(2)}) collective-permute-start(bf16[256,768]{1,0:T(8,128)(2,1)S(1)} %collective-permute-done.1.refs_8_), channel_id=1, source_target_pairs={{0,2},{1,3},{2,0},{3,1},{4,6},{5,7},{6,4},{7,5},{8,10},{9,11},{10,... | collective-permute-start | bytes 1179656 | tf_op jit(solution)/shard_map/ppermute | solution.py:306
  20.1 10.9 %collective-permute-start.9 = (bf16[256,768]{1,0:T(8,128)(2,1)S(1)}, bf16[256,768]{1,0:T(8,128)(2,1)S(1)}, u32[]{:S(2)}, u32[]{:S(2)}) collective-permute-start(bf16[256,768]{1,0:T(8,128)(2,1)S(1)} %pad_maximum_fusion.1), channel_id=1, source_target_pairs={{0,16},{16,0},{1,17},{17,1},{2,18},{18,2},{3,19},{19,3},{4,20},{20... | collective-permute-start | bytes 1179656 | tf_op jit(solution)/shard_map/ppermute | solution.py:306
  28.7 8.7 %collective-permute-start.7 = (bf16[256,768]{1,0:T(8,128)(2,1)S(1)}, bf16[256,768]{1,0:T(8,128)(2,1)S(1)}, u32[]{:S(2)}, u32[]{:S(2)}) collective-permute-start(bf16[256,768]{1,0:T(8,128)(2,1)S(1)} %pad_maximum_fusion), channel_id=1, source_target_pairs={{0,16},{16,0},{1,17},{17,1},{2,18},{18,2},{3,19},{19,3},{4,20},{20... | collective-permute-start | bytes 1179656 | tf_op jit(solution)/shard_map/ppermute | solution.py:306
  30.2 7.9 %collective-permute-start.6 = (bf16[256,768]{1,0:T(8,128)(2,1)S(1)}, bf16[256,768]{1,0:T(8,128)(2,1)S(1)}, u32[]{:S(2)}, u32[]{:S(2)}) collective-permute-start(bf16[256,768]{1,0:T(8,128)(2,1)S(1)} %collective-permute-done.5.refs_4_), channel_id=1, source_target_pairs={{0,2},{1,3},{2,0},{3,1},{4,6},{5,7},{6,4},{7,5},{8,10},{9,11},{10,... | collective-permute-start | bytes 1179656 | tf_op jit(solution)/shard_map/ppermute | solution.py:306
  30.7 7.8 %collective-permute-start.8 = (bf16[256,768]{1,0:T(8,128)(2,1)S(1)}, bf16[256,768]{1,0:T(8,128)(2,1)S(1)}, u32[]{:S(2)}, u32[]{:S(2)}) collective-permute-start(bf16[256,768]{1,0:T(8,128)(2,1)S(1)} %collective-permute-done.5.refs_4_), channel_id=1, source_target_pairs={{0,4},{1,5},{2,6},{3,7},{4,0},{5,1},{6,2},{7,3},{8,12},{9,13},{10,... | collective-permute-start | bytes 1179656 | tf_op jit(solution)/shard_map/ppermute | solution.py:306
  31.1 5.3 %collective-permute-start.10 = (bf16[128,768]{1,0:T(8,128)(2,1)S(1)}, bf16[128,768]{1,0:T(8,128)(2,1)S(1)}, u32[]{:S(2)}, u32[]{:S(2)}) collective-permute-start(bf16[128,768]{1,0:T(8,128)(2,1)S(1)} %slice.28), channel_id=1, source_target_pairs={{0,1},{1,0},{2,3},{3,2},{4,8},{5,9},{6,10},{7,11},{8,4},{9,5},{10,... | collective-permute-start | bytes 589832 | tf_op jit(solution)/shard_map/ppermute | solution.py:331
  31.1 10.7 %collective-permute-start.14 = (bf16[384,768]{1,0:T(8,128)(2,1)S(1)}, bf16[384,768]{1,0:T(8,128)(2,1)S(1)}, u32[]{:S(2)}, u32[]{:S(2)}) collective-permute-start(bf16[384,768]{1,0:T(8,128)(2,1)S(1)} %get-tuple-element.71.refs_0_), channel_id=1, source_target_pairs={{0,1},{1,0},{2,3},{3,2},{4,5},{5,4},{6,7},{7,6},{8,9},{9,8},{10,11... | collective-permute-start | bytes 1769480 | tf_op jit(solution)/shard_map/ppermute | solution.py:306
  38.5 3.3 %collective-permute-start.15 = (bf16[384,768]{1,0:T(8,128)(2,1)S(1)}, bf16[384,768]{1,0:T(8,128)(2,1)S(1)}, u32[]{:S(2)}, u32[]{:S(2)}) collective-permute-start(bf16[384,768]{1,0:T(8,128)(2,1)S(1)} %get-tuple-element.89.refs_1_), channel_id=1, source_target_pairs={{0,1},{1,0},{2,3},{3,2},{4,5},{5,4},{6,7},{7,6},{8,9},{9,8},{10,11... | collective-permute-start | bytes 1769480 | tf_op jit(solution)/shard_map/ppermute | solution.py:306
  38.6 3.2 %copy-start.6 = (bf16[192,768]{1,0:T(8,128)(2,1)S(1)}, bf16[192,768]{1,0:T(8,128)(2,1)}, u32[]{:S(2)}) copy-start(bf16[192,768]{1,0:T(8,128)(2,1)} %refs_4_.1) | copy-start | bytes 884740
  38.7 11.6 %collective-permute-start.12 = (bf16[256,768]{1,0:T(8,128)(2,1)S(1)}, bf16[256,768]{1,0:T(8,128)(2,1)S(1)}, u32[]{:S(2)}, u32[]{:S(2)}) collective-permute-start(bf16[256,768]{1,0:T(8,128)(2,1)S(1)} %pad_maximum_fusion.2), channel_id=1, source_target_pairs={{0,16},{16,0},{1,17},{17,1},{2,18},{18,2},{3,19},{19,3},{4,20},{20... | collective-permute-start | bytes 1179656 | tf_op jit(solution)/shard_map/ppermute | solution.py:306
  39.3 11.2 %collective-permute-start.11 = (bf16[256,768]{1,0:T(8,128)(2,1)S(1)}, bf16[256,768]{1,0:T(8,128)(2,1)S(1)}, u32[]{:S(2)}, u32[]{:S(2)}) collective-permute-start(bf16[256,768]{1,0:T(8,128)(2,1)S(1)} %broadcast_select_fusion.refs_7_), channel_id=1, source_target_pairs={{0,2},{1,3},{2,0},{3,1},{4,6},{5,7},{6,4},{7,5},{8,10},{9,11},{10,... | collective-permute-start | bytes 1179656 | tf_op jit(solution)/shard_map/ppermute | solution.py:306
  40.8 7.9 %collective-permute-start.13 = (bf16[128,768]{1,0:T(8,128)(2,1)S(1)}, bf16[128,768]{1,0:T(8,128)(2,1)S(1)}, u32[]{:S(2)}, u32[]{:S(2)}) collective-permute-start(bf16[128,768]{1,0:T(8,128)(2,1)S(1)} %slice.31), channel_id=1, source_target_pairs={{8,0},{9,1},{10,2},{11,3},{0,4},{1,5},{2,6},{3,7},{4,12},{5,13},{6... | collective-permute-start | bytes 589832 | tf_op jit(solution)/shard_map/ppermute | solution.py:327
  52.0 1.8 %collective-permute-start.16 = (f32[128,768]{1,0:T(8,128)S(1)}, f32[128,768]{1,0:T(8,128)S(1)}, u32[]{:S(2)}, u32[]{:S(2)}) collective-permute-start(f32[128,768]{1,0:T(8,128)S(1)} %feed_side.3), channel_id=1, source_target_pairs={{0,1},{1,0},{2,3},{3,2},{4,5},{5,4},{6,7},{7,6},{8,9},{9,8},{10,11... | collective-permute-start | bytes 1179656 | tf_op jit(solution)/shard_map/ppermute | solution.py:306
  52.0 19.5 %copy-start = (bf16[8,256,768]{2,1,0:T(8,128)(2,1)S(1)}, bf16[8,256,768]{2,1,0:T(8,128)(2,1)}, u32[]{:S(2)}) copy-start(bf16[8,256,768]{2,1,0:T(8,128)(2,1)} %books_ref.1) | copy-start | bytes 9437188
  53.5 18.1 %copy-start.1 = (bf16[8,768]{1,0:T(8,128)(2,1)S(1)}, bf16[8,768]{1,0:T(8,128)(2,1)}, u32[]{:S(2)}) copy-start(bf16[8,768]{1,0:T(8,128)(2,1)} %coarse_ref.1) | copy-start | bytes 36868
  (3 other events, 6.8 us)

commit v9 on v8

--- a/solution.py
+++ b/solution.py
@@ -364,7 +364,7 @@
     side2, x1, outer, last_inner, second = after((side2, x1, outer, last_inner, second))
 
     far3 = jnp.where(inner, middle, outer)
-    side3, x2 = side(far3), twin(cat(side2[split:], far3[split:]))
+    x2, side3 = twin(cat(side2[split:], far3[split:])), side(far3)
     last_outer = along(x1[:both], [(2, 0), (0, 1), (1, 3), (3, 2)])
     normed = ((first[0], second[0]), (sibling(first[0]), sibling(second[0])))
     own = [(0, slice(0, rows), 1, slice(0, rows))]

time: 85.6 us -> 85.6 us (level)
  no operation moved by 1% of the time
where the time goes in v9:
time: 85.6 us; the launch traced here: 85.4 us
  blocking collectives  28.6 us (33%)
  Pallas kernels  28.3 us (33%)
  starting transfers between devices  17.4 us (20%)
  waiting for transfers between devices  9.75 us (11%)
  between operations  0.91 us (1%)
    all_to_all x1, blocking collectives, local(): rows = lax.all_to_all(send, 'wide', split_axis=0, concat_axis=0, tiled=True)  17 us
    ppermute x13, starting transfers between devices, flip(): return lambda value: lax.ppermute(value, axis_name, pairs)  12.2 us
    all_to_all x1, blocking collectives, local(): lax.all_to_all(codes, 'wide', split_axis=0, concat_axis=0, tiled=True)  11.6 us
    pallas_call x2, Pallas kernels, attend(): pl.pallas_call(functools.partial(attend_kernel, pack), out_shape=(jax.Sha...  9.51 us
    ppermute x13, waiting for transfers between devices, flip(): return lambda value: lax.ppermute(value, axis_name, pairs)  9.15 us
    pallas_call x2, Pallas kernels, feed(): pl.pallas_call(functools.partial(feed_kernel, len(normed[0]), len(held),...  6.33 us
    pallas_call x1, Pallas kernels, project(): pl.pallas_call(functools.partial(project_kernel, wide=wide, capacity=capa...  5.68 us
    ppermute x2, starting transfers between devices, along(): return lax.ppermute(value, 'wide', pairs)  5.08 us
  transfers between devices with their start and end apart: 17, of which 11 were waited for; matrix products, arithmetic and copies ran while one was open for 0% of the time, Pallas kernels for 27%

profile of v9, /device:TPU:0, one launch (start us, length us, event | category | flops | bytes accessed | tf_op | source)
XLA Modules:
  0.0 85.4 jit_solution(2628630842018994892)
XLA Ops:
  0.6 1.1 %hold.1 = bf16[256,768]{1,0:T(8,128)(2,1)S(1)} custom-call(s32[1,1]{1,0:T(1,128)} %bitcast.group_ref, bf16[192,768]{1,0:T(8,128)(2,1)} %refs_4_.1, bf16[192,768]{1,0:T(8,128)(2,1)} %refs_5_.1), custom_call_target="tpu_custom_call" | custom-call | flops 2000000000 | bytes 5000000 | tf_op jit(solution)/shard_map/hold/pallas_call | solution.py:143
  1.7 3.0 %collective-permute-start = (bf16[256,768]{1,0:T(8,128)(2,1)S(1)}, bf16[256,768]{1,0:T(8,128)(2,1)S(1)}, u32[]{:S(2)}, u32[]{:S(2)}) collective-permute-start(bf16[256,768]{1,0:T(8,128)(2,1)S(1)} %hold.1), channel_id=1, source_target_pairs={{0,2},{1,3},{2,0},{3,1},{4,6},{5,7},{6,4},{7,5},{8,10},{9,11},{10,... | collective-permute-start | bytes 1179656 | tf_op jit(solution)/shard_map/ppermute | solution.py:306
  4.8 1.6 %collective-permute-start.1 = (bf16[256,768]{1,0:T(8,128)(2,1)S(1)}, bf16[256,768]{1,0:T(8,128)(2,1)S(1)}, u32[]{:S(2)}, u32[]{:S(2)}) collective-permute-start(bf16[256,768]{1,0:T(8,128)(2,1)S(1)} %hold.1), channel_id=1, source_target_pairs={{0,4},{1,5},{2,6},{3,7},{4,0},{5,1},{6,2},{7,3},{8,12},{9,13},{10,... | collective-permute-start | bytes 1179656 | tf_op jit(solution)/shard_map/ppermute | solution.py:306
  6.9 1.2 %collective-permute-done.3.other_ref = s32[2,64]{1,0:T(2,128)S(1)} collective-permute-done((s32[2,64]{1,0:T(2,128)S(1)}, s32[2,64]{1,0:T(2,128)S(1)}, u32[]{:S(2)}, u32[]{:S(2)}) %collective-permute-start.3) | collective-permute-done | bytes 544 | tf_op jit(solution)/shard_map/ppermute | solution.py:306
  8.1 5.7 %project.1 = (bf16[768,768]{1,0:T(8,128)(2,1)S(1)}, bf16[768,768]{1,0:T(8,128)(2,1)S(1)}, bf16[768,768]{1,0:T(8,128)(2,1)S(1)}, bf16[768,64]{1,0:T(8,128)(2,1)S(...) custom-call(s32[2,64]{1,0:T(2,128)S(1)} %collective-permute-done.3.other_ref, s32[2,64]{1,0:T(2,128)} %lengths_hbm.1, ...), custom_call_target="tpu_custom_call" | custom-call | flops 2000000000 | bytes 5000000 | tf_op jit(solution)/shard_map/project/pallas_call | solution.py:105
  13.9 1.5 %collective-permute-done.1.refs_8_ = bf16[256,768]{1,0:T(8,128)(2,1)S(1)} collective-permute-done((bf16[256,768]{1,0:T(8,128)(2,1)S(1)}, bf16[256,768]{1,0:T(8,128)(2,1)S(1)}, u32[]{:S(2)}, u32[]{:S(2)}) %collective-permute-start.1) | collective-permute-done | bytes 393248 | tf_op jit(solution)/shard_map/ppermute | solution.py:306
  15.4 4.1 %collective-permute-start.5 = (bf16[256,768]{1,0:T(8,128)(2,1)S(1)}, bf16[256,768]{1,0:T(8,128)(2,1)S(1)}, u32[]{:S(2)}, u32[]{:S(2)}) collective-permute-start(bf16[256,768]{1,0:T(8,128)(2,1)S(1)} %broadcast_select_fusion.1), channel_id=1, source_target_pairs={{4,0},{5,1},{6,2},{7,3},{0,8},{1,9},{2,10},{3,11},{8,12},{9,13},{1... | collective-permute-start | bytes 1179656 | tf_op jit(solution)/shard_map/ppermute | solution.py:327
  20.1 1.6 %collective-permute-start.9 = (bf16[256,768]{1,0:T(8,128)(2,1)S(1)}, bf16[256,768]{1,0:T(8,128)(2,1)S(1)}, u32[]{:S(2)}, u32[]{:S(2)}) collective-permute-start(bf16[256,768]{1,0:T(8,128)(2,1)S(1)} %pad_maximum_fusion.1), channel_id=1, source_target_pairs={{0,16},{16,0},{1,17},{17,1},{2,18},{18,2},{3,19},{19,3},{4,20},{20... | collective-permute-start | bytes 1179656 | tf_op jit(solution)/shard_map/ppermute | solution.py:306
  21.7 4.8 %attend.2 = (bf16[384,768]{1,0:T(8,128)(2,1)S(1)}, f32[64,768]{1,0:T(8,128)S(1)}) custom-call(bf16[768,768]{1,0:T(8,128)(2,1)S(1)} %get-tuple-element.82.q_ref, bf16[768,768]{1,0:T(8,128)(2,1)S(1)} %get-tuple-element.83.k_ref, bf16[768,768]{1,0:T(8,128)(2,1)S(1)} %get-tuple-element.84.v_ref, bf16[768,64]{1,0:T(8,128)(2,1)S(1)} %get-tuple-element.85.rows_ref, ...), custom_call_target="tpu_custom_call" | custom-call | flops 2000000000 | bytes 5000000 | tf_op jit(solution)/shard_map/attend/pallas_call | solution.py:193
  26.4 2.2 %collective-permute-done.4.refs_9_ = bf16[256,768]{1,0:T(8,128)(2,1)S(1)} collective-permute-done((bf16[256,768]{1,0:T(8,128)(2,1)S(1)}, bf16[256,768]{1,0:T(8,128)(2,1)S(1)}, u32[]{:S(2)}, u32[]{:S(2)}) %collective-permute-start.4) | collective-permute-done | bytes 393248 | tf_op jit(solution)/shard_map/ppermute | solution.py:306
  28.7 1.6 %collective-permute-start.7 = (bf16[256,768]{1,0:T(8,128)(2,1)S(1)}, bf16[256,768]{1,0:T(8,128)(2,1)S(1)}, u32[]{:S(2)}, u32[]{:S(2)}) collective-permute-start(bf16[256,768]{1,0:T(8,128)(2,1)S(1)} %pad_maximum_fusion), channel_id=1, source_target_pairs={{0,16},{16,0},{1,17},{17,1},{2,18},{18,2},{3,19},{19,3},{4,20},{20... | collective-permute-start | bytes 1179656 | tf_op jit(solution)/shard_map/ppermute | solution.py:306
  31.6 4.8 %attend.3 = (bf16[384,768]{1,0:T(8,128)(2,1)S(1)}, f32[64,768]{1,0:T(8,128)S(1)}) custom-call(bf16[768,768]{1,0:T(8,128)(2,1)S(1)} %get-tuple-element.82.q_ref, bf16[768,768]{1,0:T(8,128)(2,1)S(1)} %get-tuple-element.83.k_ref, bf16[768,768]{1,0:T(8,128)(2,1)S(1)} %get-tuple-element.84.v_ref, bf16[768,64]{1,0:T(8,128)(2,1)S(1)} %get-tuple-element.85.rows_ref, ...), custom_call_target="tpu_custom_call" | custom-call | flops 2000000000 | bytes 5000000 | tf_op jit(solution)/shard_map/attend/pallas_call | solution.py:193
  36.4 1.0 %collective-permute-done.7.refs_10_.refs_5_ = bf16[256,768]{1,0:T(8,128)(2,1)S(1)} collective-permute-done((bf16[256,768]{1,0:T(8,128)(2,1)S(1)}, bf16[256,768]{1,0:T(8,128)(2,1)S(1)}, u32[]{:S(2)}, u32[]{:S(2)}) %collective-permute-start.7) | collective-permute-done | bytes 393248 | tf_op jit(solution)/shard_map/ppermute | solution.py:306
  39.3 1.5 %collective-permute-start.11 = (bf16[256,768]{1,0:T(8,128)(2,1)S(1)}, bf16[256,768]{1,0:T(8,128)(2,1)S(1)}, u32[]{:S(2)}, u32[]{:S(2)}) collective-permute-start(bf16[256,768]{1,0:T(8,128)(2,1)S(1)} %broadcast_select_fusion.refs_7_), channel_id=1, source_target_pairs={{0,2},{1,3},{2,0},{3,1},{4,6},{5,7},{6,4},{7,5},{8,10},{9,11},{10,... | collective-permute-start | bytes 1179656 | tf_op jit(solution)/shard_map/ppermute | solution.py:306
  40.8 1.0 %collective-permute-start.13 = (bf16[128,768]{1,0:T(8,128)(2,1)S(1)}, bf16[128,768]{1,0:T(8,128)(2,1)S(1)}, u32[]{:S(2)}, u32[]{:S(2)}) collective-permute-start(bf16[128,768]{1,0:T(8,128)(2,1)S(1)} %slice.31), channel_id=1, source_target_pairs={{8,0},{9,1},{10,2},{11,3},{0,4},{1,5},{2,6},{3,7},{4,12},{5,13},{6... | collective-permute-start | bytes 589832 | tf_op jit(solution)/shard_map/ppermute | solution.py:327
  41.8 3.8 %feed.2 = (f32[128,768]{1,0:T(8,128)S(1)}, f32[128,768]{1,0:T(8,128)S(1)}) custom-call(bf16[256,384]{1,0:T(8,128)(2,1)S(1)} %get-tuple-element.86.columns_ref, bf16[384,768]{1,0:T(8,128)(2,1)S(1)} %get-tuple-element.71.refs_0_, bf16[384,768]{1,0:T(8,128)(2,1)S(1)} %get-tuple-element.89.refs_1_, bf16[384,768]{1,0:T(8,128)(2,1)S(1)} %collective-permute-done.14.refs_2_.refs_0_, ...), custom_call_target="tpu_custom_call" | custom-call | flops 2000000000 | bytes 5000000 | tf_op jit(solution)/shard_map/feed/pallas_call | solution.py:254
  45.6 2.5 %feed.3 = (f32[128,768]{1,0:T(8,128)S(1)}, f32[128,768]{1,0:T(8,128)S(1)}) custom-call(bf16[256,384]{1,0:T(8,128)(2,1)S(1)} %get-tuple-element.86.columns_ref, bf16[384,768]{1,0:T(8,128)(2,1)S(1)} %get-tuple-element.71.refs_0_, bf16[384,768]{1,0:T(8,128)(2,1)S(1)} %get-tuple-element.89.refs_1_, bf16[384,768]{1,0:T(8,128)(2,1)S(1)} %collective-permute-done.14.refs_2_.refs_0_, ...), custom_call_target="tpu_custom_call" | custom-call | flops 2000000000 | bytes 5000000 | tf_op jit(solution)/shard_map/feed/pallas_call | solution.py:254
  48.7 1.5 %collective-permute-done.12.refs_2_ = bf16[256,768]{1,0:T(8,128)(2,1)S(1)} collective-permute-done((bf16[256,768]{1,0:T(8,128)(2,1)S(1)}, bf16[256,768]{1,0:T(8,128)(2,1)S(1)}, u32[]{:S(2)}, u32[]{:S(2)}) %collective-permute-start.12) | collective-permute-done | bytes 393248 | tf_op jit(solution)/shard_map/ppermute | solution.py:306
  50.5 1.4 %feed_side.3 = f32[128,768]{1,0:T(8,128)S(1)} custom-call(bf16[256,384]{1,0:T(8,128)(2,1)S(1)} %get-tuple-element.86.columns_ref, bf16[384,768]{1,0:T(8,128)(2,1)S(1)} %collective-permute-done.14.refs_2_.refs_0_, bf16[384,768]{1,0:T(8,128)(2,1)S(1)} %collective-permute-done.15.refs_3_.refs_1_, bf16[256,768]{1,0:T(8,128)(2,1)S(1)} %collective-permute-done.12.refs_2_, ...), custom_call_target="tpu_custom_call" | custom-call | flops 2000000000 | bytes 5000000 | tf_op jit(solution)/shard_map/feed_side/pallas_call | solution.py:221
  52.1 1.4 %feed_side.2.acc_ref = f32[128,768]{1,0:T(8,128)S(1)} custom-call(bf16[256,384]{1,0:T(8,128)(2,1)S(1)} %get-tuple-element.86.columns_ref, bf16[384,768]{1,0:T(8,128)(2,1)S(1)} %get-tuple-element.71.refs_0_, bf16[384,768]{1,0:T(8,128)(2,1)S(1)} %get-tuple-element.89.refs_1_, bf16[256,768]{1,0:T(8,128)(2,1)S(1)} %collective-permute-done.12.refs_2_, ...), custom_call_target="tpu_custom_call" | custom-call | flops 2000000000 | bytes 5000000 | tf_op jit(solution)/shard_map/feed_side/pallas_call | solution.py:221
  54.6 17.0 %all_to_all.10 = bf16[16,16,896]{2,1,0:T(8,128)(2,1)S(1)} all-to-all(bf16[16,16,896]{2,1,0:T(8,128)(2,1)S(1)} %bitcast.9), channel_id=1, replica_groups=mesh['groups'=2,'wide'=16] {'wide'}, dimensions={0} | all-to-all | bytes 917504 | tf_op jit(solution)/shard_map/all_to_all | solution.py:430
  71.6 1.3 %codes.1 = bf16[256,256]{1,0:T(8,128)(2,1)S(1)} custom-call(bf16[256,896]{1,0:T(8,128)(2,1)S(1)} %bitcast.7, bf16[8,768]{1,0:T(8,128)(2,1)S(1)} %copy-done.1, bf16[8,256,768]{2,1,0:T(8,128)(2,1)S(1)} %copy-done), custom_call_target="tpu_custom_call" | custom-call | tf_op jit(solution)/shard_map/codes/pallas_call | solution.py:431
  72.9 11.6 %all_to_all.11 = bf16[16,16,256]{2,1,0:T(8,128)(2,1)S(1)} all-to-all(bf16[16,16,256]{2,1,0:T(8,128)(2,1)S(1)} %bitcast.8), channel_id=1, replica_groups=mesh['groups'=2,'wide'=16] {'wide'}, dimensions={0} | all-to-all | bytes 262144 | tf_op jit(solution)/shard_map/all_to_all | solution.py:438
  84.5 0.9 %take.1 = f32[128,256]{1,0:T(8,128)} custom-call(s32[1,128]{1,0:T(1,128)S(1)} %get-tuple-element.105.slot_ref, bf16[256,256]{1,0:T(8,128)(2,1)S(1)} %bitcast.10), custom_call_target="tpu_custom_call" | custom-call | flops 2000000000 | bytes 5000000 | tf_op jit(solution)/shard_map/take/pallas_call | solution.py:439
  (57 shorter events, 6.6 us)
Async XLA Ops:
  0.6 5.7 %copy-start.9 = (s32[2,64]{1,0:T(2,128)S(1)}, s32[2,64]{1,0:T(2,128)}, u32[]{:S(2)}) copy-start(s32[2,64]{1,0:T(2,128)} %lengths_hbm.1) | copy-start | bytes 1540
  1.7 12.1 %collective-permute-start = (bf16[256,768]{1,0:T(8,128)(2,1)S(1)}, bf16[256,768]{1,0:T(8,128)(2,1)S(1)}, u32[]{:S(2)}, u32[]{:S(2)}) collective-permute-start(bf16[256,768]{1,0:T(8,128)(2,1)S(1)} %hold.1), channel_id=1, source_target_pairs={{0,2},{1,3},{2,0},{3,1},{4,6},{5,7},{6,4},{7,5},{8,10},{9,11},{10,... | collective-permute-start | bytes 1179656 | tf_op jit(solution)/shard_map/ppermute | solution.py:306
  4.8 10.6 %collective-permute-start.1 = (bf16[256,768]{1,0:T(8,128)(2,1)S(1)}, bf16[256,768]{1,0:T(8,128)(2,1)S(1)}, u32[]{:S(2)}, u32[]{:S(2)}) collective-permute-start(bf16[256,768]{1,0:T(8,128)(2,1)S(1)} %hold.1), channel_id=1, source_target_pairs={{0,4},{1,5},{2,6},{3,7},{4,0},{5,1},{6,2},{7,3},{8,12},{9,13},{10,... | collective-permute-start | bytes 1179656 | tf_op jit(solution)/shard_map/ppermute | solution.py:306
  6.3 9.0 %collective-permute-start.2 = (bf16[256,768]{1,0:T(8,128)(2,1)S(1)}, bf16[256,768]{1,0:T(8,128)(2,1)S(1)}, u32[]{:S(2)}, u32[]{:S(2)}) collective-permute-start(bf16[256,768]{1,0:T(8,128)(2,1)S(1)} %hold.1), channel_id=1, source_target_pairs={{0,1},{1,0},{2,3},{3,2},{4,8},{5,9},{6,10},{7,11},{8,4},{9,5},{10,... | collective-permute-start | bytes 1179656 | tf_op jit(solution)/shard_map/ppermute | solution.py:331
  6.3 1.7 %collective-permute-start.3 = (s32[2,64]{1,0:T(2,128)S(1)}, s32[2,64]{1,0:T(2,128)S(1)}, u32[]{:S(2)}, u32[]{:S(2)}) collective-permute-start(s32[2,64]{1,0:T(2,128)S(1)} %copy-done.9), channel_id=1, source_target_pairs={{0,1},{1,0},{2,3},{3,2},{4,5},{5,4},{6,7},{7,6},{8,9},{9,8},{10,11... | collective-permute-start | bytes 1544 | tf_op jit(solution)/shard_map/ppermute | solution.py:306
  15.3 6.3 %copy-start.4 = (bf16[2,384,768]{2,1,0:T(8,128)(2,1)S(1)}, bf16[2,384,768]{2,1,0:T(8,128)(2,1)}, u32[]{:S(2)}) copy-start(bf16[2,384,768]{2,1,0:T(8,128)(2,1)} %x_ref.3) | copy-start | bytes 3538948
  15.3 6.3 %copy-start.5 = (bf16[768,768]{1,0:T(8,128)(2,1)S(1)}, bf16[768,768]{1,0:T(8,128)(2,1)}, u32[]{:S(2)}) copy-start(bf16[768,768]{1,0:T(8,128)(2,1)} %wo_ref.3) | copy-start | bytes 3538948
  15.3 6.3 %copy-start.8 = (f32[768]{0:T(1024)S(1)}, f32[768]{0:T(1024)}, u32[]{:S(2)}) copy-start(f32[768]{0:T(1024)} %gain_ref.4) | copy-start | bytes 9220
  15.4 11.0 %collective-permute-start.5 = (bf16[256,768]{1,0:T(8,128)(2,1)S(1)}, bf16[256,768]{1,0:T(8,128)(2,1)S(1)}, u32[]{:S(2)}, u32[]{:S(2)}) collective-permute-start(bf16[256,768]{1,0:T(8,128)(2,1)S(1)} %broadcast_select_fusion.1), channel_id=1, source_target_pairs={{4,0},{5,1},{6,2},{7,3},{0,8},{1,9},{2,10},{3,11},{8,12},{9,13},{1... | collective-permute-start | bytes 1179656 | tf_op jit(solution)/shard_map/ppermute | solution.py:327
  19.5 9.1 %collective-permute-start.4 = (bf16[256,768]{1,0:T(8,128)(2,1)S(1)}, bf16[256,768]{1,0:T(8,128)(2,1)S(1)}, u32[]{:S(2)}, u32[]{:S(2)}) collective-permute-start(bf16[256,768]{1,0:T(8,128)(2,1)S(1)} %collective-permute-done.1.refs_8_), channel_id=1, source_target_pairs={{0,2},{1,3},{2,0},{3,1},{4,6},{5,7},{6,4},{7,5},{8,10},{9,11},{10,... | collective-permute-start | bytes 1179656 | tf_op jit(solution)/shard_map/ppermute | solution.py:306
  20.1 10.9 %collective-permute-start.9 = (bf16[256,768]{1,0:T(8,128)(2,1)S(1)}, bf16[256,768]{1,0:T(8,128)(2,1)S(1)}, u32[]{:S(2)}, u32[]{:S(2)}) collective-permute-start(bf16[256,768]{1,0:T(8,128)(2,1)S(1)} %pad_maximum_fusion.1), channel_id=1, source_target_pairs={{0,16},{16,0},{1,17},{17,1},{2,18},{18,2},{3,19},{19,3},{4,20},{20... | collective-permute-start | bytes 1179656 | tf_op jit(solution)/shard_map/ppermute | solution.py:306
  28.7 8.7 %collective-permute-start.7 = (bf16[256,768]{1,0:T(8,128)(2,1)S(1)}, bf16[256,768]{1,0:T(8,128)(2,1)S(1)}, u32[]{:S(2)}, u32[]{:S(2)}) collective-permute-start(bf16[256,768]{1,0:T(8,128)(2,1)S(1)} %pad_maximum_fusion), channel_id=1, source_target_pairs={{0,16},{16,0},{1,17},{17,1},{2,18},{18,2},{3,19},{19,3},{4,20},{20... | collective-permute-start | bytes 1179656 | tf_op jit(solution)/shard_map/ppermute | solution.py:306
  30.2 7.9 %collective-permute-start.6 = (bf16[256,768]{1,0:T(8,128)(2,1)S(1)}, bf16[256,768]{1,0:T(8,128)(2,1)S(1)}, u32[]{:S(2)}, u32[]{:S(2)}) collective-permute-start(bf16[256,768]{1,0:T(8,128)(2,1)S(1)} %collective-permute-done.5.refs_4_), channel_id=1, source_target_pairs={{0,2},{1,3},{2,0},{3,1},{4,6},{5,7},{6,4},{7,5},{8,10},{9,11},{10,... | collective-permute-start | bytes 1179656 | tf_op jit(solution)/shard_map/ppermute | solution.py:306
  30.7 7.8 %collective-permute-start.8 = (bf16[256,768]{1,0:T(8,128)(2,1)S(1)}, bf16[256,768]{1,0:T(8,128)(2,1)S(1)}, u32[]{:S(2)}, u32[]{:S(2)}) collective-permute-start(bf16[256,768]{1,0:T(8,128)(2,1)S(1)} %collective-permute-done.5.refs_4_), channel_id=1, source_target_pairs={{0,4},{1,5},{2,6},{3,7},{4,0},{5,1},{6,2},{7,3},{8,12},{9,13},{10,... | collective-permute-start | bytes 1179656 | tf_op jit(solution)/shard_map/ppermute | solution.py:306
  31.1 5.3 %collective-permute-start.10 = (bf16[128,768]{1,0:T(8,128)(2,1)S(1)}, bf16[128,768]{1,0:T(8,128)(2,1)S(1)}, u32[]{:S(2)}, u32[]{:S(2)}) collective-permute-start(bf16[128,768]{1,0:T(8,128)(2,1)S(1)} %slice.28), channel_id=1, source_target_pairs={{0,1},{1,0},{2,3},{3,2},{4,8},{5,9},{6,10},{7,11},{8,4},{9,5},{10,... | collective-permute-start | bytes 589832 | tf_op jit(solution)/shard_map/ppermute | solution.py:331
  31.1 10.7 %collective-permute-start.14 = (bf16[384,768]{1,0:T(8,128)(2,1)S(1)}, bf16[384,768]{1,0:T(8,128)(2,1)S(1)}, u32[]{:S(2)}, u32[]{:S(2)}) collective-permute-start(bf16[384,768]{1,0:T(8,128)(2,1)S(1)} %get-tuple-element.71.refs_0_), channel_id=1, source_target_pairs={{0,1},{1,0},{2,3},{3,2},{4,5},{5,4},{6,7},{7,6},{8,9},{9,8},{10,11... | collective-permute-start | bytes 1769480 | tf_op jit(solution)/shard_map/ppermute | solution.py:306
  38.5 3.3 %collective-permute-start.15 = (bf16[384,768]{1,0:T(8,128)(2,1)S(1)}, bf16[384,768]{1,0:T(8,128)(2,1)S(1)}, u32[]{:S(2)}, u32[]{:S(2)}) collective-permute-start(bf16[384,768]{1,0:T(8,128)(2,1)S(1)} %get-tuple-element.89.refs_1_), channel_id=1, source_target_pairs={{0,1},{1,0},{2,3},{3,2},{4,5},{5,4},{6,7},{7,6},{8,9},{9,8},{10,11... | collective-permute-start | bytes 1769480 | tf_op jit(solution)/shard_map/ppermute | solution.py:306
  38.6 3.2 %copy-start.6 = (bf16[192,768]{1,0:T(8,128)(2,1)S(1)}, bf16[192,768]{1,0:T(8,128)(2,1)}, u32[]{:S(2)}) copy-start(bf16[192,768]{1,0:T(8,128)(2,1)} %refs_4_.1) | copy-start | bytes 884740
  38.7 11.6 %collective-permute-start.12 = (bf16[256,768]{1,0:T(8,128)(2,1)S(1)}, bf16[256,768]{1,0:T(8,128)(2,1)S(1)}, u32[]{:S(2)}, u32[]{:S(2)}) collective-permute-start(bf16[256,768]{1,0:T(8,128)(2,1)S(1)} %pad_maximum_fusion.2), channel_id=1, source_target_pairs={{0,16},{16,0},{1,17},{17,1},{2,18},{18,2},{3,19},{19,3},{4,20},{20... | collective-permute-start | bytes 1179656 | tf_op jit(solution)/shard_map/ppermute | solution.py:306
  39.3 11.2 %collective-permute-start.11 = (bf16[256,768]{1,0:T(8,128)(2,1)S(1)}, bf16[256,768]{1,0:T(8,128)(2,1)S(1)}, u32[]{:S(2)}, u32[]{:S(2)}) collective-permute-start(bf16[256,768]{1,0:T(8,128)(2,1)S(1)} %broadcast_select_fusion.refs_7_), channel_id=1, source_target_pairs={{0,2},{1,3},{2,0},{3,1},{4,6},{5,7},{6,4},{7,5},{8,10},{9,11},{10,... | collective-permute-start | bytes 1179656 | tf_op jit(solution)/shard_map/ppermute | solution.py:306
  40.8 7.9 %collective-permute-start.13 = (bf16[128,768]{1,0:T(8,128)(2,1)S(1)}, bf16[128,768]{1,0:T(8,128)(2,1)S(1)}, u32[]{:S(2)}, u32[]{:S(2)}) collective-permute-start(bf16[128,768]{1,0:T(8,128)(2,1)S(1)} %slice.31), channel_id=1, source_target_pairs={{8,0},{9,1},{10,2},{11,3},{0,4},{1,5},{2,6},{3,7},{4,12},{5,13},{6... | collective-permute-start | bytes 589832 | tf_op jit(solution)/shard_map/ppermute | solution.py:327
  52.0 1.8 %collective-permute-start.16 = (f32[128,768]{1,0:T(8,128)S(1)}, f32[128,768]{1,0:T(8,128)S(1)}, u32[]{:S(2)}, u32[]{:S(2)}) collective-permute-start(f32[128,768]{1,0:T(8,128)S(1)} %feed_side.3), channel_id=1, source_target_pairs={{0,1},{1,0},{2,3},{3,2},{4,5},{5,4},{6,7},{7,6},{8,9},{9,8},{10,11... | collective-permute-start | bytes 1179656 | tf_op jit(solution)/shard_map/ppermute | solution.py:306
  52.0 19.5 %copy-start = (bf16[8,256,768]{2,1,0:T(8,128)(2,1)S(1)}, bf16[8,256,768]{2,1,0:T(8,128)(2,1)}, u32[]{:S(2)}) copy-start(bf16[8,256,768]{2,1,0:T(8,128)(2,1)} %books_ref.1) | copy-start | bytes 9437188
  53.5 18.1 %copy-start.1 = (bf16[8,768]{1,0:T(8,128)(2,1)S(1)}, bf16[8,768]{1,0:T(8,128)(2,1)}, u32[]{:S(2)}) copy-start(bf16[8,768]{1,0:T(8,128)(2,1)} %coarse_ref.1) | copy-start | bytes 36868
  (3 other events, 6.8 us)
